TPU v7x, 256 devices: a whole 4x4x8 slice. The times are simulated.
256 devices in a mesh: blk: 4 (over x_hi, core), tower: 64 (over x_lo, z, y).
Axes of the slice: x: 4 (x_hi: 2, x_lo: 2; x = x_hi * 2 + x_lo), y: 4, z: 8, core: 2. Of those that a mesh axis runs over, the one named last changes fastest.
Arguments:
- clip_tokens: bfloat16 [16384, 16, 3200], P(('blk', 'tower')), may hold values from -6 to 6
- clip_video: int32 [16384], P(('blk', 'tower')), may hold values from 0 to 511, as said below
- pool_vectors: bfloat16 [25, 3200], replicated, may hold values from -0.29882812 to 0.29882812
- out_proj: bfloat16 [3200, 768], replicated, may hold values from -0.109375 to 0.109375
- text_embed: bfloat16 [2048, 768], P(('blk', 'tower')), may hold values from -0.59765625 to 0.59765625
- pair_text: int32 [2048], P(('blk', 'tower')), may hold values from 0 to 2047, each once
Outputs:
- video_embed: bfloat16 [2048, 768], P(('blk', 'tower'))
- video_grad: float32 [2048, 768], P(('blk', 'tower'))
- text_grad: float32 [2048, 768], P(('blk', 'tower'))
- loss: float32 [], replicated
Inputs may be any that keep to these rules, and one draw needn't show every extreme that they name: `clip_video`: owner of video v of a row is device v // 8 of that row's 64 devices (in the order of tower); every video has 1 to 16 clips; the clips of one device name videos of any one owner at most 2 times; in every row one owner is named exactly 2 times by every device of the row, all its videos having 16 clips.
All inputs are finite; a program needn't handle non-finite values.
Results may differ from a plain program's by a relative error of at most 0.004.
Values may be sent and summed in bfloat16 or wider, within the bound.
No kernel may reach another device: no remote copies, remote signals or barrier semaphores. Data moves between devices by JAX's collectives and lax.ppermute only.
A program may use at most 128 MiB of HBM per device.

v0:
```python
import jax
import jax.numpy as jnp
from jax import lax
from jax.sharding import PartitionSpec as P

HD = 128
VID_DEV = 8


SOFT_CAP = 20.0
LOGIT_SCALE = 40.0
EPSILON = 1e-06


def clip_partials(clip_block, pool_vectors):
    clip_count, per_clip, model_width = clip_block.shape
    head_count = pool_vectors.shape[0]
    flat_tokens = clip_block.reshape(clip_count * per_clip, model_width)
    scores = lax.dot_general(
        pool_vectors, flat_tokens, (((1,), (1,)), ((), ())), preferred_element_type=jnp.float32
    )
    weights = jnp.exp(SOFT_CAP * jnp.tanh(scores / SOFT_CAP)).astype(jnp.bfloat16)
    weights = weights.reshape(head_count, clip_count, per_clip)
    denominators = jnp.sum(weights.astype(jnp.float32), axis=2).T
    split_heads = clip_block.reshape(clip_count, per_clip, head_count, model_width // head_count)
    numerators = jnp.einsum(
        "hck,ckhd->chd", weights, split_heads, preferred_element_type=jnp.float32
    )
    return (numerators.reshape(clip_count, model_width), denominators)


def unit_rows(values):
    norms = jnp.sqrt(jnp.sum(values * values, axis=1) + EPSILON)
    return (values / norms[:, None], norms)


def body(clip_tokens, clip_video, pool_vectors, out_proj, text_embed, pair_text):
    tower_size = lax.axis_size("tower")
    tower_index = lax.axis_index("tower")
    clip_count = clip_tokens.shape[0]
    capacity = max(2, 2 * clip_count // tower_size)
    slot_total = tower_size * capacity
    owner_of = clip_video // VID_DEV
    owner_hot = (owner_of[:, None] == jnp.arange(tower_size, dtype=jnp.int32)[None, :]).astype(
        jnp.int32
    )
    owner_rank = jnp.sum((jnp.cumsum(owner_hot, axis=0) - 1) * owner_hot, axis=1)
    slot_of = owner_of * capacity + owner_rank
    slot_place = (slot_of[:, None] == jnp.arange(slot_total, dtype=jnp.int32)[None, :]).astype(
        jnp.int32
    )
    slot_clip = jnp.sum(slot_place * jnp.arange(clip_count, dtype=jnp.int32)[:, None], axis=0)
    slot_used = jnp.sum(slot_place, axis=0) > 0
    owner_lists = lax.all_gather(clip_video, "tower", axis=0, tiled=True).reshape(
        tower_size, clip_count
    )
    is_mine = owner_lists // VID_DEV == tower_index
    mine_rank = jnp.cumsum(is_mine.astype(jnp.int32), axis=1) - 1
    slot_hot = (
        mine_rank[:, :, None] == jnp.arange(capacity, dtype=jnp.int32)[None, None, :]
    ) & is_mine[:, :, None]
    local_video = owner_lists % VID_DEV
    slot_video = jnp.sum(jnp.where(slot_hot, local_video[:, :, None], 0), axis=1).reshape(-1)
    slot_live = jnp.sum(slot_hot.astype(jnp.int32), axis=1).reshape(-1) > 0
    assign = (
        (slot_video[None, :] == jnp.arange(VID_DEV, dtype=jnp.int32)[:, None]) & slot_live[None, :]
    ).astype(jnp.float32)
    outgoing = jnp.where(
        slot_used[:, None, None], clip_tokens[slot_clip], jnp.zeros((), jnp.bfloat16)
    )
    arrived = lax.all_to_all(outgoing, "tower", split_axis=0, concat_axis=0, tiled=True)
    numerators, denominators = clip_partials(arrived, pool_vectors)
    video_num = jnp.dot(assign, numerators, precision=lax.Precision.HIGHEST)
    video_den = jnp.dot(assign, denominators, precision=lax.Precision.HIGHEST)
    pooled = video_num / jnp.repeat(video_den, HD, axis=1)
    embedding = jnp.dot(pooled, out_proj.astype(jnp.float32), precision=lax.Precision.HIGHEST)
    video_hat, video_norm = unit_rows(embedding)
    text_hat, text_norm = unit_rows(text_embed.astype(jnp.float32))
    video_low = video_hat.astype(jnp.bfloat16)
    text_low = text_hat.astype(jnp.bfloat16)
    texts_all = lax.all_gather(text_low, ("blk", "tower"), axis=0, tiled=True)
    video_total = texts_all.shape[0]
    logits = LOGIT_SCALE * lax.dot_general(
        video_low, texts_all, (((1,), (1,)), ((), ())), preferred_element_type=jnp.float32
    )
    exp_rows = jnp.exp(logits)
    row_sums = jnp.sum(exp_rows, axis=1)
    onehot = (pair_text[:, None] == jnp.arange(video_total, dtype=jnp.int32)[None, :]).astype(
        jnp.float32
    )
    positive = jnp.sum(logits * onehot, axis=1)
    col_part = jnp.sum(exp_rows, axis=0)
    loss_part = jnp.sum(jnp.log(row_sums) - 2.0 * positive)
    col_sums, loss_total = lax.psum((col_part, loss_part), ("blk", "tower"))
    loss = (loss_total + jnp.sum(jnp.log(col_sums))) / (2.0 * video_total)
    probe = (exp_rows / row_sums[:, None] + exp_rows / col_sums[None, :] - 2.0 * onehot).astype(
        jnp.bfloat16
    )
    video_dir = LOGIT_SCALE * jnp.dot(probe, texts_all, preferred_element_type=jnp.float32)
    text_dir = lax.psum_scatter(
        LOGIT_SCALE
        * lax.dot_general(
            probe, video_low, (((0,), (0,)), ((), ())), preferred_element_type=jnp.float32
        ),
        ("blk", "tower"),
        scatter_dimension=0,
        tiled=True,
    )
    video_grad = (
        video_dir - jnp.sum(video_dir * video_hat, axis=1, keepdims=True) * video_hat
    ) / video_norm[:, None]
    text_grad = (
        text_dir - jnp.sum(text_dir * text_hat, axis=1, keepdims=True) * text_hat
    ) / text_norm[:, None]
    return (embedding.astype(jnp.bfloat16), video_grad, text_grad, loss)


def solution(mesh):
    return jax.shard_map(
        body,
        mesh=mesh,
        in_specs=(
            P(("blk", "tower"), None, None),
            P(("blk", "tower")),
            P(),
            P(),
            P(("blk", "tower"), None),
            P(("blk", "tower")),
        ),
        out_specs=(
            P(("blk", "tower"), None),
            P(("blk", "tower"), None),
            P(("blk", "tower"), None),
            P(),
        ),
        check_vma=False,
    )
```

profile of v0, /device:TPU:0, one launch (start us, length us, event | category | flops | bytes accessed | tf_op | source)
XLA Modules:
  0.0 2250.3 jit_solution(12023594068877086780)
XLA Ops:
  7.2 0.7 and_select_fusion
  8.1 0.2 select_reduce_fusion.3
  8.2 0.7 multiply_add_fusion
  9.0 11.3 gather_fusion
  20.3 11.1 broadcast_select_fusion
  31.5 11.7 all-to-all-start
  43.3 0.7 fusion.22
  44.1 0.6 dynamic-slice
  45.4 0.3 dynamic-update-slice
  45.6 576.3 %all-reduce = s32[4096]{0:T(1024)S(1)} all-reduce(s32[4096]{0:T(1024)S(1)} %dynamic-update-slice), channel_id=1, replica_groups=mesh['blk'=4,'tower'=64] {'tower'}, use_global_device_ids=true, to_apply=%add | all-reduce | flops 4096 | bytes 32768
  622.1 0.2 reduce_window_sum.22
  622.6 0.1 eq.88
  623.0 8.7 fusion.4
  631.7 0.7 reshape.154
  632.4 0.2 bitcast_convert_fusion
  632.6 0.6 copy.27
  633.2 18.2 copy.26
  651.4 0.3 convert_reduce_fusion
  651.9 8.9 multiply_reduce_fusion
  660.8 0.9 convolution_divide_fusion
  661.7 4.5 multiply_reduce_fusion.3
  666.2 183.9 %all-gather.2.cloned.1.call-done = bf16[2048,768]{1,0:T(8,128)(2,1)} async-done(((bf16[8,768]{1,0:T(8,128)(2,1)}), bf16[2048,768]{1,0:T(8,128)(2,1)}) %all-gather.2.cloned.1.call-update) | async-done | bytes 3145744 | tf_op jit(solution)/shard_map/all_gather | solution.py:81
  850.2 3.0 select_reduce_fusion
  853.1 0.6 subtract_reduce_fusion
  853.8 104.6 %all-reduce.1 = (f32[2048]{0:T(1024)S(1)}, f32[]{:T(128)}) all-reduce(f32[2048]{0:T(1024)S(1)} %get-tuple-element.5, f32[]{:T(128)} %subtract_reduce_fusion), channel_id=1, replica_groups=mesh['blk'=4,'tower'=64] {'blk','tower'}, use_global_device_ids=true, to_apply=%region_12.13 | all-reduce | flops 2049 | bytes 16392 | tf_op jit(solution)/shard_map/psum | solution.py:94
  958.3 3.8 convolution_multiply_fusion
  962.1 0.6 log_reduce_fusion
  964.0 0.7 multiply_reduce_fusion.2
  964.7 0.7 subtract_divide_fusion.1
  965.4 1274.5 %reduce-scatter.2.cloned.1.call-done = f32[8,768]{1,0:T(8,128)} async-done(((f32[2048,768]{1,0:T(8,128)}), f32[8,768]{1,0:T(8,128)}) %reduce-scatter.2.cloned.1.call-update) | async-done | bytes 24592 | tf_op jit(solution)/shard_map/reduce_scatter | solution.py:100
  2239.9 0.9 multiply_reduce_fusion.1
  2240.9 1.4 subtract_divide_fusion
  (38 shorter events, 1.3 us)
Async XLA Ops:
  7.2 615.9 %copy-start = (bf16[25,3200]{1,0:T(8,128)(2,1)S(1)}, bf16[25,3200]{1,0:T(8,128)(2,1)}, u32[]{:S(2)}) copy-start(bf16[25,3200]{1,0:T(8,128)(2,1)} %param.8) | copy-start | bytes 480004
  31.5 11.7 copy-start.3
  31.5 12.6 copy-start.6
  31.5 13.9 copy-start.5
  31.5 591.6 %all-to-all-start = ((bf16[128,16,3200]{2,1,0:T(8,128)(2,1)}), bf16[128,16,3200]{2,1,0:T(8,128)(2,1)}, u32[]{:S(2)}, u32[]{:S(2)}) async-start(bf16[128,16,3200]{2,1,0:T(8,128)(2,1)} %broadcast_select_fusion), calls=%async_computation | async-start | bytes 26214400 | tf_op jit(solution)/shard_map/all_to_all | solution.py:71
  43.1 807.0 %all-gather.2.cloned.1.call-start = ((), (), s32[]{:S(2)}) async-start(), calls=%async_computation.2 | async-start | bytes 3158016 | tf_op jit(solution)/shard_map/all_gather | solution.py:81
  44.0 2195.9 %reduce-scatter.2.cloned.1.call-start = ((), (), s32[]{:S(2)}) async-start(), calls=%async_computation.3 | async-start | bytes 6316032 | tf_op jit(solution)/shard_map/reduce_scatter | solution.py:100
  660.8 189.4 %copy-start.4 = (s32[8]{0:T(128)S(1)}, s32[8]{0:T(128)}, u32[]{:S(2)}) copy-start(s32[8]{0:T(128)} %param.11) | copy-start | bytes 100
  958.3 5.7 copy-start.2
  958.3 1284.0 %copy-start.1 = (bf16[25,3200]{1,0:T(8,128)(2,1)S(1)}, bf16[25,3200]{1,0:T(8,128)(2,1)}, u32[]{:S(2)}) copy-start(bf16[25,3200]{1,0:T(8,128)(2,1)} %param.8) | copy-start | bytes 480004
Sparse Core Ops, SparseCore 0:
  46.4 803.6 all-gather.1
  962.2 1277.6 reduce-scatter.1
where the time goes:
time: 2250 us
  waiting for transfers between devices  1460 us (65%)
  blocking collectives  681 us (30%)
  local copies, waits for them, and re-layouts  32.3 us (1%)
  other arithmetic  27.9 us (1%)
    reduce_scatter x1, waiting for transfers between devices, body(): lax.psum_scatter(LOGIT_SCALE * lax.dot_general(probe, video_low, (((0,),...  1270 us
    unnamed x1, blocking collectives  576 us
    all_gather x1, waiting for transfers between devices, body(): texts_all = lax.all_gather(text_low, ('blk', 'tower'), axis=0, tiled=True)  184 us
    psum x1, blocking collectives, body(): col_sums, loss_total = lax.psum((col_part, loss_part), ('blk', 'tower'))  105 us
  transfers between devices with their start and end apart: 3, of which 2 were waited for; matrix products, arithmetic and copies ran while one was open for 2% of the time, Pallas kernels for 0%

commit v1 on v0

v1 whole, which is shorter than its diff:
```python
import jax
import jax.numpy as jnp
import numpy as np
from jax import lax
from jax.experimental import pallas as pl
from jax.experimental.pallas import tpu as pltpu
from jax.sharding import Mesh, PartitionSpec as P

H = 25
HD = 128
D = 3200
E = 768
TOK = 16
CLIPS = 64
SLOTS = 128
SOFT_CAP = 20.0
SCALE = 40.0
EPS = 1e-06
TAIL = D + 128
ETEXT = E + 128
HALF = 1024
ALL = ("xh", "c", "xl", "z", "y")
ROW = ("xl", "z", "y")
WIDE = ("xh", "xl", "y")
CHUNK = 16
TOKS = CHUNK * TOK
TILE = 256
VMEM = pl.BlockSpec(memory_space=pltpu.VMEM)
SMEM = pl.BlockSpec(memory_space=pltpu.SMEM)
f32 = jnp.float32
bf16 = jnp.bfloat16
NT = (((1,), (1,)), ((), ()))
TN = (((0,), (0,)), ((), ()))


def dot(a, b, dims=(((1,), (0,)), ((), ()))):
    return lax.dot_general(a, b, dims, preferred_element_type=f32)


def iota(shape, dim):
    return lax.broadcasted_iota(jnp.int32, shape, dim)


def column_of(row):
    n = row.shape[1]
    eye = iota((n, n), 0) == iota((n, n), 1)
    return jnp.sum(jnp.where(eye, jnp.broadcast_to(row, (n, n)), 0.0), axis=1, keepdims=True)


def clip_kernel(video_ref, token_ref, pool_ref, out_ref, weight_scr, num_scr):
    step = pl.program_id(0)

    @pl.when(step == 0)
    def _():
        weight_scr[...] = jnp.zeros_like(weight_scr)

    x = token_ref[...]
    scores = dot(pool_ref[...], x, NT)
    weights = jnp.exp(SOFT_CAP * jnp.tanh(scores / SOFT_CAP))
    weight_scr[0:H, :] = weights
    weight_scr[32 : 32 + H, :] = weights
    mine = iota((CHUNK, TOKS), 1) // TOK == iota((CHUNK, TOKS), 0)
    rows = pl.ds(step * CHUNK, CHUNK)
    den = dot(mine.astype(f32).astype(bf16), weight_scr[...].astype(bf16), NT)
    den_hi = den.astype(bf16).astype(f32)
    select = iota((CHUNK, CLIPS), 1) == iota((CHUNK, CLIPS), 0) + step * CHUNK
    video = jnp.sum(
        jnp.where(select, jnp.broadcast_to(video_ref[...].astype(f32), (CHUNK, CLIPS)), 0.0),
        axis=1,
        keepdims=True,
    ).astype(jnp.int32)
    lane = iota((CHUNK, 128), 1)
    local = jnp.where(lane - 64 == video % 8, 1.0, 0.0)
    tail = jnp.where(lane < 32, den_hi, jnp.where(lane < 64, den - den_hi, local))
    num_scr[rows, D:TAIL] = tail.astype(bf16)
    for h in range(0, H, 2):
        pair = range(h, min(h + 2, H))
        lhs = jnp.concatenate(
            [
                jnp.where(mine, jnp.broadcast_to(weight_scr[k : k + 1, :], (CHUNK, TOKS)), 0.0)
                for k in pair
            ],
            axis=0,
        ).astype(bf16)
        part = dot(lhs, x[:, h * HD : (h + len(pair)) * HD])
        for n, k in enumerate(pair):
            num_scr[rows, k * HD : (k + 1) * HD] = part[
                n * CHUNK : (n + 1) * CHUNK, n * HD : (n + 1) * HD
            ].astype(bf16)

    @pl.when(step == pl.num_programs(0) - 1)
    def _():
        owner = (video_ref[...] // 8).astype(f32)
        owner_col = column_of(owner)
        before = (owner_col == owner) & (iota((CLIPS, CLIPS), 0) < iota((CLIPS, CLIPS), 1))
        rank = jnp.sum(jnp.where(before, 1.0, 0.0), axis=0, keepdims=True)
        slot = (owner * 2.0 + rank).astype(jnp.int32)
        place = jnp.where(iota((SLOTS, CLIPS), 0) == slot, 1.0, 0.0).astype(bf16)
        out_ref[...] = dot(place, num_scr[...]).astype(bf16)


def clip_sums(clip_tokens, clip_video, pool_vectors):
    tokens = clip_tokens.reshape(CLIPS * TOK, D)
    return pl.pallas_call(
        clip_kernel,
        grid=(CLIPS // CHUNK,),
        in_specs=[
            pl.BlockSpec((1, CLIPS), lambda i: (0, 0)),
            pl.BlockSpec((TOKS, D), lambda i: (i, 0)),
            pl.BlockSpec((H, D), lambda i: (0, 0)),
        ],
        out_specs=pl.BlockSpec((SLOTS, TAIL), lambda i: (0, 0)),
        out_shape=jax.ShapeDtypeStruct((SLOTS, TAIL), bf16),
        scratch_shapes=[pltpu.VMEM((128, TOKS), f32), pltpu.VMEM((CLIPS, TAIL), bf16)],
        compiler_params=pltpu.CompilerParams(vmem_limit_bytes=24 << 20),
        cost_estimate=pl.CostEstimate(
            flops=2 * 1024 * D * 64, bytes_accessed=8 << 20, transcendentals=1 << 17
        ),
    )(clip_video.reshape(1, CLIPS), tokens, pool_vectors)


def embed_kernel(arrived_ref, proj_ref, emb_ref, hat_ref, norm_ref, send_ref):
    assign = arrived_ref[:, D:TAIL].astype(f32).T[64:72, :].astype(bf16)
    sums = dot(assign, arrived_ref[...])
    den = sums[:, D : D + 32] + sums[:, D + 32 : D + 64]
    pooled = jnp.concatenate(
        [sums[:, h * HD : (h + 1) * HD] / den[:, h : h + 1] for h in range(H)], axis=1
    )
    hi = pooled.astype(bf16).astype(f32)
    mid = (pooled - hi).astype(bf16).astype(f32)
    low = pooled - hi - mid
    parts = dot(jnp.concatenate([hi, mid, low], axis=0).astype(bf16), proj_ref[...])
    emb = parts[0:8] + parts[8:16] + parts[16:24]
    norm = jnp.sqrt(jnp.sum(emb * emb, axis=1, keepdims=True) + EPS)
    hat = emb / norm
    emb_ref[...] = emb.astype(bf16)
    hat_ref[...] = hat
    norm_ref[...] = norm
    hat_low = hat.astype(bf16)
    for k in range(8):
        send_ref[k] = hat_low


def embed(arrived, out_proj):
    return pl.pallas_call(
        embed_kernel,
        in_specs=[VMEM, VMEM],
        out_specs=[VMEM] * 4,
        out_shape=[
            jax.ShapeDtypeStruct((8, E), bf16),
            jax.ShapeDtypeStruct((8, E), f32),
            jax.ShapeDtypeStruct((8, 1), f32),
            jax.ShapeDtypeStruct((8, 8, E), bf16),
        ],
        compiler_params=pltpu.CompilerParams(vmem_limit_bytes=24 << 20),
        cost_estimate=pl.CostEstimate(
            flops=2 * 24 * D * E, bytes_accessed=6 << 20, transcendentals=0
        ),
    )(arrived, out_proj)


def logits_kernel(
    place_ref, video_ref, own_ref, other_ref, near_ref,
    payload_ref, rowsum_ref, rows_ref, cols_ref, tile_scr, sum_scr,
):
    base = pl.multiple_of(place_ref[0], 8)
    side = place_ref[1].astype(f32)
    code = own_ref[:, E:ETEXT].astype(f32)
    target = code[:, 0:1] * 64.0 + code[:, 1:2] + 1024.0 * side
    target = jnp.where(target >= 2048.0, target - 2048.0, target)
    videos = video_ref[...]
    positive = jnp.zeros((1, TILE), f32)
    lane = iota((1, TILE), 1).astype(f32)
    for t in range(8):
        ref = own_ref if t < 4 else other_ref
        texts = ref[t % 4 * TILE : (t % 4 + 1) * TILE, 0:E]
        logits = SCALE * dot(videos, texts, NT)
        ex = jnp.exp(logits)
        tile_scr[...] = ex
        payload_ref[:, t * TILE : (t + 1) * TILE] = jnp.sum(ex, axis=0, keepdims=True)
        halves = ex[:, 0:128] + ex[:, 128:TILE]
        if t == 0:
            sum_scr[...] = halves
        else:
            sum_scr[...] += halves
        hit = target - float(t * TILE) == lane
        positive += jnp.sum(jnp.where(hit, logits, 0.0), axis=0, keepdims=True)
        rows_ref[:, t * TILE : (t + 1) * TILE] = tile_scr[pl.ds(base, 8), :]
    rowsum = jnp.sum(sum_scr[...], axis=1, keepdims=True)
    rowsum_ref[...] = rowsum
    cols = jnp.exp(SCALE * dot(videos, near_ref[...], NT))
    cols_ref[...] = cols
    colsum = jnp.sum(cols, axis=0, keepdims=True)
    total = jnp.sum(jnp.log(rowsum), axis=0, keepdims=True) - 2.0 * jnp.sum(
        positive, axis=1, keepdims=True
    )
    payload_ref[:, 2048:2176] = jnp.concatenate([colsum, jnp.zeros((1, 112), f32)], axis=1)
    payload_ref[:, 2176:2304] = jnp.broadcast_to(total, (1, 128))


def all_logits(place, videos, own, other, near):
    return pl.pallas_call(
        logits_kernel,
        in_specs=[SMEM] + [VMEM] * 4,
        out_specs=[VMEM] * 4,
        out_shape=[
            jax.ShapeDtypeStruct((1, 2304), f32),
            jax.ShapeDtypeStruct((HALF, 1), f32),
            jax.ShapeDtypeStruct((8, 2048), f32),
            jax.ShapeDtypeStruct((HALF, 16), f32),
        ],
        scratch_shapes=[pltpu.VMEM((HALF, TILE), f32), pltpu.VMEM((HALF, 128), f32)],
        compiler_params=pltpu.CompilerParams(vmem_limit_bytes=32 << 20),
        cost_estimate=pl.CostEstimate(
            flops=2 * HALF * 2048 * E, bytes_accessed=6 << 20, transcendentals=1 << 21
        ),
    )(place, videos, own, other, near)


def grad_kernel(
    place_ref, mine_ref, theirs_ref, rowsum_ref, rows_ref, cols_ref, video_ref, own_ref, other_ref,
    hat_ref, norm_ref, target_ref, loss_ref, grad_ref, near_ref, far_ref,
):
    base = place_ref[0].astype(f32)
    side = place_ref[1].astype(f32)
    mine, theirs = mine_ref[...], theirs_ref[...]
    colsum = mine[:, 0:2048] + jnp.concatenate([theirs[:, 1024:2048], theirs[:, 0:1024]], axis=1)
    loss = mine[:, 2176:2177] + theirs[:, 2176:2177]
    loss += jnp.sum(jnp.log(colsum), axis=1, keepdims=True)
    loss_ref[...] = loss / 4096.0
    rows = rows_ref[...]
    target = target_ref[...] + 1024.0 * side
    target = jnp.where(target >= 2048.0, target - 2048.0, target)
    hot = jnp.where(target == iota((8, 2048), 1).astype(f32), 2.0, 0.0)
    probe = rows / jnp.sum(rows, axis=1, keepdims=True) + rows / colsum - hot
    probe = probe.astype(bf16)
    direction = SCALE * (
        dot(probe[:, 0:HALF], own_ref[:, 0:E]) + dot(probe[:, HALF:2048], other_ref[:, 0:E])
    )
    hat = hat_ref[...]
    grad_ref[...] = (
        direction - jnp.sum(direction * hat, axis=1, keepdims=True) * hat
    ) / norm_ref[...]
    far = theirs[:, 2048:2176]
    nearsum = mine[:, 2048:2064] + jnp.concatenate([far[:, 8:16], far[:, 0:8]], axis=1)
    code = own_ref[:, E:ETEXT].astype(f32)
    target = code[:, 0:1] * 64.0 + code[:, 1:2] + 1024.0 * side
    target = jnp.where(target >= 2048.0, target - 2048.0, target)
    spot = iota((1, 16), 1)
    place = jnp.where(spot < 8, spot, spot - 8 + HALF).astype(f32) + base
    cols = cols_ref[...]
    hot = jnp.where(target == place, 2.0, 0.0)
    probe = (cols / rowsum_ref[...] + cols / nearsum - hot).astype(bf16)
    text = SCALE * dot(probe, video_ref[...], TN)
    near_ref[...] = text[0:8]
    far_ref[...] = text[8:16]


def gradients(*args):
    return pl.pallas_call(
        grad_kernel,
        in_specs=[SMEM] + [VMEM] * 11,
        out_specs=[VMEM] * 4,
        out_shape=[
            jax.ShapeDtypeStruct((1, 1), f32),
            jax.ShapeDtypeStruct((8, E), f32),
            jax.ShapeDtypeStruct((8, E), f32),
            jax.ShapeDtypeStruct((8, E), f32),
        ],
        compiler_params=pltpu.CompilerParams(vmem_limit_bytes=32 << 20),
        cost_estimate=pl.CostEstimate(
            flops=2 * 32 * 2048 * E, bytes_accessed=8 << 20, transcendentals=2048
        ),
    )(*args)


def unit_rows(values):
    norms = jnp.sqrt(jnp.sum(values * values, axis=1, keepdims=True) + EPS)
    return values / norms, norms


def spread(block):
    n = block.shape[-1]
    column = lax.all_to_all(block, "z", 0, 0, tiled=True).reshape(64, n)
    wide = jnp.broadcast_to(column[None], (16, 64, n))
    return lax.all_to_all(wide, WIDE, 0, 0, tiled=True).reshape(HALF, n)


def swap(x):
    return lax.ppermute(x, "c", [(0, 1), (1, 0)])


def body(clip_tokens, clip_video, pool_vectors, out_proj, text_embed, pair_text):
    xh, c, xl, z, y = (lax.axis_index(a) for a in ALL)
    base = (((xh * 2 + xl) * 4 + y) * 8 + z) * 8
    place = jnp.stack([base, c]).astype(jnp.int32)
    device, row = pair_text // 8, pair_text % 8
    spot = ((device // 128 * 2 + device // 32 % 2) * 4 + device % 4) * 8 + device // 4 % 8
    target = (device // 64 % 2) * HALF + spot * 8 + row
    text_hat, text_norm = unit_rows(text_embed.astype(f32))
    text_low = text_hat.astype(bf16)
    code = jnp.stack([target // 64, target % 64], axis=1).astype(bf16)
    text_row = jnp.concatenate([text_low, jnp.pad(code, ((0, 0), (0, 126)))], axis=1)
    own = spread(jnp.broadcast_to(text_row[None], (8, 8, ETEXT)))
    other = swap(own)
    near = jnp.concatenate([text_low, lax.dynamic_slice(other, (base, 0), (8, E))], axis=0)

    outgoing = clip_sums(clip_tokens, clip_video, pool_vectors)
    arrived = lax.all_to_all(outgoing.reshape(64, 2, TAIL), ROW, 0, 0, tiled=True)
    video_embed, video_hat, video_norm, send = embed(arrived.reshape(SLOTS, TAIL), out_proj)
    videos = spread(send)
    payload, rowsum, rows, cols = all_logits(place, videos, own, other, near)
    theirs = swap(payload)
    loss, video_grad, near_dir, far_dir = gradients(
        place, payload, theirs, rowsum, rows, cols, videos, own, other,
        video_hat, video_norm, target.astype(f32)[:, None],
    )
    text_dir = near_dir + swap(far_dir)
    text_grad = (
        text_dir - jnp.sum(text_dir * text_hat, axis=1, keepdims=True) * text_hat
    ) / text_norm
    return video_embed, video_grad, text_grad, loss.reshape(())


def solution(mesh):
    split = Mesh(mesh.devices.reshape(2, 2, 2, 8, 4), ALL)
    return jax.shard_map(
        body,
        mesh=split,
        in_specs=(P(ALL, None, None), P(ALL), P(), P(), P(ALL, None), P(ALL)),
        out_specs=(P(ALL, None), P(ALL, None), P(ALL, None), P()),
        check_vma=False,
    )
```

time: 2250 us -> 144 us (0.06)
  the two profiles are of different devices: /device:TPU:0 before, /device:TPU:1 now
where the time goes in v1:
time: 144 us
  waiting for transfers between devices  48.2 us (33%)
  starting transfers between devices  29.9 us (21%)
  blocking collectives  28.1 us (20%)
  Pallas kernels  17.2 us (12%)
  local copies, waits for them, and re-layouts  16.2 us (11%)
  other arithmetic  3.31 us (2%)
    all_to_all x2, waiting for transfers between devices, spread(): return lax.all_to_all(wide, WIDE, 0, 0, tiled=True).reshape(HALF, n)  31 us
    all_to_all x2, blocking collectives, spread(): column = lax.all_to_all(block, 'z', 0, 0, tiled=True).reshape(64, n)  28.1 us
    all_to_all x1, waiting for transfers between devices, body(): lax.all_to_all(outgoing.reshape(64, 2, TAIL), ROW, 0, 0, tiled=True)  15.5 us
    all_to_all x2, starting transfers between devices, spread(): return lax.all_to_all(wide, WIDE, 0, 0, tiled=True).reshape(HALF, n)  13.4 us
    ppermute x3, starting transfers between devices, swap(): return lax.ppermute(x, 'c', [(0, 1), (1, 0)])  10 us
    unnamed x18, local copies, waits for them, and re-layouts  8.92 us
    all_to_all x1, starting transfers between devices, body(): lax.all_to_all(outgoing.reshape(64, 2, TAIL), ROW, 0, 0, tiled=True)  6.49 us
    pallas_call x1, Pallas kernels, all_logits(): pl.pallas_call(logits_kernel, in_specs=[SMEM] + [VMEM] * 4, out_specs=[VM...  6.42 us
  transfers between devices with their start and end apart: 6, of which 5 were waited for; matrix products, arithmetic and copies ran while one was open for 4% of the time, Pallas kernels for 5%

profile of v1, /device:TPU:1, one launch (start us, length us, event | category | flops | bytes accessed | tf_op | source)
XLA Modules:
  0.0 143.7 jit_solution(11506223916353982424)
XLA Ops:
  0.6 0.8 fusion.1
  1.5 0.7 convert_bitcast_fusion
  2.3 0.8 fusion.14
  3.1 16.4 %all_to_all.25 = bf16[8,8,896]{2,1,0:T(8,128)(2,1)S(1)} all-to-all(bf16[8,8,896]{2,1,0:T(8,128)(2,1)S(1)} %broadcast_in_dim.27), channel_id=1, replica_groups=mesh['xh'=2,'c'=2,'xl'=2,'z'=8,'y'=4] {'z'}, dimensions={0} | all-to-all | bytes 229376 | tf_op jit(solution)/shard_map/all_to_all | solution.py:284
  19.5 1.5 %broadcast_in_dim.29 = bf16[16,64,896]{2,1,0:T(8,128)(2,1)} broadcast(bf16[64,896]{1,0:T(8,128)(2,1)S(1)} %bitcast.22), dimensions={1,2} | broadcast | bytes 1949696 | tf_op jit(solution)/shard_map/broadcast_in_dim | solution.py:285
  21.1 6.9 %all-to-all-start.4 = ((bf16[16,64,896]{2,1,0:T(8,128)(2,1)}), bf16[16,64,896]{2,1,0:T(8,128)(2,1)S(1)}, u32[]{:S(2)}, u32[]{:S(2)}) async-start(bf16[16,64,896]{2,1,0:T(8,128)(2,1)} %broadcast_in_dim.29), calls=%async_computation.4 | async-start | bytes 3670016 | tf_op jit(solution)/shard_map/all_to_all | solution.py:286
  28.0 2.9 %copy-done = bf16[64,16,3200]{2,1,0:T(8,128)(2,1)S(1)} copy-done((bf16[64,16,3200]{2,1,0:T(8,128)(2,1)S(1)}, bf16[64,16,3200]{2,1,0:T(8,128)(2,1)}, u32[]{:S(2)}) %copy-start) | copy-done | bytes 6553624
  30.8 5.8 %shard_map.93 = bf16[128,3328]{1,0:T(8,128)(2,1)S(1)} custom-call(s32[1,64]{1,0:T(1,128)S(1)} %bitcast.21, bf16[1024,3200]{1,0:T(8,128)(2,1)S(1)} %bitcast.18, bf16[25,3200]{1,0:T(8,128)(2,1)S(1)} %copy-done.6), custom_call_target="tpu_custom_call" | custom-call | flops 419430400 | bytes 8388608 | tf_op jit(solution)/shard_map/pallas_call | solution.py:104
  36.7 1.2 reshape.41
  37.9 12.8 %all-to-all-done.4 = bf16[16,64,896]{2,1,0:T(8,128)(2,1)S(1)} async-done(((bf16[16,64,896]{2,1,0:T(8,128)(2,1)}), bf16[16,64,896]{2,1,0:T(8,128)(2,1)S(1)}, u32[]{:S(2)}, u32[]{:S(2)}) %all-to-all-start.4) | async-done | bytes 1835040 | tf_op jit(solution)/shard_map/all_to_all | solution.py:286
  50.8 6.5 %all-to-all-start = ((bf16[64,2,3328]{2,1,0:T(2,128)(2,1)}), bf16[64,2,3328]{2,1,0:T(2,128)(2,1)}, u32[]{:S(2)}, u32[]{:S(2)}) async-start(bf16[64,2,3328]{2,1,0:T(2,128)(2,1)} %reshape.41), calls=%async_computation | async-start | bytes 1703936 | tf_op jit(solution)/shard_map/all_to_all | solution.py:309
  57.3 3.9 %collective-permute-start = (bf16[1024,896]{1,0:T(8,128)(2,1)S(1)}, bf16[1024,896]{1,0:T(8,128)(2,1)}, u32[]{:S(2)}, u32[]{:S(2)}) collective-permute-start(bf16[1024,896]{1,0:T(8,128)(2,1)S(1)} %bitcast.15), channel_id=1, source_target_pairs={{0,64},{64,0},{1,65},{65,1},{2,66},{66,2},{3,67},{67,3},{4,68},{68... | collective-permute-start | bytes 5505032 | tf_op jit(solution)/shard_map/ppermute | solution.py:290
  61.2 15.5 %all-to-all-done = bf16[64,2,3328]{2,1,0:T(2,128)(2,1)} async-done(((bf16[64,2,3328]{2,1,0:T(2,128)(2,1)}), bf16[64,2,3328]{2,1,0:T(2,128)(2,1)}, u32[]{:S(2)}, u32[]{:S(2)}) %all-to-all-start) | async-done | bytes 852000 | tf_op jit(solution)/shard_map/all_to_all | solution.py:309
  76.7 2.4 %reshape.42.arrived_ref = bf16[128,3328]{1,0:T(8,128)(2,1)S(1)} reshape(bf16[64,2,3328]{2,1,0:T(2,128)(2,1)} %all-to-all-done) | data formatting | bytes 1703936 | tf_op jit(solution)/shard_map/reshape | solution.py:310
  79.1 2.4 %copy-done.1 = bf16[3200,768]{1,0:T(8,128)(2,1)S(1)} copy-done((bf16[3200,768]{1,0:T(8,128)(2,1)S(1)}, bf16[3200,768]{1,0:T(8,128)(2,1)}, u32[]{:S(2)}) %copy-start.1) | copy-done | bytes 4915224
  81.5 1.8 %shard_map.94 = (bf16[8,768]{1,0:T(8,128)(2,1)}, f32[8,768]{1,0:T(8,128)S(1)}, f32[8,1]{1,0:T(8,128)S(1)}, bf16[8,8,768]{2,1,0:T(8,128)(2,1)S(1)}) custom-call(bf16[128,3328]{1,0:T(8,128)(2,1)S(1)} %reshape.42.arrived_ref, bf16[3200,768]{1,0:T(8,128)(2,1)S(1)} %copy-done.1), custom_call_target="tpu_custom_call" | custom-call | flops 117964800 | bytes 6291456 | tf_op jit(solution)/shard_map/pallas_call | solution.py:145
  83.3 11.7 %all_to_all.26 = bf16[8,8,768]{2,1,0:T(8,128)(2,1)S(1)} all-to-all(bf16[8,8,768]{2,1,0:T(8,128)(2,1)S(1)} %get-tuple-element.17), channel_id=1, replica_groups=mesh['xh'=2,'c'=2,'xl'=2,'z'=8,'y'=4] {'z'}, dimensions={0} | all-to-all | bytes 196608 | tf_op jit(solution)/shard_map/all_to_all | solution.py:284
  95.0 1.3 broadcast_in_dim.26
  96.3 6.6 %all-to-all-start.2 = ((bf16[16,64,768]{2,1,0:T(8,128)(2,1)}), bf16[16,64,768]{2,1,0:T(8,128)(2,1)S(1)}, u32[]{:S(2)}, u32[]{:S(2)}) async-start(bf16[16,64,768]{2,1,0:T(8,128)(2,1)} %broadcast_in_dim.26), calls=%async_computation.2 | async-start | bytes 3145728 | tf_op jit(solution)/shard_map/all_to_all | solution.py:286
  102.9 0.7 constant_dynamic-slice_fusion
  103.7 18.2 %all-to-all-done.2 = bf16[16,64,768]{2,1,0:T(8,128)(2,1)S(1)} async-done(((bf16[16,64,768]{2,1,0:T(8,128)(2,1)}), bf16[16,64,768]{2,1,0:T(8,128)(2,1)S(1)}, u32[]{:S(2)}, u32[]{:S(2)}) %all-to-all-start.2) | async-done | bytes 1572896 | tf_op jit(solution)/shard_map/all_to_all | solution.py:286
  121.8 6.4 %shard_map.95 = (f32[1,2304]{1,0:T(1,128)S(1)}, f32[1024,1]{1,0:T(8,128)S(1)}, f32[8,2048]{1,0:T(8,128)S(1)}, f32[1024,16]{1,0:T(8,128)S(1)}) custom-call(s32[2]{0:T(128)S(1)} %pad_add_fusion.place_ref, bf16[1024,768]{1,0:T(8,128)(2,1)S(1)} %bitcast.19, bf16[1024,896]{1,0:T(8,128)(2,1)S(1)} %bitcast.16, bf16[1024,896]{1,0:T(8,128)(2,1)} %collective-permute-done.other_ref, ...), custom_call_target="tpu_custom_call" | custom-call | flops 3221225472 | bytes 6291456 | tf_op jit(solution)/shard_map/pallas_call | solution.py:202
  128.3 0.8 copy-done.2
  129.0 0.8 copy-done.4
  129.8 5.8 %collective-permute-start.1 = (f32[1,2304]{1,0:T(1,128)S(1)}, f32[1,2304]{1,0:T(1,128)S(1)}, u32[]{:S(2)}, u32[]{:S(2)}) collective-permute-start(f32[1,2304]{1,0:T(1,128)S(1)} %get-tuple-element.18.mine_ref), channel_id=1, source_target_pairs={{0,64},{64,0},{1,65},{65,1},{2,66},{66,2},{3,67},{67,3},{4,68},{68... | collective-permute-start | bytes 27656 | tf_op jit(solution)/shard_map/ppermute | solution.py:290
  135.7 0.7 collective-permute-done.1.theirs_ref
  136.4 1.0 copy-done.3
  137.5 1.0 copy-done.5
  138.5 3.1 %shard_map.96 = (f32[1,1]{1,0:T(1,128)}, f32[8,768]{1,0:T(8,128)}, f32[8,768]{1,0:T(8,128)S(1)}, f32[8,768]{1,0:T(8,128)S(1)}) custom-call(s32[2]{0:T(128)S(1)} %pad_add_fusion.place_ref, f32[1,2304]{1,0:T(1,128)S(1)} %get-tuple-element.18.mine_ref, f32[1,2304]{1,0:T(1,128)S(1)} %collective-permute-done.1.theirs_ref, f32[1024,1]{1,0:T(8,128)S(1)} %copy-done.3, ...), custom_call_target="tpu_custom_call" | custom-call | flops 100663296 | bytes 8388608 | tf_op jit(solution)/shard_map/pallas_call | solution.py:260
  141.6 0.3 collective-permute-start.2
  141.9 0.9 collective-permute-done.2
  143.0 0.7 subtract_divide_fusion
  (23 shorter events, 0.5 us)
Async XLA Ops:
  21.0 6.9 %copy-start.6 = (bf16[25,3200]{1,0:T(8,128)(2,1)S(1)}, bf16[25,3200]{1,0:T(8,128)(2,1)}, u32[]{:S(2)}) copy-start(bf16[25,3200]{1,0:T(8,128)(2,1)} %pool_ref.1) | copy-start | bytes 480004
  21.0 6.9 %copy-start.7 = (s32[64]{0:T(128)S(1)}, s32[64]{0:T(128)}, u32[]{:S(2)}) copy-start(s32[64]{0:T(128)} %param.7) | copy-start | bytes 772
  21.1 29.7 %all-to-all-start.4 = ((bf16[16,64,896]{2,1,0:T(8,128)(2,1)}), bf16[16,64,896]{2,1,0:T(8,128)(2,1)S(1)}, u32[]{:S(2)}, u32[]{:S(2)}) async-start(bf16[16,64,896]{2,1,0:T(8,128)(2,1)} %broadcast_in_dim.29), calls=%async_computation.4 | async-start | bytes 3670016 | tf_op jit(solution)/shard_map/all_to_all | solution.py:286
  28.0 2.9 %copy-start = (bf16[64,16,3200]{2,1,0:T(8,128)(2,1)S(1)}, bf16[64,16,3200]{2,1,0:T(8,128)(2,1)}, u32[]{:S(2)}) copy-start(bf16[64,16,3200]{2,1,0:T(8,128)(2,1)} %param.6) | copy-start | bytes 19660804
  50.8 25.9 %all-to-all-start = ((bf16[64,2,3328]{2,1,0:T(2,128)(2,1)}), bf16[64,2,3328]{2,1,0:T(2,128)(2,1)}, u32[]{:S(2)}, u32[]{:S(2)}) async-start(bf16[64,2,3328]{2,1,0:T(2,128)(2,1)} %reshape.41), calls=%async_computation | async-start | bytes 1703936 | tf_op jit(solution)/shard_map/all_to_all | solution.py:309
  57.3 45.7 %collective-permute-start = (bf16[1024,896]{1,0:T(8,128)(2,1)S(1)}, bf16[1024,896]{1,0:T(8,128)(2,1)}, u32[]{:S(2)}, u32[]{:S(2)}) collective-permute-start(bf16[1024,896]{1,0:T(8,128)(2,1)S(1)} %bitcast.15), channel_id=1, source_target_pairs={{0,64},{64,0},{1,65},{65,1},{2,66},{66,2},{3,67},{67,3},{4,68},{68... | collective-permute-start | bytes 5505032 | tf_op jit(solution)/shard_map/ppermute | solution.py:290
  79.1 2.4 %copy-start.1 = (bf16[3200,768]{1,0:T(8,128)(2,1)S(1)}, bf16[3200,768]{1,0:T(8,128)(2,1)}, u32[]{:S(2)}) copy-start(bf16[3200,768]{1,0:T(8,128)(2,1)} %proj_ref.1) | copy-start | bytes 14745604
  96.3 25.5 %all-to-all-start.2 = ((bf16[16,64,768]{2,1,0:T(8,128)(2,1)}), bf16[16,64,768]{2,1,0:T(8,128)(2,1)S(1)}, u32[]{:S(2)}, u32[]{:S(2)}) async-start(bf16[16,64,768]{2,1,0:T(8,128)(2,1)} %broadcast_in_dim.26), calls=%async_computation.2 | async-start | bytes 3145728 | tf_op jit(solution)/shard_map/all_to_all | solution.py:286
  128.3 0.8 copy-start.2
  129.0 0.8 copy-start.4
  129.8 6.6 %collective-permute-start.1 = (f32[1,2304]{1,0:T(1,128)S(1)}, f32[1,2304]{1,0:T(1,128)S(1)}, u32[]{:S(2)}, u32[]{:S(2)}) collective-permute-start(f32[1,2304]{1,0:T(1,128)S(1)} %get-tuple-element.18.mine_ref), channel_id=1, source_target_pairs={{0,64},{64,0},{1,65},{65,1},{2,66},{66,2},{3,67},{67,3},{4,68},{68... | collective-permute-start | bytes 27656 | tf_op jit(solution)/shard_map/ppermute | solution.py:290
  136.4 1.0 copy-start.3
  137.5 1.0 copy-start.5
  138.5 4.3 %copy-start.8 = (bf16[8,768]{1,0:T(8,128)(2,1)S(1)}, bf16[8,768]{1,0:T(8,128)(2,1)}, u32[]{:S(2)}) copy-start(bf16[8,768]{1,0:T(8,128)(2,1)} %param.10) | copy-start | bytes 36868
  141.6 1.2 collective-permute-start.2

commit v2 on v1

v2 whole, which is shorter than its diff:
```python
import jax
import jax.numpy as jnp
from jax import lax
from jax.experimental import pallas as pl
from jax.experimental.pallas import tpu as pltpu
from jax.sharding import Mesh, PartitionSpec as P

H = 25
HD = 128
D = 3200
E = 768
TOK = 16
CLIPS = 64
SOFT_CAP = 20.0
SCALE = 40.0
EPS = 1e-06
ALL = ("xh", "c", "xl", "z", "y")
ROW = ("xl", "z", "y")
PLANE = ("z", "y")
GROUP = ("xh", "c", "xl")
CHUNK = 16
TOKS = CHUNK * TOK
PARTS = 4
WIDE = 7
SENT = WIDE * HD
TAIL = 4 * HD
TILE = 256
SET = 512
PLANE_ROWS = 256
VMEM = pl.BlockSpec(memory_space=pltpu.VMEM)
f32 = jnp.float32
bf16 = jnp.bfloat16
NT = (((1,), (1,)), ((), ()))
TN = (((0,), (0,)), ((), ()))


def dot(a, b, dims=(((1,), (0,)), ((), ()))):
    return lax.dot_general(a, b, dims, preferred_element_type=f32)


def iota(shape, dim):
    return lax.broadcasted_iota(jnp.int32, shape, dim)


def column_of(row):
    n = row.shape[1]
    eye = iota((n, n), 0) == iota((n, n), 1)
    return jnp.sum(jnp.where(eye, jnp.broadcast_to(row, (n, n)), 0.0), axis=1, keepdims=True)


def unit_rows(values):
    norms = jnp.sqrt(jnp.sum(values * values, axis=1, keepdims=True) + EPS)
    return values / norms, norms


def clip_kernel(
    video_ref, token_ref, pool_ref, text_ref, pair_ref,
    out_ref, hat_ref, norm_ref, weight_scr, num_scr,
):
    step = pl.program_id(0)

    @pl.when(step == 0)
    def _():
        weight_scr[...] = jnp.zeros_like(weight_scr)
        num_scr[...] = jnp.zeros_like(num_scr)
        hat, norm = unit_rows(text_ref[...].astype(f32))
        hat_ref[...] = hat
        norm_ref[...] = norm
        texts = jnp.broadcast_to(hat[None], (CLIPS, 8, E)).reshape(CLIPS * 8, E)
        out_ref[:, SENT : SENT + E] = texts.astype(bf16)

    x = token_ref[...]
    scores = dot(pool_ref[...], x, NT)
    weights = jnp.exp(SOFT_CAP * jnp.tanh(scores / SOFT_CAP))
    weight_scr[0:H, :] = weights
    weight_scr[32 : 32 + H, :] = weights
    mine = iota((CHUNK, TOKS), 1) // TOK == iota((CHUNK, TOKS), 0)
    den = dot(mine.astype(f32).astype(bf16), weight_scr[...].astype(bf16), NT)
    den_hi = den.astype(bf16).astype(f32)
    here = iota((CHUNK, CLIPS), 1) == iota((CHUNK, CLIPS), 0) + step * CHUNK
    video = jnp.broadcast_to(video_ref[...].astype(f32), (CHUNK, CLIPS))
    video = jnp.sum(jnp.where(here, video, 0.0), axis=1, keepdims=True).astype(jnp.int32)
    lane = iota((CHUNK, HD), 1)
    local = jnp.where(lane - 64 == video % 8, 1.0, 0.0)
    tail = jnp.where(lane < 32, den_hi, jnp.where(lane < 64, den - den_hi, local))

    def put(j, value):
        rows = pl.ds(pl.multiple_of(j // WIDE * CLIPS + step * CHUNK, CHUNK), CHUNK)
        num_scr[rows, j % WIDE * HD : (j % WIDE + 1) * HD] = value.astype(bf16)

    put(H, tail)
    for h in range(0, H, 2):
        pair = range(h, min(h + 2, H))
        lhs = jnp.concatenate(
            [
                jnp.where(mine, jnp.broadcast_to(weight_scr[k : k + 1, :], (CHUNK, TOKS)), 0.0)
                for k in pair
            ],
            axis=0,
        ).astype(bf16)
        part = dot(lhs, x[:, h * HD : (h + len(pair)) * HD])
        for n, k in enumerate(pair):
            put(k, part[n * CHUNK : (n + 1) * CHUNK, n * HD : (n + 1) * HD])

    @pl.when(step == pl.num_programs(0) - 1)
    def _():
        owner = (video_ref[...] // 8).astype(f32)
        before = (column_of(owner) == owner) & (
            iota((CLIPS, CLIPS), 0) < iota((CLIPS, CLIPS), 1)
        )
        rank = jnp.sum(jnp.where(before, 1.0, 0.0), axis=0, keepdims=True)
        slot = owner * 2.0 + rank
        slots = jnp.concatenate([slot] * PARTS, axis=1).astype(jnp.int32)
        shape = (CLIPS * 8, PARTS * CLIPS)
        row, col = iota(shape, 0), iota(shape, 1)
        place = (row // PARTS == slots) & (row % PARTS == col // CLIPS)
        out = dot(jnp.where(place, 1.0, 0.0).astype(bf16), num_scr[...])
        pair = pair_ref[...]
        codes = jnp.concatenate(
            [
                jnp.zeros((1, 72), f32),
                (pair // 64).astype(f32),
                (pair % 64).astype(f32),
                jnp.zeros((1, 40), f32),
            ],
            axis=1,
        )
        last = iota((CLIPS * 8, HD), 0) % PARTS == PARTS - 1
        out_ref[:, 0:TAIL] = out[:, 0:TAIL].astype(bf16)
        out_ref[:, TAIL : TAIL + HD] = (
            out[:, TAIL : TAIL + HD] + jnp.where(last, codes, 0.0)
        ).astype(bf16)
        out_ref[:, TAIL + HD : SENT] = out[:, TAIL + HD : SENT].astype(bf16)


def clip_sums(clip_tokens, clip_video, pool_vectors, text_embed, pair_text):
    whole = lambda *shape: pl.BlockSpec(shape, lambda i: (0,) * len(shape))
    return pl.pallas_call(
        clip_kernel,
        grid=(CLIPS // CHUNK,),
        in_specs=[
            whole(1, CLIPS),
            pl.BlockSpec((TOKS, D), lambda i: (i, 0)),
            whole(H, D),
            whole(8, E),
            whole(1, 8),
        ],
        out_specs=[whole(CLIPS * 8, SENT + E), whole(8, E), whole(8, 1)],
        out_shape=[
            jax.ShapeDtypeStruct((CLIPS * 8, SENT + E), bf16),
            jax.ShapeDtypeStruct((8, E), f32),
            jax.ShapeDtypeStruct((8, 1), f32),
        ],
        scratch_shapes=[pltpu.VMEM((128, TOKS), f32), pltpu.VMEM((PARTS * CLIPS, SENT), bf16)],
        compiler_params=pltpu.CompilerParams(vmem_limit_bytes=56 << 20),
        cost_estimate=pl.CostEstimate(
            flops=2 * 1024 * D * 64, bytes_accessed=8 << 20, transcendentals=1 << 17
        ),
    )(
        clip_video.reshape(1, CLIPS),
        clip_tokens.reshape(CLIPS * TOK, D),
        pool_vectors,
        text_embed,
        pair_text.reshape(1, 8),
    )


def embed_kernel(
    arrived_ref, proj_ref, emb_ref, hat_ref, norm_ref, send_ref, text_ref, target_ref
):
    rows = CLIPS * 8
    text_ref[...] = arrived_ref[:, SENT : SENT + E]
    tails = arrived_ref[:, TAIL : TAIL + HD]
    pick = jnp.where(iota((8, HD), 1) - 64 == iota((8, HD), 0), 1.0, 0.0).astype(bf16)
    hot = dot(pick, tails, NT)
    hot = jnp.where(iota((8, rows), 1) % PARTS == PARTS - 1, hot, 0.0)
    assign = jnp.concatenate(
        [hot if p == PARTS - 1 else pltpu.roll(hot, rows - (PARTS - 1 - p), 1) for p in range(PARTS)],
        axis=0,
    )
    sums = dot(assign.astype(bf16), arrived_ref[:, 0:SENT])

    def chunk(j):
        p, q = j // WIDE, j % WIDE
        return sums[p * 8 : (p + 1) * 8, q * HD : (q + 1) * HD]

    den = chunk(H)
    den = den[:, 0:32] + den[:, 32:64]
    pooled = jnp.concatenate([chunk(h) / den[:, h : h + 1] for h in range(H)], axis=1)
    hi = pooled.astype(bf16).astype(f32)
    mid = (pooled - hi).astype(bf16).astype(f32)
    low = pooled - hi - mid
    parts = dot(jnp.concatenate([hi, mid, low], axis=0).astype(bf16), proj_ref[...])
    emb = parts[0:8] + parts[8:16] + parts[16:24]
    emb_ref[...] = emb.astype(bf16)
    hat, norm = unit_rows(emb)
    hat_ref[...] = hat
    norm_ref[...] = norm
    hat_low = hat.astype(bf16)
    for k in range(32):
        send_ref[k] = hat_low
    code = tails.astype(f32).reshape(CLIPS, 8, HD)[:, 3:4, :]
    code = jnp.broadcast_to(code, (CLIPS, 8, HD)).reshape(rows, HD)
    lane, own = iota((rows, HD), 1), iota((rows, HD), 0) % 8
    code = jnp.where(lane - 72 == own, 64.0 * code, jnp.where(lane - 80 == own, code, 0.0))
    target_ref[...] = jnp.sum(code, axis=1, keepdims=True)


def embed(arrived, out_proj):
    return pl.pallas_call(
        embed_kernel,
        in_specs=[VMEM, VMEM],
        out_specs=[VMEM] * 6,
        out_shape=[
            jax.ShapeDtypeStruct((8, E), bf16),
            jax.ShapeDtypeStruct((8, E), f32),
            jax.ShapeDtypeStruct((8, 1), f32),
            jax.ShapeDtypeStruct((32, 8, E), bf16),
            jax.ShapeDtypeStruct((SET, E), bf16),
            jax.ShapeDtypeStruct((SET, 1), f32),
        ],
        compiler_params=pltpu.CompilerParams(vmem_limit_bytes=24 << 20),
        cost_estimate=pl.CostEstimate(
            flops=2 * 24 * D * E, bytes_accessed=6 << 20, transcendentals=0
        ),
    )(arrived, out_proj)


def position():
    xh, c, xl, z, y = (lax.axis_index(a) for a in ALL)
    return xh, c, xl, z * 4 + y


def rows_of(xh, c, k):
    a, b = k // 2, k % 2
    return (xh + a - 2 * a * xh) * 2 + (c + b - 2 * b * c)


def logits_kernel(
    video_ref, target_ref, set0_ref, set1_ref, set2_ref, set3_ref,
    send_ref, own_ref, tile_scr, col_scr,
):
    xh, c, xl, spot = position()
    sets = (set0_ref, set1_ref, set2_ref, set3_ref)
    target = target_ref[pl.ds(pl.multiple_of(xl * PLANE_ROWS, PLANE_ROWS), PLANE_ROWS), :]
    videos = video_ref[...]
    lane = iota((1, TILE), 1).astype(f32)
    base = pl.multiple_of(spot * 8, 8)
    positive = jnp.zeros((1, TILE), f32)
    halves = jnp.zeros((PLANE_ROWS, 128), f32)
    for k, ref in enumerate(sets):
        row = rows_of(xh, c, k)
        for t in range(2):
            tile = row * 2 + t
            logits = SCALE * dot(videos, ref[t * TILE : (t + 1) * TILE, :], NT)
            ex = jnp.exp(logits)
            tile_scr[...] = ex
            col_scr[pl.ds(tile, 1), :] = jnp.sum(ex, axis=0, keepdims=True)
            halves += ex[:, 0:128] + ex[:, 128:TILE]
            hit = target == (tile * TILE).astype(f32) + lane
            positive += jnp.sum(jnp.where(hit, logits, 0.0), axis=0, keepdims=True)
            at = k * SET + t * TILE
            own_ref[:, at : at + TILE] = tile_scr[pl.ds(base, 8), :]
    rowsum = jnp.sum(halves, axis=1, keepdims=True)
    total = jnp.sum(jnp.log(rowsum), axis=0, keepdims=True) - 2.0 * jnp.sum(
        positive, axis=1, keepdims=True
    )
    odd = spot % 2 == 1
    near, groups = [], []
    for k, ref in enumerate(sets):
        for half in range(2):
            at = pl.multiple_of(half * PLANE_ROWS + spot // 2 * 16, 16)
            pair = ref[pl.ds(at, 16), :].astype(f32)
            near.append(jnp.where(odd, pair[8:16], pair[0:8]))
            groups.append(rows_of(xh, c, k) * 2 + half)
    near = jnp.concatenate(near, axis=0).astype(bf16)
    ex = jnp.exp(SCALE * dot(videos, near, NT))
    slot = iota((1, 64), 1)
    group = sum(jnp.where(slot // 8 == n, g, 0) for n, g in enumerate(groups))
    text = ((group * 32 + spot) * 8 + slot % 8).astype(f32)
    first = ex / rowsum - jnp.where(target == text, 2.0, 0.0)
    first_hi = first.astype(bf16).astype(f32)
    ex_hi = ex.astype(bf16).astype(f32)
    terms = jnp.concatenate([first_hi, first - first_hi, ex_hi, ex - ex_hi], axis=1)
    sums = dot(terms.astype(bf16), videos, TN)
    first, second = sums[0:64] + sums[64:128], sums[128:192] + sums[192:256]
    cols = col_scr[...]
    total = jnp.broadcast_to(total, (8, 128))
    for n, g in enumerate(groups):
        send_ref[g, :, 0:E] = first[n * 8 : (n + 1) * 8]
        send_ref[g, :, E : 2 * E] = second[n * 8 : (n + 1) * 8]
        send_ref[g, :, 2 * E : 2 * E + TILE] = cols
        send_ref[g, :, 2 * E + TILE :] = total


def all_logits(videos, target, *sets):
    return pl.pallas_call(
        logits_kernel,
        in_specs=[VMEM] * 6,
        out_specs=[VMEM] * 2,
        out_shape=[
            jax.ShapeDtypeStruct((8, 8, 2 * E + TILE + 128), f32),
            jax.ShapeDtypeStruct((8, 4 * SET), f32),
        ],
        scratch_shapes=[pltpu.VMEM((PLANE_ROWS, TILE), f32), pltpu.VMEM((8, TILE), f32)],
        compiler_params=pltpu.CompilerParams(vmem_limit_bytes=32 << 20),
        cost_estimate=pl.CostEstimate(
            flops=2 * PLANE_ROWS * 2048 * E, bytes_accessed=5 << 20, transcendentals=1 << 19
        ),
    )(videos, target, *sets)


def grad_kernel(
    arrived_ref, own_ref, target_ref, set0_ref, set1_ref, set2_ref, set3_ref,
    video_hat_ref, video_norm_ref, text_hat_ref, text_norm_ref,
    loss_ref, video_grad_ref, text_grad_ref, col_scr,
):
    xh, c, xl, spot = position()
    got = arrived_ref[0]
    for k in range(1, 8):
        got = got + arrived_ref[k]
    cols = got[:, 2 * E : 2 * E + TILE]
    col_scr[...] = cols
    logs = jnp.sum(jnp.sum(jnp.log(cols), axis=0, keepdims=True), axis=1, keepdims=True)
    loss_ref[...] = (logs + got[0:1, 2 * E + TILE : 2 * E + TILE + 1]) / 4096.0

    def project(direction, hat, norm):
        return (direction - jnp.sum(direction * hat, axis=1, keepdims=True) * hat) / norm

    group = (xh * 2 + c) * 2 + xl
    mine = jnp.broadcast_to(col_scr[pl.ds(group, 1), :], (8, TILE))
    here = iota((8, TILE), 1) == spot * 8 + iota((8, TILE), 0)
    mine = jnp.sum(jnp.where(here, mine, 0.0), axis=1, keepdims=True)
    text_dir = SCALE * (got[:, 0:E] + got[:, E : 2 * E] / mine)
    text_grad_ref[...] = project(text_dir, text_hat_ref[...], text_norm_ref[...])

    rows = own_ref[...]
    rowsum = jnp.sum(rows, axis=1, keepdims=True)
    target = target_ref[pl.ds(pl.multiple_of((xl * 32 + spot) * 8, 8), 8), :]
    lane = iota((8, TILE), 1).astype(f32)
    direction = jnp.zeros((8, E), f32)
    for k, ref in enumerate((set0_ref, set1_ref, set2_ref, set3_ref)):
        row = rows_of(xh, c, k)
        for t in range(2):
            tile = row * 2 + t
            at = k * SET + t * TILE
            ex = rows[:, at : at + TILE]
            hot = jnp.where(target == (tile * TILE).astype(f32) + lane, 2.0, 0.0)
            probe = ex / rowsum + ex / col_scr[pl.ds(tile, 1), :] - hot
            direction += dot(probe.astype(bf16), ref[t * TILE : (t + 1) * TILE, :])
    video_grad_ref[...] = project(SCALE * direction, video_hat_ref[...], video_norm_ref[...])


def gradients(*args):
    return pl.pallas_call(
        grad_kernel,
        in_specs=[VMEM] * 11,
        out_specs=[VMEM] * 3,
        out_shape=[
            jax.ShapeDtypeStruct((1, 1), f32),
            jax.ShapeDtypeStruct((8, E), f32),
            jax.ShapeDtypeStruct((8, E), f32),
        ],
        scratch_shapes=[pltpu.VMEM((8, TILE), f32)],
        compiler_params=pltpu.CompilerParams(vmem_limit_bytes=32 << 20),
        cost_estimate=pl.CostEstimate(
            flops=2 * 8 * 2048 * E, bytes_accessed=5 << 20, transcendentals=2048
        ),
    )(*args)


def exchange(x, axes):
    return lax.all_to_all(x, axes, 0, 0, tiled=True)


def swap(x):
    return lax.ppermute(x, "c", [(0, 1), (1, 0)])


def cross(x):
    return lax.ppermute(x, ("xh", "xl"), [(0, 3), (3, 0), (1, 2), (2, 1)])


def body(clip_tokens, clip_video, pool_vectors, out_proj, text_embed, pair_text):
    outgoing, text_hat, text_norm = clip_sums(
        clip_tokens, clip_video, pool_vectors, text_embed, pair_text
    )
    arrived = exchange(outgoing.reshape(CLIPS, 8, SENT + E), ROW)
    video_embed, video_hat, video_norm, send, texts, target = embed(
        arrived.reshape(CLIPS * 8, SENT + E), out_proj
    )
    crossed = cross(texts)
    sets = (texts, swap(texts), crossed, swap(crossed))
    videos = exchange(send, PLANE).reshape(PLANE_ROWS, E)
    terms, own = all_logits(videos, target, *sets)
    loss, video_grad, text_grad = gradients(
        exchange(terms, GROUP), own, target, *sets, video_hat, video_norm, text_hat, text_norm
    )
    return video_embed, video_grad, text_grad, loss.reshape(())


def solution(mesh):
    split = Mesh(mesh.devices.reshape(2, 2, 2, 8, 4), ALL)
    return jax.shard_map(
        body,
        mesh=split,
        in_specs=(P(ALL, None, None), P(ALL), P(), P(), P(ALL, None), P(ALL)),
        out_specs=(P(ALL, None), P(ALL, None), P(ALL, None), P()),
        check_vma=False,
    )
```

time: 144 us -> 125 us (0.87)
  blocking collectives: 28.1 us -> 88.4 us
  waiting for transfers between devices: 48.2 us -> 12.1 us
  starting transfers between devices: 29.9 us -> 9.1 us
  local copies, waits for them, and re-layouts: 16.2 us -> 0.02 us
  other arithmetic: 3.31 us -> 0.01 us
  Pallas kernels: 17.2 us -> 14.5 us
    all_to_all x2 -> x3, blocking collectives: 28.1 us -> 88.4 us  [exchange(): return lax.all_to_all(x, axes, 0, 0, tiled=True)]
    all_to_all x3 -> x0, waiting for transfers between devices: 46.6 us -> none  [the longest x2 31 us: spread(): return lax.all_to_all(wide, WIDE, 0, 0, tiled=True).reshape(HALF, n)]
    all_to_all x3 -> x0, starting transfers between devices: 19.9 us -> none  [the longest x2 13.4 us: spread(): return lax.all_to_all(wide, WIDE, 0, 0, tiled=True).reshape(HALF, n)]
    ppermute x0 -> x1, waiting for transfers between devices: none -> 12.1 us  [cross(): return lax.ppermute(x, ('xh', 'xl'), [(0, 3), (3, 0), (1, 2), (2, 1)])]
    unnamed x18 -> x8, local copies, waits for them, and re-layouts: 8.92 us -> 0.02 us
    reshape x2 -> x0, local copies, waits for them, and re-layouts: 3.58 us -> none  [the longest x1 2.36 us: body(): arrived.reshape(SLOTS, TAIL)]
    broadcast_in_dim x4 -> x0, local copies, waits for them, and re-layouts: 2.91 us -> none  [the longest x2 2.82 us: spread(): wide = jnp.broadcast_to(column[None], (16, 64, n))]
    pallas_call x4, Pallas kernels: 17.2 us -> 14.5 us  [the longest x1 9.09 us: clip_sums(): pl.pallas_call(clip_kernel, grid=(CLIPS // CHUNK,), in_specs=[whole(1, CL...]
  transfers between devices with their start and end apart: 6 -> 3, of which waited for: 5 -> 1; matrix products, arithmetic and copies ran while one was open for 4% -> 0% of each run, Pallas kernels for 5% -> 0%
where the time goes in v2:
time: 125 us
  blocking collectives  88.4 us (71%)
  Pallas kernels  14.5 us (12%)
  waiting for transfers between devices  12.1 us (10%)
  starting transfers between devices  9.1 us (7%)
    all_to_all x3, blocking collectives, exchange(): return lax.all_to_all(x, axes, 0, 0, tiled=True)  88.4 us
    ppermute x1, waiting for transfers between devices, cross(): return lax.ppermute(x, ('xh', 'xl'), [(0, 3), (3, 0), (1, 2), (2, 1)])  12.1 us
    pallas_call x1, Pallas kernels, clip_sums(): pl.pallas_call(clip_kernel, grid=(CLIPS // CHUNK,), in_specs=[whole(1, CL...  9.09 us
    ppermute x2, starting transfers between devices, swap(): return lax.ppermute(x, 'c', [(0, 1), (1, 0)])  7.65 us
  transfers between devices with their start and end apart: 3, of which 1 were waited for; matrix products, arithmetic and copies ran while one was open for 0% of the time, Pallas kernels for 0%

profile of v2, /device:TPU:1, one launch (start us, length us, event | category | flops | bytes accessed | tf_op | source)
XLA Modules:
  0.0 124.8 jit_solution(8603124755890976037)
XLA Ops:
  0.6 0.0 slice-start
  0.6 0.0 slice-start.1
  0.7 9.1 %shard_map.93 = (bf16[512,1664]{1,0:T(8,128)(2,1)}, f32[8,768]{1,0:T(8,128)}, f32[8,1]{1,0:T(8,128)}) custom-call(s32[1,64]{1,0:T(1,128)} %bitcast.13, bf16[1024,3200]{1,0:T(8,128)(2,1)} %bitcast.11, bf16[25,3200]{1,0:T(8,128)(2,1)} %pool_ref.1, bf16[8,768]{1,0:T(8,128)(2,1)} %text_ref.1, s32[1,8]{1,0:T(1,128)} %bitcast.14), custom_call_target="tpu_custom_call" | custom-call | flops 419430400 | bytes 8388608 | tf_op jit(solution)/shard_map/pallas_call | solution.py:138
  9.7 53.4 %all_to_all.15 = bf16[64,8,1664]{2,1,0:T(8,128)(2,1)S(1)} all-to-all(bf16[64,8,1664]{2,1,0:T(8,128)(2,1)} %bitcast.12), channel_id=1, replica_groups=mesh['xh'=2,'c'=2,'xl'=2,'z'=8,'y'=4] {'xl','z','y'}, dimensions={0} | all-to-all | bytes 3407872 | tf_op jit(solution)/shard_map/all_to_all | solution.py:373
  63.2 0.0 slice-done
  63.2 0.0 slice-done.1
  63.2 0.0 copy-start
  63.2 0.0 copy-start.1
  63.2 2.3 %shard_map.94 = (bf16[8,768]{1,0:T(8,128)(2,1)}, f32[8,768]{1,0:T(8,128)S(1)}, f32[8,1]{1,0:T(8,128)S(1)}, bf16[32,8,768]{2,1,0:T(8,128)(2,1)S(1)}, bf16[512,768]{1,0:T(8,128)(2,1)S(1)}, /*index=5*/f32[512,1]{1,0:T(8,128)S(1)}) custom-call(bf16[512,1664]{1,0:T(8,128)(2,1)S(1)} %bitcast.7, bf16[3200,768]{1,0:T(8,128)(2,1)S(1)} %bitcast.9), custom_call_target="tpu_custom_call" | custom-call | flops 117964800 | bytes 6291456 | tf_op jit(solution)/shard_map/pallas_call | solution.py:210
  65.5 1.5 %collective-permute-start.1 = (bf16[512,768]{1,0:T(8,128)(2,1)S(1)}, bf16[512,768]{1,0:T(8,128)(2,1)S(1)}, u32[]{:S(2)}, u32[]{:S(2)}) collective-permute-start(bf16[512,768]{1,0:T(8,128)(2,1)S(1)} %get-tuple-element.22.set0_ref), channel_id=1, source_target_pairs={{0,160},{160,0},{32,128},{128,32},{1,161},{161,1},{33,129},{129,33... | collective-permute-start | bytes 2359304 | tf_op jit(solution)/shard_map/ppermute | solution.py:381
  66.9 3.5 %collective-permute-start = (bf16[512,768]{1,0:T(8,128)(2,1)S(1)}, bf16[512,768]{1,0:T(8,128)(2,1)S(1)}, u32[]{:S(2)}, u32[]{:S(2)}) collective-permute-start(bf16[512,768]{1,0:T(8,128)(2,1)S(1)} %get-tuple-element.22.set0_ref), channel_id=1, source_target_pairs={{0,64},{64,0},{1,65},{65,1},{2,66},{66,2},{3,67},{67,3},{4,68},{68... | collective-permute-start | bytes 2359304 | tf_op jit(solution)/shard_map/ppermute | solution.py:377
  70.4 12.1 %collective-permute-done.1.set2_ref = bf16[512,768]{1,0:T(8,128)(2,1)S(1)} collective-permute-done((bf16[512,768]{1,0:T(8,128)(2,1)S(1)}, bf16[512,768]{1,0:T(8,128)(2,1)S(1)}, u32[]{:S(2)}, u32[]{:S(2)}) %collective-permute-start.1) | collective-permute-done | bytes 786464 | tf_op jit(solution)/shard_map/ppermute | solution.py:381
  82.5 4.2 %collective-permute-start.2 = (bf16[512,768]{1,0:T(8,128)(2,1)S(1)}, bf16[512,768]{1,0:T(8,128)(2,1)S(1)}, u32[]{:S(2)}, u32[]{:S(2)}) collective-permute-start(bf16[512,768]{1,0:T(8,128)(2,1)S(1)} %collective-permute-done.1.set2_ref), channel_id=1, source_target_pairs={{0,64},{64,0},{1,65},{65,1},{2,66},{66,2},{3,67},{67,3},{4,68},{68... | collective-permute-start | bytes 2359304 | tf_op jit(solution)/shard_map/ppermute | solution.py:377
  86.6 21.7 %all_to_all.16 = bf16[32,8,768]{2,1,0:T(8,128)(2,1)S(1)} all-to-all(bf16[32,8,768]{2,1,0:T(8,128)(2,1)S(1)} %get-tuple-element.20), channel_id=1, replica_groups=mesh['xh'=2,'c'=2,'xl'=2,'z'=8,'y'=4] {'z','y'}, dimensions={0} | all-to-all | bytes 786432 | tf_op jit(solution)/shard_map/all_to_all | solution.py:373
  108.3 0.0 collective-permute-done.set1_ref
  108.3 0.0 collective-permute-done.2.set3_ref
  108.4 1.9 %shard_map.95 = (f32[8,8,1920]{2,1,0:T(8,128)S(1)}, f32[8,2048]{1,0:T(8,128)S(1)}) custom-call(bf16[256,768]{1,0:T(8,128)(2,1)S(1)} %bitcast.10, f32[512,1]{1,0:T(8,128)S(1)} %get-tuple-element.21.target_ref, bf16[512,768]{1,0:T(8,128)(2,1)S(1)} %get-tuple-element.22.set0_ref, bf16[512,768]{1,0:T(8,128)(2,1)S(1)} %collective-permute-done.set1_ref, ...), custom_call_target="tpu_custom_call" | custom-call | flops 805306368 | bytes 5242880 | tf_op jit(solution)/shard_map/pallas_call | solution.py:297
  110.2 13.2 %all_to_all.17.arrived_ref = f32[8,8,1920]{2,1,0:T(8,128)S(1)} all-to-all(f32[8,8,1920]{2,1,0:T(8,128)S(1)} %get-tuple-element.23), channel_id=1, replica_groups=mesh['xh'=2,'c'=2,'xl'=2,'z'=8,'y'=4] {'xh','c','xl'}, dimensions={0} | all-to-all | bytes 983040 | tf_op jit(solution)/shard_map/all_to_all | solution.py:373
  123.5 0.0 copy-done
  123.5 0.0 copy-done.1
  123.5 1.3 %shard_map.96 = (f32[1,1]{1,0:T(1,128)}, f32[8,768]{1,0:T(8,128)}, f32[8,768]{1,0:T(8,128)}) custom-call(f32[8,8,1920]{2,1,0:T(8,128)S(1)} %all_to_all.17.arrived_ref, f32[8,2048]{1,0:T(8,128)S(1)} %get-tuple-element.24.own_ref, f32[512,1]{1,0:T(8,128)S(1)} %get-tuple-element.21.target_ref, bf16[512,768]{1,0:T(8,128)(2,1)S(1)} %get-tuple-element.22.set0_ref, ...), custom_call_target="tpu_custom_call" | custom-call | flops 25165824 | bytes 5242880 | tf_op jit(solution)/shard_map/pallas_call | solution.py:355
  (1 shorter events, 0.0 us)
Async XLA Ops:
  0.6 62.5 %slice-start = ((s8[4915200]{0:T(1024)(128)(4,1)}), s8[4194304]{0:T(1024)(128)(4,1)S(1)}, s32[]{:S(2)}) async-start(s8[4915200]{0:T(1024)(128)(4,1)} %bitcast.8), calls=%async_computation.3 | async-start | bytes 8388608
  0.6 62.5 %slice-start.1 = ((s8[4915200]{0:T(1024)(128)(4,1)}), s8[720896]{0:T(1024)(128)(4,1)S(1)}, s32[]{:S(2)}) async-start(s8[4915200]{0:T(1024)(128)(4,1)} %bitcast.8), calls=%async_computation.4 | async-start | bytes 1441792
  63.2 60.3 %copy-start = (f32[8,768]{1,0:T(8,128)S(1)}, f32[8,768]{1,0:T(8,128)}, u32[]{:S(2)}) copy-start(f32[8,768]{1,0:T(8,128)} %get-tuple-element.27.text_hat_ref) | copy-start | bytes 73732
  63.2 60.3 %copy-start.1 = (f32[8,1]{1,0:T(8,128)S(1)}, f32[8,1]{1,0:T(8,128)}, u32[]{:S(2)}) copy-start(f32[8,1]{1,0:T(8,128)} %get-tuple-element.28.text_norm_ref) | copy-start | bytes 100
  65.5 17.0 %collective-permute-start.1 = (bf16[512,768]{1,0:T(8,128)(2,1)S(1)}, bf16[512,768]{1,0:T(8,128)(2,1)S(1)}, u32[]{:S(2)}, u32[]{:S(2)}) collective-permute-start(bf16[512,768]{1,0:T(8,128)(2,1)S(1)} %get-tuple-element.22.set0_ref), channel_id=1, source_target_pairs={{0,160},{160,0},{32,128},{128,32},{1,161},{161,1},{33,129},{129,33... | collective-permute-start | bytes 2359304 | tf_op jit(solution)/shard_map/ppermute | solution.py:381
  66.9 41.4 %collective-permute-start = (bf16[512,768]{1,0:T(8,128)(2,1)S(1)}, bf16[512,768]{1,0:T(8,128)(2,1)S(1)}, u32[]{:S(2)}, u32[]{:S(2)}) collective-permute-start(bf16[512,768]{1,0:T(8,128)(2,1)S(1)} %get-tuple-element.22.set0_ref), channel_id=1, source_target_pairs={{0,64},{64,0},{1,65},{65,1},{2,66},{66,2},{3,67},{67,3},{4,68},{68... | collective-permute-start | bytes 2359304 | tf_op jit(solution)/shard_map/ppermute | solution.py:377
  82.5 25.9 %collective-permute-start.2 = (bf16[512,768]{1,0:T(8,128)(2,1)S(1)}, bf16[512,768]{1,0:T(8,128)(2,1)S(1)}, u32[]{:S(2)}, u32[]{:S(2)}) collective-permute-start(bf16[512,768]{1,0:T(8,128)(2,1)S(1)} %collective-permute-done.1.set2_ref), channel_id=1, source_target_pairs={{0,64},{64,0},{1,65},{65,1},{2,66},{66,2},{3,67},{67,3},{4,68},{68... | collective-permute-start | bytes 2359304 | tf_op jit(solution)/shard_map/ppermute | solution.py:377

commit v3 on v2

--- a/solution.py
+++ b/solution.py
@@ -18,8 +18,9 @@
 ROW = ("xl", "z", "y")
 PLANE = ("z", "y")
 GROUP = ("xh", "c", "xl")
-CHUNK = 16
+CHUNK = 32
 TOKS = CHUNK * TOK
+STEPS = CLIPS // CHUNK
 PARTS = 4
 WIDE = 7
 SENT = WIDE * HD
@@ -54,115 +55,135 @@
 
 
 def clip_kernel(
-    video_ref, token_ref, pool_ref, text_ref, pair_ref,
-    out_ref, hat_ref, norm_ref, weight_scr, num_scr,
+    video_hbm, token_hbm, pool_hbm, text_hbm, pair_hbm,
+    out_ref, hat_ref, norm_ref,
+    video_ref, token_ref, pool_ref, text_ref, pair_ref, weight_scr, num_scr, sems,
 ):
-    step = pl.program_id(0)
-
-    @pl.when(step == 0)
-    def _():
-        weight_scr[...] = jnp.zeros_like(weight_scr)
-        num_scr[...] = jnp.zeros_like(num_scr)
-        hat, norm = unit_rows(text_ref[...].astype(f32))
-        hat_ref[...] = hat
-        norm_ref[...] = norm
-        texts = jnp.broadcast_to(hat[None], (CLIPS, 8, E)).reshape(CLIPS * 8, E)
-        out_ref[:, SENT : SENT + E] = texts.astype(bf16)
-
-    x = token_ref[...]
-    scores = dot(pool_ref[...], x, NT)
-    weights = jnp.exp(SOFT_CAP * jnp.tanh(scores / SOFT_CAP))
-    weight_scr[0:H, :] = weights
-    weight_scr[32 : 32 + H, :] = weights
+    small = ((pool_hbm, pool_ref), (video_hbm, video_ref), (text_hbm, text_ref), (pair_hbm, pair_ref))
+    chunks = [pl.ds(i * TOKS, TOKS) for i in range(STEPS)]
+    loads = [
+        pltpu.make_async_copy(token_hbm.at[chunk], token_ref.at[chunk], sems.at[i])
+        for i, chunk in enumerate(chunks)
+    ]
+    early = [
+        pltpu.make_async_copy(src, dst, sems.at[STEPS + i]) for i, (src, dst) in enumerate(small)
+    ]
+    early[0].start()
+    loads[0].start()
+    for copy in early[1:] + loads[1:]:
+        copy.start()
+    weight_scr[...] = jnp.zeros_like(weight_scr)
+    num_scr[...] = jnp.zeros_like(num_scr)
     mine = iota((CHUNK, TOKS), 1) // TOK == iota((CHUNK, TOKS), 0)
-    den = dot(mine.astype(f32).astype(bf16), weight_scr[...].astype(bf16), NT)
-    den_hi = den.astype(bf16).astype(f32)
-    here = iota((CHUNK, CLIPS), 1) == iota((CHUNK, CLIPS), 0) + step * CHUNK
-    video = jnp.broadcast_to(video_ref[...].astype(f32), (CHUNK, CLIPS))
-    video = jnp.sum(jnp.where(here, video, 0.0), axis=1, keepdims=True).astype(jnp.int32)
+    ones = mine.astype(f32).astype(bf16)
     lane = iota((CHUNK, HD), 1)
-    local = jnp.where(lane - 64 == video % 8, 1.0, 0.0)
-    tail = jnp.where(lane < 32, den_hi, jnp.where(lane < 64, den - den_hi, local))
-
-    def put(j, value):
-        rows = pl.ds(pl.multiple_of(j // WIDE * CLIPS + step * CHUNK, CHUNK), CHUNK)
-        num_scr[rows, j % WIDE * HD : (j % WIDE + 1) * HD] = value.astype(bf16)
-
-    put(H, tail)
-    for h in range(0, H, 2):
-        pair = range(h, min(h + 2, H))
-        lhs = jnp.concatenate(
-            [
-                jnp.where(mine, jnp.broadcast_to(weight_scr[k : k + 1, :], (CHUNK, TOKS)), 0.0)
-                for k in pair
-            ],
-            axis=0,
-        ).astype(bf16)
-        part = dot(lhs, x[:, h * HD : (h + len(pair)) * HD])
-        for n, k in enumerate(pair):
-            put(k, part[n * CHUNK : (n + 1) * CHUNK, n * HD : (n + 1) * HD])
-
-    @pl.when(step == pl.num_programs(0) - 1)
-    def _():
-        owner = (video_ref[...] // 8).astype(f32)
-        before = (column_of(owner) == owner) & (
-            iota((CLIPS, CLIPS), 0) < iota((CLIPS, CLIPS), 1)
-        )
-        rank = jnp.sum(jnp.where(before, 1.0, 0.0), axis=0, keepdims=True)
-        slot = owner * 2.0 + rank
-        slots = jnp.concatenate([slot] * PARTS, axis=1).astype(jnp.int32)
-        shape = (CLIPS * 8, PARTS * CLIPS)
-        row, col = iota(shape, 0), iota(shape, 1)
-        place = (row // PARTS == slots) & (row % PARTS == col // CLIPS)
-        out = dot(jnp.where(place, 1.0, 0.0).astype(bf16), num_scr[...])
-        pair = pair_ref[...]
-        codes = jnp.concatenate(
-            [
-                jnp.zeros((1, 72), f32),
-                (pair // 64).astype(f32),
-                (pair % 64).astype(f32),
-                jnp.zeros((1, 40), f32),
-            ],
-            axis=1,
-        )
-        last = iota((CLIPS * 8, HD), 0) % PARTS == PARTS - 1
-        out_ref[:, 0:TAIL] = out[:, 0:TAIL].astype(bf16)
-        out_ref[:, TAIL : TAIL + HD] = (
-            out[:, TAIL : TAIL + HD] + jnp.where(last, codes, 0.0)
-        ).astype(bf16)
-        out_ref[:, TAIL + HD : SENT] = out[:, TAIL + HD : SENT].astype(bf16)
+    for copy in early[1:]:
+        copy.wait()
+    videos = video_ref[...].astype(f32)
+    hat, norm = unit_rows(text_ref[...].astype(f32))
+    hat_ref[...] = hat
+    norm_ref[...] = norm
+    texts = jnp.broadcast_to(hat[None], (CLIPS, 8, E)).reshape(CLIPS * 8, E)
+    out_ref[:, SENT : SENT + E] = texts.astype(bf16)
+    early[0].wait()
+    pool = pool_ref[...]
+
+    def put(step, j, value):
+        at = j // WIDE * CLIPS + step * CHUNK
+        num_scr[at : at + CHUNK, j % WIDE * HD : (j % WIDE + 1) * HD] = value.astype(bf16)
+
+    def weigh(step):
+        loads[step].wait()
+        scores = dot(pool, token_ref[chunks[step], :], NT)
+        weights = jnp.exp(SOFT_CAP * jnp.tanh(scores / SOFT_CAP))
+        weight_scr[step, 0:H, :] = weights
+        weight_scr[step, 32 : 32 + H, :] = weights
+
+    def total(step):
+        den = dot(ones, weight_scr[step].astype(bf16), NT)
+        den_hi = den.astype(bf16).astype(f32)
+        here = iota((CHUNK, CLIPS), 1) == iota((CHUNK, CLIPS), 0) + step * CHUNK
+        video = jnp.where(here, jnp.broadcast_to(videos, (CHUNK, CLIPS)), 0.0)
+        video = jnp.sum(video, axis=1, keepdims=True).astype(jnp.int32)
+        local = jnp.where(lane - 64 == video % 8, 1.0, 0.0)
+        tail = jnp.where(lane < 32, den_hi, jnp.where(lane < 64, den - den_hi, local))
+        put(step, H, tail)
+        for h in range(0, H, 2):
+            pair = range(h, min(h + 2, H))
+            lhs = jnp.concatenate(
+                [
+                    jnp.where(
+                        mine, jnp.broadcast_to(weight_scr[step, k : k + 1, :], (CHUNK, TOKS)), 0.0
+                    )
+                    for k in pair
+                ],
+                axis=0,
+            ).astype(bf16)
+            part = dot(lhs, token_ref[chunks[step], h * HD : (h + len(pair)) * HD])
+            for n, k in enumerate(pair):
+                put(step, k, part[n * CHUNK : (n + 1) * CHUNK, n * HD : (n + 1) * HD])
+
+    for step in range(STEPS):
+        weigh(step)
+        if step:
+            total(step - 1)
+    total(STEPS - 1)
+
+    owner = (video_ref[...] // 8).astype(f32)
+    before = (column_of(owner) == owner) & (iota((CLIPS, CLIPS), 0) < iota((CLIPS, CLIPS), 1))
+    rank = jnp.sum(jnp.where(before, 1.0, 0.0), axis=0, keepdims=True)
+    slot = owner * 2.0 + rank
+    slots = jnp.concatenate([slot] * PARTS, axis=1).astype(jnp.int32)
+    shape = (CLIPS * 8, PARTS * CLIPS)
+    row, col = iota(shape, 0), iota(shape, 1)
+    place = (row // PARTS == slots) & (row % PARTS == col // CLIPS)
+    out = dot(jnp.where(place, 1.0, 0.0).astype(bf16), num_scr[...])
+    pair = pair_ref[...]
+    codes = jnp.concatenate(
+        [
+            jnp.zeros((1, 72), f32),
+            (pair // 64).astype(f32),
+            (pair % 64).astype(f32),
+            jnp.zeros((1, 40), f32),
+        ],
+        axis=1,
+    )
+    last = iota((CLIPS * 8, HD), 0) % PARTS == PARTS - 1
+    out_ref[:, 0:TAIL] = out[:, 0:TAIL].astype(bf16)
+    out_ref[:, TAIL : TAIL + HD] = (
+        out[:, TAIL : TAIL + HD] + jnp.where(last, codes, 0.0)
+    ).astype(bf16)
+    out_ref[:, TAIL + HD : SENT] = out[:, TAIL + HD : SENT].astype(bf16)
 
 
 def clip_sums(clip_tokens, clip_video, pool_vectors, text_embed, pair_text):
-    whole = lambda *shape: pl.BlockSpec(shape, lambda i: (0,) * len(shape))
-    return pl.pallas_call(
-        clip_kernel,
-        grid=(CLIPS // CHUNK,),
-        in_specs=[
-            whole(1, CLIPS),
-            pl.BlockSpec((TOKS, D), lambda i: (i, 0)),
-            whole(H, D),
-            whole(8, E),
-            whole(1, 8),
-        ],
-        out_specs=[whole(CLIPS * 8, SENT + E), whole(8, E), whole(8, 1)],
-        out_shape=[
-            jax.ShapeDtypeStruct((CLIPS * 8, SENT + E), bf16),
-            jax.ShapeDtypeStruct((8, E), f32),
-            jax.ShapeDtypeStruct((8, 1), f32),
-        ],
-        scratch_shapes=[pltpu.VMEM((128, TOKS), f32), pltpu.VMEM((PARTS * CLIPS, SENT), bf16)],
-        compiler_params=pltpu.CompilerParams(vmem_limit_bytes=56 << 20),
-        cost_estimate=pl.CostEstimate(
-            flops=2 * 1024 * D * 64, bytes_accessed=8 << 20, transcendentals=1 << 17
-        ),
-    )(
+    args = (
         clip_video.reshape(1, CLIPS),
         clip_tokens.reshape(CLIPS * TOK, D),
         pool_vectors,
         text_embed,
         pair_text.reshape(1, 8),
     )
+    return pl.pallas_call(
+        clip_kernel,
+        in_specs=[pl.BlockSpec(memory_space=pltpu.HBM)] * 5,
+        out_specs=[VMEM] * 3,
+        out_shape=[
+            jax.ShapeDtypeStruct((CLIPS * 8, SENT + E), bf16),
+            jax.ShapeDtypeStruct((8, E), f32),
+            jax.ShapeDtypeStruct((8, 1), f32),
+        ],
+        scratch_shapes=[pltpu.VMEM(x.shape, x.dtype) for x in args]
+        + [
+            pltpu.VMEM((STEPS, 128, TOKS), f32),
+            pltpu.VMEM((PARTS * CLIPS, SENT), bf16),
+            pltpu.SemaphoreType.DMA((STEPS + 4,)),
+        ],
+        compiler_params=pltpu.CompilerParams(vmem_limit_bytes=24 << 20),
+        cost_estimate=pl.CostEstimate(
+            flops=2 * 1024 * D * 64, bytes_accessed=8 << 20, transcendentals=1 << 17
+        ),
+    )(*(pltpu.with_memory_space_constraint(x, pltpu.HBM) for x in args))
 
 
 def embed_kernel(
@@ -390,8 +411,9 @@
         arrived.reshape(CLIPS * 8, SENT + E), out_proj
     )
     crossed = cross(texts)
+    videos, crossed = lax.optimization_barrier((exchange(send, PLANE), crossed))
+    videos = videos.reshape(PLANE_ROWS, E)
     sets = (texts, swap(texts), crossed, swap(crossed))
-    videos = exchange(send, PLANE).reshape(PLANE_ROWS, E)
     terms, own = all_logits(videos, target, *sets)
     loss, video_grad, text_grad = gradients(
         exchange(terms, GROUP), own, target, *sets, video_hat, video_norm, text_hat, text_norm

time: 125 us -> 105 us (0.84)
  blocking collectives: 88.4 us -> 65 us
  starting transfers between devices: 9.1 us -> 14.6 us
  Pallas kernels: 14.5 us -> 11.7 us
    all_to_all x3 -> x2, blocking collectives: 88.4 us -> 65 us  [exchange(): return lax.all_to_all(x, axes, 0, 0, tiled=True)]
    ppermute x1, waiting for transfers between devices: 12.1 us -> 0.01 us  [cross(): return lax.ppermute(x, ('xh', 'xl'), [(0, 3), (3, 0), (1, 2), (2, 1)])]
    all_to_all x0 -> x1, waiting for transfers between devices: none -> 10.4 us  [exchange(): return lax.all_to_all(x, axes, 0, 0, tiled=True)]
    all_to_all x0 -> x1, starting transfers between devices: none -> 7.28 us  [exchange(): return lax.all_to_all(x, axes, 0, 0, tiled=True)]
    pallas_call x1, Pallas kernels: 9.09 us -> 6.02 us  [clip_sums(): pl.pallas_call(clip_kernel, in_specs=[pl.BlockSpec(memory_space=pltpu.HBM...]
    ppermute x2, waiting for transfers between devices: 0.01 us -> 1.91 us  [swap(): return lax.ppermute(x, 'c', [(0, 1), (1, 0)])]
    ppermute x2, starting transfers between devices: 7.65 us -> 5.86 us  [swap(): return lax.ppermute(x, 'c', [(0, 1), (1, 0)])]
  transfers between devices with their start and end apart: 3 -> 4, of which waited for: 1 -> 2; matrix products, arithmetic and copies ran while one was open for 0% -> 0% of each run, Pallas kernels for 0% -> 0%
where the time goes in v3:
time: 105 us; the launch traced here: 104 us
  blocking collectives  65 us (62%)
  starting transfers between devices  14.6 us (14%)
  waiting for transfers between devices  12.3 us (12%)
  Pallas kernels  11.7 us (11%)
    all_to_all x2, blocking collectives, exchange(): return lax.all_to_all(x, axes, 0, 0, tiled=True)  65 us
    all_to_all x1, waiting for transfers between devices, exchange(): return lax.all_to_all(x, axes, 0, 0, tiled=True)  10.4 us
    all_to_all x1, starting transfers between devices, exchange(): return lax.all_to_all(x, axes, 0, 0, tiled=True)  7.28 us
    pallas_call x1, Pallas kernels, clip_sums(): pl.pallas_call(clip_kernel, in_specs=[pl.BlockSpec(memory_space=pltpu.HBM...  6.02 us
    ppermute x2, starting transfers between devices, swap(): return lax.ppermute(x, 'c', [(0, 1), (1, 0)])  5.86 us
    pallas_call x1, Pallas kernels, embed(): pl.pallas_call(embed_kernel, in_specs=[VMEM, VMEM], out_specs=[VMEM] * 6,...  2.54 us
  transfers between devices with their start and end apart: 4, of which 2 were waited for; matrix products, arithmetic and copies ran while one was open for 0% of the time, Pallas kernels for 0%

profile of v3, /device:TPU:1, one launch (start us, length us, event | category | flops | bytes accessed | tf_op | source)
XLA Modules:
  0.0 104.2 jit_solution(5980904416743864260)
XLA Ops:
  0.6 0.0 slice-start
  0.6 0.0 slice-start.1
  0.7 6.0 %shard_map.93 = (bf16[512,1664]{1,0:T(8,128)(2,1)S(1)}, f32[8,768]{1,0:T(8,128)S(1)}, f32[8,1]{1,0:T(8,128)S(1)}) custom-call(s32[1,64]{1,0:T(1,128)} %bitcast.13, bf16[1024,3200]{1,0:T(8,128)(2,1)} %bitcast.12, bf16[25,3200]{1,0:T(8,128)(2,1)} %pool_hbm.1, bf16[8,768]{1,0:T(8,128)(2,1)} %text_hbm.1, s32[1,8]{1,0:T(1,128)} %bitcast.14), custom_call_target="tpu_custom_call" | custom-call | flops 419430400 | bytes 8388608 | tf_op jit(solution)/shard_map/pallas_call | solution.py:167
  6.7 53.2 %all_to_all.15 = bf16[64,8,1664]{2,1,0:T(8,128)(2,1)S(1)} all-to-all(bf16[64,8,1664]{2,1,0:T(8,128)(2,1)S(1)} %bitcast.10), channel_id=1, replica_groups=mesh['xh'=2,'c'=2,'xl'=2,'z'=8,'y'=4] {'xl','z','y'}, dimensions={0} | all-to-all | bytes 3407872 | tf_op jit(solution)/shard_map/all_to_all | solution.py:394
  59.9 0.0 slice-done
  59.9 0.0 slice-done.1
  59.9 2.5 %shard_map.94 = (bf16[8,768]{1,0:T(8,128)(2,1)}, f32[8,768]{1,0:T(8,128)S(1)}, f32[8,1]{1,0:T(8,128)S(1)}, bf16[32,8,768]{2,1,0:T(8,128)(2,1)}, bf16[512,768]{1,0:T(8,128)(2,1)S(1)}, /*index=5*/f32[512,1]{1,0:T(8,128)S(1)}) custom-call(bf16[512,1664]{1,0:T(8,128)(2,1)S(1)} %bitcast.7, bf16[3200,768]{1,0:T(8,128)(2,1)S(1)} %bitcast.9), custom_call_target="tpu_custom_call" | custom-call | flops 117964800 | bytes 6291456 | tf_op jit(solution)/shard_map/pallas_call | solution.py:231
  62.5 1.4 %collective-permute-start = (bf16[512,768]{1,0:T(8,128)(2,1)S(1)}, bf16[512,768]{1,0:T(8,128)(2,1)S(1)}, u32[]{:S(2)}, u32[]{:S(2)}) collective-permute-start(bf16[512,768]{1,0:T(8,128)(2,1)S(1)} %get-tuple-element.23.set0_ref), channel_id=1, source_target_pairs={{0,160},{160,0},{32,128},{128,32},{1,161},{161,1},{33,129},{129,33... | collective-permute-start | bytes 2359304 | tf_op jit(solution)/shard_map/ppermute | solution.py:402
  63.9 7.3 %all-to-all-start.1 = ((bf16[32,8,768]{2,1,0:T(8,128)(2,1)}), bf16[32,8,768]{2,1,0:T(8,128)(2,1)S(1)}, u32[]{:S(2)}, u32[]{:S(2)}) async-start(bf16[32,8,768]{2,1,0:T(8,128)(2,1)} %get-tuple-element.22), calls=%async_computation.1 | async-start | bytes 786432 | tf_op jit(solution)/shard_map/all_to_all | solution.py:394
  71.2 2.2 %collective-permute-start.1 = (bf16[512,768]{1,0:T(8,128)(2,1)S(1)}, bf16[512,768]{1,0:T(8,128)(2,1)S(1)}, u32[]{:S(2)}, u32[]{:S(2)}) collective-permute-start(bf16[512,768]{1,0:T(8,128)(2,1)S(1)} %get-tuple-element.23.set0_ref), channel_id=1, source_target_pairs={{0,64},{64,0},{1,65},{65,1},{2,66},{66,2},{3,67},{67,3},{4,68},{68... | collective-permute-start | bytes 2359304 | tf_op jit(solution)/shard_map/ppermute | solution.py:398
  73.3 10.4 %all-to-all-done.1 = bf16[32,8,768]{2,1,0:T(8,128)(2,1)S(1)} async-done(((bf16[32,8,768]{2,1,0:T(8,128)(2,1)}), bf16[32,8,768]{2,1,0:T(8,128)(2,1)S(1)}, u32[]{:S(2)}, u32[]{:S(2)}) %all-to-all-start.1) | async-done | bytes 393248 | tf_op jit(solution)/shard_map/all_to_all | solution.py:394
  83.7 0.0 collective-permute-done.set2_ref
  83.7 3.7 %collective-permute-start.2 = (bf16[512,768]{1,0:T(8,128)(2,1)S(1)}, bf16[512,768]{1,0:T(8,128)(2,1)S(1)}, u32[]{:S(2)}, u32[]{:S(2)}) collective-permute-start(bf16[512,768]{1,0:T(8,128)(2,1)S(1)} %collective-permute-done.set2_ref), channel_id=1, source_target_pairs={{0,64},{64,0},{1,65},{65,1},{2,66},{66,2},{3,67},{67,3},{4,68},{68... | collective-permute-start | bytes 2359304 | tf_op jit(solution)/shard_map/ppermute | solution.py:398
  87.4 0.0 collective-permute-done.1.set1_ref
  87.4 1.9 %collective-permute-done.2.set3_ref = bf16[512,768]{1,0:T(8,128)(2,1)S(1)} collective-permute-done((bf16[512,768]{1,0:T(8,128)(2,1)S(1)}, bf16[512,768]{1,0:T(8,128)(2,1)S(1)}, u32[]{:S(2)}, u32[]{:S(2)}) %collective-permute-start.2) | collective-permute-done | bytes 786464 | tf_op jit(solution)/shard_map/ppermute | solution.py:398
  89.3 1.9 %shard_map.95 = (f32[8,8,1920]{2,1,0:T(8,128)S(1)}, f32[8,2048]{1,0:T(8,128)S(1)}) custom-call(bf16[256,768]{1,0:T(8,128)(2,1)S(1)} %bitcast.11, f32[512,1]{1,0:T(8,128)S(1)} %get-tuple-element.25.target_ref, bf16[512,768]{1,0:T(8,128)(2,1)S(1)} %get-tuple-element.23.set0_ref, bf16[512,768]{1,0:T(8,128)(2,1)S(1)} %collective-permute-done.1.set1_ref, ...), custom_call_target="tpu_custom_call" | custom-call | flops 805306368 | bytes 5242880 | tf_op jit(solution)/shard_map/pallas_call | solution.py:318
  91.2 11.7 %all_to_all.16.arrived_ref = f32[8,8,1920]{2,1,0:T(8,128)S(1)} all-to-all(f32[8,8,1920]{2,1,0:T(8,128)S(1)} %get-tuple-element.27), channel_id=1, replica_groups=mesh['xh'=2,'c'=2,'xl'=2,'z'=8,'y'=4] {'xh','c','xl'}, dimensions={0} | all-to-all | bytes 983040 | tf_op jit(solution)/shard_map/all_to_all | solution.py:394
  102.9 1.3 %shard_map.96 = (f32[1,1]{1,0:T(1,128)}, f32[8,768]{1,0:T(8,128)}, f32[8,768]{1,0:T(8,128)}) custom-call(f32[8,8,1920]{2,1,0:T(8,128)S(1)} %all_to_all.16.arrived_ref, f32[8,2048]{1,0:T(8,128)S(1)} %get-tuple-element.28.own_ref, f32[512,1]{1,0:T(8,128)S(1)} %get-tuple-element.25.target_ref, bf16[512,768]{1,0:T(8,128)(2,1)S(1)} %get-tuple-element.23.set0_ref, ...), custom_call_target="tpu_custom_call" | custom-call | flops 25165824 | bytes 5242880 | tf_op jit(solution)/shard_map/pallas_call | solution.py:376
  (1 shorter events, 0.0 us)
Async XLA Ops:
  0.6 59.3 %slice-start = ((s8[4915200]{0:T(1024)(128)(4,1)}), s8[4194304]{0:T(1024)(128)(4,1)S(1)}, s32[]{:S(2)}) async-start(s8[4915200]{0:T(1024)(128)(4,1)} %bitcast.8), calls=%async_computation.3 | async-start | bytes 8388608
  0.6 59.3 %slice-start.1 = ((s8[4915200]{0:T(1024)(128)(4,1)}), s8[720896]{0:T(1024)(128)(4,1)S(1)}, s32[]{:S(2)}) async-start(s8[4915200]{0:T(1024)(128)(4,1)} %bitcast.8), calls=%async_computation.4 | async-start | bytes 1441792
  62.5 21.3 %collective-permute-start = (bf16[512,768]{1,0:T(8,128)(2,1)S(1)}, bf16[512,768]{1,0:T(8,128)(2,1)S(1)}, u32[]{:S(2)}, u32[]{:S(2)}) collective-permute-start(bf16[512,768]{1,0:T(8,128)(2,1)S(1)} %get-tuple-element.23.set0_ref), channel_id=1, source_target_pairs={{0,160},{160,0},{32,128},{128,32},{1,161},{161,1},{33,129},{129,33... | collective-permute-start | bytes 2359304 | tf_op jit(solution)/shard_map/ppermute | solution.py:402
  63.9 19.8 %all-to-all-start.1 = ((bf16[32,8,768]{2,1,0:T(8,128)(2,1)}), bf16[32,8,768]{2,1,0:T(8,128)(2,1)S(1)}, u32[]{:S(2)}, u32[]{:S(2)}) async-start(bf16[32,8,768]{2,1,0:T(8,128)(2,1)} %get-tuple-element.22), calls=%async_computation.1 | async-start | bytes 786432 | tf_op jit(solution)/shard_map/all_to_all | solution.py:394
  71.2 16.2 %collective-permute-start.1 = (bf16[512,768]{1,0:T(8,128)(2,1)S(1)}, bf16[512,768]{1,0:T(8,128)(2,1)S(1)}, u32[]{:S(2)}, u32[]{:S(2)}) collective-permute-start(bf16[512,768]{1,0:T(8,128)(2,1)S(1)} %get-tuple-element.23.set0_ref), channel_id=1, source_target_pairs={{0,64},{64,0},{1,65},{65,1},{2,66},{66,2},{3,67},{67,3},{4,68},{68... | collective-permute-start | bytes 2359304 | tf_op jit(solution)/shard_map/ppermute | solution.py:398
  83.7 5.6 %collective-permute-start.2 = (bf16[512,768]{1,0:T(8,128)(2,1)S(1)}, bf16[512,768]{1,0:T(8,128)(2,1)S(1)}, u32[]{:S(2)}, u32[]{:S(2)}) collective-permute-start(bf16[512,768]{1,0:T(8,128)(2,1)S(1)} %collective-permute-done.set2_ref), channel_id=1, source_target_pairs={{0,64},{64,0},{1,65},{65,1},{2,66},{66,2},{3,67},{67,3},{4,68},{68... | collective-permute-start | bytes 2359304 | tf_op jit(solution)/shard_map/ppermute | solution.py:398

commit v4 on v3

--- a/solution.py
+++ b/solution.py
@@ -17,7 +17,6 @@
 ALL = ("xh", "c", "xl", "z", "y")
 ROW = ("xl", "z", "y")
 PLANE = ("z", "y")
-GROUP = ("xh", "c", "xl")
 CHUNK = 32
 TOKS = CHUNK * TOK
 STEPS = CLIPS // CHUNK
@@ -28,6 +27,7 @@
 TILE = 256
 SET = 512
 PLANE_ROWS = 256
+SUMS = 2 * E + TILE + 128
 VMEM = pl.BlockSpec(memory_space=pltpu.VMEM)
 f32 = jnp.float32
 bf16 = jnp.bfloat16
@@ -257,35 +257,53 @@
     return (xh + a - 2 * a * xh) * 2 + (c + b - 2 * b * c)
 
 
-def logits_kernel(
-    video_ref, target_ref, set0_ref, set1_ref, set2_ref, set3_ref,
-    send_ref, own_ref, tile_scr, col_scr,
+def score(videos, target, ref, row, own_ref, at, tile_scr, cols_ref, halves, positive, base):
+    lane = iota((1, TILE), 1).astype(f32)
+    for t in range(2):
+        tile = row * 2 + t
+        logits = SCALE * dot(videos, ref[t * TILE : (t + 1) * TILE, :], NT)
+        ex = jnp.exp(logits)
+        tile_scr[...] = ex
+        cols_ref[pl.ds(tile, 1), :] = jnp.sum(ex, axis=0, keepdims=True)
+        halves += ex[:, 0:128] + ex[:, 128:TILE]
+        hit = target == (tile * TILE).astype(f32) + lane
+        positive += jnp.sum(jnp.where(hit, logits, 0.0), axis=0, keepdims=True)
+        own_ref[:, at + t * TILE : at + (t + 1) * TILE] = tile_scr[pl.ds(base, 8), :]
+    return halves, positive
+
+
+def plane_rows(target_ref, xl):
+    return target_ref[pl.ds(pl.multiple_of(xl * PLANE_ROWS, PLANE_ROWS), PLANE_ROWS), :]
+
+
+def first_kernel(
+    video_ref, target_ref, set0_ref, set1_ref, set2_ref,
+    own_ref, cols_ref, halves_ref, positive_ref, tile_scr,
 ):
     xh, c, xl, spot = position()
+    target = plane_rows(target_ref, xl)
+    videos = video_ref[...]
+    base = pl.multiple_of(spot * 8, 8)
+    cols_ref[...] = jnp.zeros_like(cols_ref)
+    halves, positive = jnp.zeros((PLANE_ROWS, 128), f32), jnp.zeros((1, TILE), f32)
+    for k, ref in enumerate((set0_ref, set1_ref, set2_ref)):
+        halves, positive = score(
+            videos, target, ref, rows_of(xh, c, k), own_ref, k * SET, tile_scr, cols_ref,
+            halves, positive, base,
+        )
+    halves_ref[...] = halves
+    positive_ref[...] = positive
+
+
+def second_kernel(
+    video_ref, target_ref, set0_ref, set1_ref, set2_ref, set3_ref, cols_ref, halves_ref, positive_ref,
+    keep_ref, send_ref, own_ref, tile_scr, col_scr,
+):
+    xh, c, xl, spot = position()
+    target = plane_rows(target_ref, xl)
+    videos = video_ref[...]
+    base = pl.multiple_of(spot * 8, 8)
     sets = (set0_ref, set1_ref, set2_ref, set3_ref)
-    target = target_ref[pl.ds(pl.multiple_of(xl * PLANE_ROWS, PLANE_ROWS), PLANE_ROWS), :]
-    videos = video_ref[...]
-    lane = iota((1, TILE), 1).astype(f32)
-    base = pl.multiple_of(spot * 8, 8)
-    positive = jnp.zeros((1, TILE), f32)
-    halves = jnp.zeros((PLANE_ROWS, 128), f32)
-    for k, ref in enumerate(sets):
-        row = rows_of(xh, c, k)
-        for t in range(2):
-            tile = row * 2 + t
-            logits = SCALE * dot(videos, ref[t * TILE : (t + 1) * TILE, :], NT)
-            ex = jnp.exp(logits)
-            tile_scr[...] = ex
-            col_scr[pl.ds(tile, 1), :] = jnp.sum(ex, axis=0, keepdims=True)
-            halves += ex[:, 0:128] + ex[:, 128:TILE]
-            hit = target == (tile * TILE).astype(f32) + lane
-            positive += jnp.sum(jnp.where(hit, logits, 0.0), axis=0, keepdims=True)
-            at = k * SET + t * TILE
-            own_ref[:, at : at + TILE] = tile_scr[pl.ds(base, 8), :]
-    rowsum = jnp.sum(halves, axis=1, keepdims=True)
-    total = jnp.sum(jnp.log(rowsum), axis=0, keepdims=True) - 2.0 * jnp.sum(
-        positive, axis=1, keepdims=True
-    )
     odd = spot % 2 == 1
     near, groups = [], []
     for k, ref in enumerate(sets):
@@ -295,51 +313,99 @@
             near.append(jnp.where(odd, pair[8:16], pair[0:8]))
             groups.append(rows_of(xh, c, k) * 2 + half)
     near = jnp.concatenate(near, axis=0).astype(bf16)
-    ex = jnp.exp(SCALE * dot(videos, near, NT))
+    near = jnp.exp(SCALE * dot(videos, near, NT))
+    col_scr[...] = cols_ref[...]
+    halves, positive = score(
+        videos, target, set3_ref, rows_of(xh, c, 3), own_ref, 0, tile_scr, col_scr,
+        halves_ref[...], positive_ref[...], base,
+    )
+    rowsum = jnp.sum(halves, axis=1, keepdims=True)
+    total = jnp.sum(jnp.log(rowsum), axis=0, keepdims=True) - 2.0 * jnp.sum(
+        positive, axis=1, keepdims=True
+    )
     slot = iota((1, 64), 1)
     group = sum(jnp.where(slot // 8 == n, g, 0) for n, g in enumerate(groups))
     text = ((group * 32 + spot) * 8 + slot % 8).astype(f32)
-    first = ex / rowsum - jnp.where(target == text, 2.0, 0.0)
+    first = near / rowsum - jnp.where(target == text, 2.0, 0.0)
     first_hi = first.astype(bf16).astype(f32)
-    ex_hi = ex.astype(bf16).astype(f32)
-    terms = jnp.concatenate([first_hi, first - first_hi, ex_hi, ex - ex_hi], axis=1)
+    near_hi = near.astype(bf16).astype(f32)
+    terms = jnp.concatenate([first_hi, first - first_hi, near_hi, near - near_hi], axis=1)
     sums = dot(terms.astype(bf16), videos, TN)
     first, second = sums[0:64] + sums[64:128], sums[128:192] + sums[192:256]
     cols = col_scr[...]
     total = jnp.broadcast_to(total, (8, 128))
-    for n, g in enumerate(groups):
-        send_ref[g, :, 0:E] = first[n * 8 : (n + 1) * 8]
-        send_ref[g, :, E : 2 * E] = second[n * 8 : (n + 1) * 8]
-        send_ref[g, :, 2 * E : 2 * E + TILE] = cols
-        send_ref[g, :, 2 * E + TILE :] = total
-
-
-def all_logits(videos, target, *sets):
+    for k in range(4):
+        for half in range(2):
+            n = k * 2 + half
+            there = (xh + k // 2 - 2 * (k // 2) * xh) * 2 + half
+            step = (there - (xh * 2 + xl) + 4) % 4
+            out_ref = send_ref if k % 2 else keep_ref
+            out_ref[step, :, 0:E] = first[n * 8 : (n + 1) * 8]
+            out_ref[step, :, E : 2 * E] = second[n * 8 : (n + 1) * 8]
+            out_ref[step, :, 2 * E : 2 * E + TILE] = cols
+            out_ref[step, :, 2 * E + TILE :] = total
+
+
+def first_logits(videos, target, *sets):
     return pl.pallas_call(
-        logits_kernel,
-        in_specs=[VMEM] * 6,
-        out_specs=[VMEM] * 2,
+        first_kernel,
+        in_specs=[VMEM] * 5,
+        out_specs=[VMEM] * 4,
         out_shape=[
-            jax.ShapeDtypeStruct((8, 8, 2 * E + TILE + 128), f32),
-            jax.ShapeDtypeStruct((8, 4 * SET), f32),
-        ],
-        scratch_shapes=[pltpu.VMEM((PLANE_ROWS, TILE), f32), pltpu.VMEM((8, TILE), f32)],
-        compiler_params=pltpu.CompilerParams(vmem_limit_bytes=32 << 20),
+            jax.ShapeDtypeStruct((8, 3 * SET), f32),
+            jax.ShapeDtypeStruct((8, TILE), f32),
+            jax.ShapeDtypeStruct((PLANE_ROWS, 128), f32),
+            jax.ShapeDtypeStruct((1, TILE), f32),
+        ],
+        scratch_shapes=[pltpu.VMEM((PLANE_ROWS, TILE), f32)],
+        compiler_params=pltpu.CompilerParams(vmem_limit_bytes=24 << 20),
         cost_estimate=pl.CostEstimate(
-            flops=2 * PLANE_ROWS * 2048 * E, bytes_accessed=5 << 20, transcendentals=1 << 19
+            flops=2 * PLANE_ROWS * 1536 * E, bytes_accessed=3 << 20, transcendentals=3 << 17
         ),
     )(videos, target, *sets)
 
 
+def second_logits(*args):
+    return pl.pallas_call(
+        second_kernel,
+        in_specs=[VMEM] * 9,
+        out_specs=[VMEM] * 3,
+        out_shape=[
+            jax.ShapeDtypeStruct((4, 8, SUMS), f32),
+            jax.ShapeDtypeStruct((4, 8, SUMS), f32),
+            jax.ShapeDtypeStruct((8, SET), f32),
+        ],
+        scratch_shapes=[pltpu.VMEM((PLANE_ROWS, TILE), f32), pltpu.VMEM((8, TILE), f32)],
+        compiler_params=pltpu.CompilerParams(vmem_limit_bytes=24 << 20),
+        cost_estimate=pl.CostEstimate(
+            flops=2 * PLANE_ROWS * 1024 * E, bytes_accessed=3 << 20, transcendentals=1 << 17
+        ),
+    )(*args)
+
+
+def add_kernel(keep_ref, got_ref, *out_refs):
+    for k, out_ref in enumerate(out_refs):
+        out_ref[...] = keep_ref[k] + got_ref[k]
+
+
+def add_parts(keep, got):
+    return pl.pallas_call(
+        add_kernel,
+        in_specs=[VMEM] * 2,
+        out_specs=[VMEM] * 4,
+        out_shape=[jax.ShapeDtypeStruct((8, SUMS), f32)] * 4,
+        compiler_params=pltpu.CompilerParams(vmem_limit_bytes=16 << 20),
+        cost_estimate=pl.CostEstimate(flops=1 << 16, bytes_accessed=1 << 19, transcendentals=0),
+    )(keep, got)
+
+
 def grad_kernel(
-    arrived_ref, own_ref, target_ref, set0_ref, set1_ref, set2_ref, set3_ref,
-    video_hat_ref, video_norm_ref, text_hat_ref, text_norm_ref,
-    loss_ref, video_grad_ref, text_grad_ref, col_scr,
+    part0_ref, part1_ref, part2_ref, part3_ref, own_ref, last_ref, target_ref,
+    set0_ref, set1_ref, set2_ref, set3_ref, video_hat_ref, video_norm_ref,
+    text_hat_ref, text_norm_ref, loss_ref, video_grad_ref, text_grad_ref, col_scr,
 ):
     xh, c, xl, spot = position()
-    got = arrived_ref[0]
-    for k in range(1, 8):
-        got = got + arrived_ref[k]
+    got = (part0_ref[...] + part1_ref[...]) + (part2_ref[...] + part3_ref[...])
     cols = got[:, 2 * E : 2 * E + TILE]
     col_scr[...] = cols
     logs = jnp.sum(jnp.sum(jnp.log(cols), axis=0, keepdims=True), axis=1, keepdims=True)
@@ -355,7 +421,7 @@
     text_dir = SCALE * (got[:, 0:E] + got[:, E : 2 * E] / mine)
     text_grad_ref[...] = project(text_dir, text_hat_ref[...], text_norm_ref[...])
 
-    rows = own_ref[...]
+    rows = jnp.concatenate([own_ref[...], last_ref[...]], axis=1)
     rowsum = jnp.sum(rows, axis=1, keepdims=True)
     target = target_ref[pl.ds(pl.multiple_of((xl * 32 + spot) * 8, 8), 8), :]
     lane = iota((8, TILE), 1).astype(f32)
@@ -375,7 +441,7 @@
 def gradients(*args):
     return pl.pallas_call(
         grad_kernel,
-        in_specs=[VMEM] * 11,
+        in_specs=[VMEM] * 15,
         out_specs=[VMEM] * 3,
         out_shape=[
             jax.ShapeDtypeStruct((1, 1), f32),
@@ -398,6 +464,10 @@
     return lax.ppermute(x, "c", [(0, 1), (1, 0)])
 
 
+def turn(x, step):
+    return lax.ppermute(x, ("xh", "xl"), [(k, (k + step) % 4) for k in range(4)])
+
+
 def cross(x):
     return lax.ppermute(x, ("xh", "xl"), [(0, 3), (3, 0), (1, 2), (2, 1)])
 
@@ -414,9 +484,12 @@
     videos, crossed = lax.optimization_barrier((exchange(send, PLANE), crossed))
     videos = videos.reshape(PLANE_ROWS, E)
     sets = (texts, swap(texts), crossed, swap(crossed))
-    terms, own = all_logits(videos, target, *sets)
+    own, cols, halves, positive = first_logits(videos, target, *sets[0:3])
+    keep, send, last = second_logits(videos, target, *sets, cols, halves, positive)
+    parts = add_parts(keep, swap(send))
+    parts = [parts[0], turn(parts[1], 1), turn(parts[3], 3), turn(parts[2], 2)]
     loss, video_grad, text_grad = gradients(
-        exchange(terms, GROUP), own, target, *sets, video_hat, video_norm, text_hat, text_norm
+        *parts, own, last, target, *sets, video_hat, video_norm, text_hat, text_norm
     )
     return video_embed, video_grad, text_grad, loss.reshape(())
 

time: 105 us -> 101 us (0.962)
  blocking collectives: 65 us -> 53.2 us
  waiting for transfers between devices: 12.3 us -> 17 us
  starting transfers between devices: 14.6 us -> 17.8 us
    all_to_all x2 -> x1, blocking collectives: 65 us -> 53.2 us  [exchange(): return lax.all_to_all(x, axes, 0, 0, tiled=True)]
    ppermute x0 -> x3, waiting for transfers between devices: none -> 4.53 us  [turn(): lax.ppermute(x, ('xh', 'xl'), [(k, (k + step) % 4) for k in range(4)])]
    ppermute x0 -> x3, starting transfers between devices: none -> 2.8 us  [turn(): lax.ppermute(x, ('xh', 'xl'), [(k, (k + step) % 4) for k in range(4)])]
    ppermute x2 -> x3, starting transfers between devices: 5.86 us -> 6.32 us  [swap(): return lax.ppermute(x, 'c', [(0, 1), (1, 0)])]
    pallas_call x2 -> x4, Pallas kernels: 3.15 us -> 3.43 us  [the longest x1 1.29 us: gradients(): pl.pallas_call(grad_kernel, in_specs=[VMEM] * 15, out_specs=[VMEM] * 3, o...]
  transfers between devices with their start and end apart: 4 -> 8, of which waited for: 2 -> 5; matrix products, arithmetic and copies ran while one was open for 0% -> 0% of each run, Pallas kernels for 0% -> 1%
where the time goes in v4:
time: 101 us
  blocking collectives  53.2 us (53%)
  starting transfers between devices  17.8 us (18%)
  waiting for transfers between devices  17 us (17%)
  Pallas kernels  12 us (12%)
    all_to_all x1, blocking collectives, exchange(): return lax.all_to_all(x, axes, 0, 0, tiled=True)  53.2 us
    all_to_all x1, waiting for transfers between devices, exchange(): return lax.all_to_all(x, axes, 0, 0, tiled=True)  10.4 us
    all_to_all x1, starting transfers between devices, exchange(): return lax.all_to_all(x, axes, 0, 0, tiled=True)  7.28 us
    ppermute x3, starting transfers between devices, swap(): return lax.ppermute(x, 'c', [(0, 1), (1, 0)])  6.32 us
    pallas_call x1, Pallas kernels, clip_sums(): pl.pallas_call(clip_kernel, in_specs=[pl.BlockSpec(memory_space=pltpu.HBM...  6.02 us
    ppermute x3, waiting for transfers between devices, turn(): lax.ppermute(x, ('xh', 'xl'), [(k, (k + step) % 4) for k in range(4)])  4.53 us
    ppermute x3, starting transfers between devices, turn(): lax.ppermute(x, ('xh', 'xl'), [(k, (k + step) % 4) for k in range(4)])  2.8 us
    pallas_call x1, Pallas kernels, embed(): pl.pallas_call(embed_kernel, in_specs=[VMEM, VMEM], out_specs=[VMEM] * 6,...  2.55 us
  transfers between devices with their start and end apart: 8, of which 5 were waited for; matrix products, arithmetic and copies ran while one was open for 0% of the time, Pallas kernels for 1%

profile of v4, /device:TPU:1, one launch (start us, length us, event | category | flops | bytes accessed | tf_op | source)
XLA Modules:
  0.0 100.7 jit_solution(11355906609044890869)
XLA Ops:
  0.6 0.0 slice-start
  0.6 0.0 slice-start.1
  0.7 6.0 %shard_map.93 = (bf16[512,1664]{1,0:T(8,128)(2,1)S(1)}, f32[8,768]{1,0:T(8,128)S(1)}, f32[8,1]{1,0:T(8,128)S(1)}) custom-call(s32[1,64]{1,0:T(1,128)} %bitcast.14, bf16[1024,3200]{1,0:T(8,128)(2,1)} %bitcast.13, bf16[25,3200]{1,0:T(8,128)(2,1)} %pool_hbm.1, bf16[8,768]{1,0:T(8,128)(2,1)} %text_hbm.1, s32[1,8]{1,0:T(1,128)} %bitcast.15), custom_call_target="tpu_custom_call" | custom-call | flops 419430400 | bytes 8388608 | tf_op jit(solution)/shard_map/pallas_call | solution.py:167
  6.7 53.2 %all_to_all.10 = bf16[64,8,1664]{2,1,0:T(8,128)(2,1)S(1)} all-to-all(bf16[64,8,1664]{2,1,0:T(8,128)(2,1)S(1)} %bitcast.12), channel_id=1, replica_groups=mesh['xh'=2,'c'=2,'xl'=2,'z'=8,'y'=4] {'xl','z','y'}, dimensions={0} | all-to-all | bytes 3407872 | tf_op jit(solution)/shard_map/all_to_all | solution.py:460
  59.9 0.0 slice-done
  59.9 0.0 slice-done.1
  59.9 2.5 %shard_map.94 = (bf16[8,768]{1,0:T(8,128)(2,1)}, f32[8,768]{1,0:T(8,128)S(1)}, f32[8,1]{1,0:T(8,128)S(1)}, bf16[32,8,768]{2,1,0:T(8,128)(2,1)}, bf16[512,768]{1,0:T(8,128)(2,1)S(1)}, /*index=5*/f32[512,1]{1,0:T(8,128)S(1)}) custom-call(bf16[512,1664]{1,0:T(8,128)(2,1)S(1)} %bitcast.7, bf16[3200,768]{1,0:T(8,128)(2,1)S(1)} %bitcast.9), custom_call_target="tpu_custom_call" | custom-call | flops 117964800 | bytes 6291456 | tf_op jit(solution)/shard_map/pallas_call | solution.py:231
  62.5 1.4 %collective-permute-start = (bf16[512,768]{1,0:T(8,128)(2,1)S(1)}, bf16[512,768]{1,0:T(8,128)(2,1)S(1)}, u32[]{:S(2)}, u32[]{:S(2)}) collective-permute-start(bf16[512,768]{1,0:T(8,128)(2,1)S(1)} %get-tuple-element.32.set0_ref), channel_id=1, source_target_pairs={{0,160},{160,0},{32,128},{128,32},{1,161},{161,1},{33,129},{129,33... | collective-permute-start | bytes 2359304 | tf_op jit(solution)/shard_map/ppermute | solution.py:472
  63.9 7.3 %all-to-all-start.1 = ((bf16[32,8,768]{2,1,0:T(8,128)(2,1)}), bf16[32,8,768]{2,1,0:T(8,128)(2,1)S(1)}, u32[]{:S(2)}, u32[]{:S(2)}) async-start(bf16[32,8,768]{2,1,0:T(8,128)(2,1)} %get-tuple-element.31), calls=%async_computation.1 | async-start | bytes 786432 | tf_op jit(solution)/shard_map/all_to_all | solution.py:460
  71.2 2.2 %collective-permute-start.1 = (bf16[512,768]{1,0:T(8,128)(2,1)S(1)}, bf16[512,768]{1,0:T(8,128)(2,1)S(1)}, u32[]{:S(2)}, u32[]{:S(2)}) collective-permute-start(bf16[512,768]{1,0:T(8,128)(2,1)S(1)} %get-tuple-element.32.set0_ref), channel_id=1, source_target_pairs={{0,64},{64,0},{1,65},{65,1},{2,66},{66,2},{3,67},{67,3},{4,68},{68... | collective-permute-start | bytes 2359304 | tf_op jit(solution)/shard_map/ppermute | solution.py:464
  73.3 10.4 %all-to-all-done.1 = bf16[32,8,768]{2,1,0:T(8,128)(2,1)S(1)} async-done(((bf16[32,8,768]{2,1,0:T(8,128)(2,1)}), bf16[32,8,768]{2,1,0:T(8,128)(2,1)S(1)}, u32[]{:S(2)}, u32[]{:S(2)}) %all-to-all-start.1) | async-done | bytes 393248 | tf_op jit(solution)/shard_map/all_to_all | solution.py:460
  83.7 0.0 collective-permute-done.set2_ref
  83.7 3.7 %collective-permute-start.2 = (bf16[512,768]{1,0:T(8,128)(2,1)S(1)}, bf16[512,768]{1,0:T(8,128)(2,1)S(1)}, u32[]{:S(2)}, u32[]{:S(2)}) collective-permute-start(bf16[512,768]{1,0:T(8,128)(2,1)S(1)} %collective-permute-done.set2_ref), channel_id=1, source_target_pairs={{0,64},{64,0},{1,65},{65,1},{2,66},{66,2},{3,67},{67,3},{4,68},{68... | collective-permute-start | bytes 2359304 | tf_op jit(solution)/shard_map/ppermute | solution.py:464
  87.4 0.0 collective-permute-done.1.set1_ref
  87.4 1.0 shard_map.95
  88.4 0.9 collective-permute-done.2.set3_ref
  89.3 1.1 %shard_map.96 = (f32[4,8,1920]{2,1,0:T(8,128)S(1)}, f32[4,8,1920]{2,1,0:T(8,128)S(1)}, f32[8,512]{1,0:T(8,128)S(1)}) custom-call(bf16[256,768]{1,0:T(8,128)(2,1)S(1)} %bitcast.11, f32[512,1]{1,0:T(8,128)S(1)} %get-tuple-element.34.target_ref, bf16[512,768]{1,0:T(8,128)(2,1)S(1)} %get-tuple-element.32.set0_ref, ...), custom_call_target="tpu_custom_call" | custom-call | flops 402653184 | bytes 3145728 | tf_op jit(solution)/shard_map/pallas_call | solution.py:369
  90.5 0.5 collective-permute-start.3
  90.9 1.1 %collective-permute-done.3.got_ref = f32[4,8,1920]{2,1,0:T(8,128)S(1)} collective-permute-done((f32[4,8,1920]{2,1,0:T(8,128)S(1)}, f32[4,8,1920]{2,1,0:T(8,128)S(1)}, u32[]{:S(2)}, u32[]{:S(2)}) %collective-permute-start.3) | collective-permute-done | bytes 245792 | tf_op jit(solution)/shard_map/ppermute | solution.py:464
  92.1 0.9 collective-permute-start.4
  93.0 1.8 %collective-permute-start.5 = (f32[8,1920]{1,0:T(8,128)S(1)}, f32[8,1920]{1,0:T(8,128)S(1)}, u32[]{:S(2)}, u32[]{:S(2)}) collective-permute-start(f32[8,1920]{1,0:T(8,128)S(1)} %get-tuple-element.43), channel_id=1, source_target_pairs={{0,160},{32,0},{128,32},{160,128},{1,161},{33,1},{129,33},{161,129... | collective-permute-start | bytes 184328 | tf_op jit(solution)/shard_map/ppermute | solution.py:468
  94.9 0.0 collective-permute-start.6
  94.9 1.6 %collective-permute-done.4.part1_ref = f32[8,1920]{1,0:T(8,128)S(1)} collective-permute-done((f32[8,1920]{1,0:T(8,128)S(1)}, f32[8,1920]{1,0:T(8,128)S(1)}, u32[]{:S(2)}, u32[]{:S(2)}) %collective-permute-start.4) | collective-permute-done | bytes 61472 | tf_op jit(solution)/shard_map/ppermute | solution.py:468
  96.5 0.0 collective-permute-done.5.part2_ref
  96.5 3.0 %collective-permute-done.6.part3_ref = f32[8,1920]{1,0:T(8,128)S(1)} collective-permute-done((f32[8,1920]{1,0:T(8,128)S(1)}, f32[8,1920]{1,0:T(8,128)S(1)}, u32[]{:S(2)}, u32[]{:S(2)}) %collective-permute-start.6) | collective-permute-done | bytes 61472 | tf_op jit(solution)/shard_map/ppermute | solution.py:468
  99.4 1.3 %shard_map.98 = (f32[1,1]{1,0:T(1,128)}, f32[8,768]{1,0:T(8,128)}, f32[8,768]{1,0:T(8,128)}) custom-call(f32[8,1920]{1,0:T(8,128)S(1)} %get-tuple-element.41.part0_ref, f32[8,1920]{1,0:T(8,128)S(1)} %collective-permute-done.4.part1_ref, f32[8,1920]{1,0:T(8,128)S(1)} %collective-permute-done.5.part2_ref, f32[8,1920]{1,0:T(8,128)S(1)} %collective-permute-done.6.part3_ref, ...), custom_call_target="tpu_custom_call" | custom-call | flops 25165824 | bytes 5242880 | tf_op jit(solution)/shard_map/pallas_call | solution.py:442
  (2 shorter events, 0.0 us)
Async XLA Ops:
  0.6 59.3 %slice-start = ((s8[4915200]{0:T(1024)(128)(4,1)}), s8[4194304]{0:T(1024)(128)(4,1)S(1)}, s32[]{:S(2)}) async-start(s8[4915200]{0:T(1024)(128)(4,1)} %bitcast.8), calls=%async_computation.2 | async-start | bytes 8388608
  0.6 59.3 %slice-start.1 = ((s8[4915200]{0:T(1024)(128)(4,1)}), s8[720896]{0:T(1024)(128)(4,1)S(1)}, s32[]{:S(2)}) async-start(s8[4915200]{0:T(1024)(128)(4,1)} %bitcast.8), calls=%async_computation.3 | async-start | bytes 1441792
  62.5 21.3 %collective-permute-start = (bf16[512,768]{1,0:T(8,128)(2,1)S(1)}, bf16[512,768]{1,0:T(8,128)(2,1)S(1)}, u32[]{:S(2)}, u32[]{:S(2)}) collective-permute-start(bf16[512,768]{1,0:T(8,128)(2,1)S(1)} %get-tuple-element.32.set0_ref), channel_id=1, source_target_pairs={{0,160},{160,0},{32,128},{128,32},{1,161},{161,1},{33,129},{129,33... | collective-permute-start | bytes 2359304 | tf_op jit(solution)/shard_map/ppermute | solution.py:472
  63.9 19.8 %all-to-all-start.1 = ((bf16[32,8,768]{2,1,0:T(8,128)(2,1)}), bf16[32,8,768]{2,1,0:T(8,128)(2,1)S(1)}, u32[]{:S(2)}, u32[]{:S(2)}) async-start(bf16[32,8,768]{2,1,0:T(8,128)(2,1)} %get-tuple-element.31), calls=%async_computation.1 | async-start | bytes 786432 | tf_op jit(solution)/shard_map/all_to_all | solution.py:460
  71.2 16.2 %collective-permute-start.1 = (bf16[512,768]{1,0:T(8,128)(2,1)S(1)}, bf16[512,768]{1,0:T(8,128)(2,1)S(1)}, u32[]{:S(2)}, u32[]{:S(2)}) collective-permute-start(bf16[512,768]{1,0:T(8,128)(2,1)S(1)} %get-tuple-element.32.set0_ref), channel_id=1, source_target_pairs={{0,64},{64,0},{1,65},{65,1},{2,66},{66,2},{3,67},{67,3},{4,68},{68... | collective-permute-start | bytes 2359304 | tf_op jit(solution)/shard_map/ppermute | solution.py:464
  83.7 5.6 %collective-permute-start.2 = (bf16[512,768]{1,0:T(8,128)(2,1)S(1)}, bf16[512,768]{1,0:T(8,128)(2,1)S(1)}, u32[]{:S(2)}, u32[]{:S(2)}) collective-permute-start(bf16[512,768]{1,0:T(8,128)(2,1)S(1)} %collective-permute-done.set2_ref), channel_id=1, source_target_pairs={{0,64},{64,0},{1,65},{65,1},{2,66},{66,2},{3,67},{67,3},{4,68},{68... | collective-permute-start | bytes 2359304 | tf_op jit(solution)/shard_map/ppermute | solution.py:464
  90.5 1.6 %collective-permute-start.3 = (f32[4,8,1920]{2,1,0:T(8,128)S(1)}, f32[4,8,1920]{2,1,0:T(8,128)S(1)}, u32[]{:S(2)}, u32[]{:S(2)}) collective-permute-start(f32[4,8,1920]{2,1,0:T(8,128)S(1)} %get-tuple-element.40), channel_id=1, source_target_pairs={{0,64},{64,0},{1,65},{65,1},{2,66},{66,2},{3,67},{67,3},{4,68},{68... | collective-permute-start | bytes 737288 | tf_op jit(solution)/shard_map/ppermute | solution.py:464
  92.1 4.4 %collective-permute-start.4 = (f32[8,1920]{1,0:T(8,128)S(1)}, f32[8,1920]{1,0:T(8,128)S(1)}, u32[]{:S(2)}, u32[]{:S(2)}) collective-permute-start(f32[8,1920]{1,0:T(8,128)S(1)} %get-tuple-element.42), channel_id=1, source_target_pairs={{0,32},{32,128},{128,160},{160,0},{1,33},{33,129},{129,161},{161,1... | collective-permute-start | bytes 184328 | tf_op jit(solution)/shard_map/ppermute | solution.py:468
  93.0 3.4 %collective-permute-start.5 = (f32[8,1920]{1,0:T(8,128)S(1)}, f32[8,1920]{1,0:T(8,128)S(1)}, u32[]{:S(2)}, u32[]{:S(2)}) collective-permute-start(f32[8,1920]{1,0:T(8,128)S(1)} %get-tuple-element.43), channel_id=1, source_target_pairs={{0,160},{32,0},{128,32},{160,128},{1,161},{33,1},{129,33},{161,129... | collective-permute-start | bytes 184328 | tf_op jit(solution)/shard_map/ppermute | solution.py:468
  94.9 4.6 %collective-permute-start.6 = (f32[8,1920]{1,0:T(8,128)S(1)}, f32[8,1920]{1,0:T(8,128)S(1)}, u32[]{:S(2)}, u32[]{:S(2)}) collective-permute-start(f32[8,1920]{1,0:T(8,128)S(1)} %get-tuple-element.44), channel_id=1, source_target_pairs={{0,128},{32,160},{128,0},{160,32},{1,129},{33,161},{129,1},{161,33... | collective-permute-start | bytes 184328 | tf_op jit(solution)/shard_map/ppermute | solution.py:468

commit v5 on v4

--- a/solution.py
+++ b/solution.py
@@ -28,6 +28,7 @@
 SET = 512
 PLANE_ROWS = 256
 SUMS = 2 * E + TILE + 128
+PIECE = E // 2
 VMEM = pl.BlockSpec(memory_space=pltpu.VMEM)
 f32 = jnp.float32
 bf16 = jnp.bfloat16
@@ -83,8 +84,10 @@
     hat, norm = unit_rows(text_ref[...].astype(f32))
     hat_ref[...] = hat
     norm_ref[...] = norm
-    texts = jnp.broadcast_to(hat[None], (CLIPS, 8, E)).reshape(CLIPS * 8, E)
-    out_ref[:, SENT : SENT + E] = texts.astype(bf16)
+    for k in range(2):
+        texts = hat[None, :, k * PIECE : (k + 1) * PIECE]
+        texts = jnp.broadcast_to(texts, (CLIPS // 2, 8, PIECE)).reshape(CLIPS * 4, PIECE)
+        out_ref[k * CLIPS * 4 : (k + 1) * CLIPS * 4, SENT : SENT + PIECE] = texts.astype(bf16)
     early[0].wait()
     pool = pool_ref[...]
 
@@ -169,7 +172,7 @@
         in_specs=[pl.BlockSpec(memory_space=pltpu.HBM)] * 5,
         out_specs=[VMEM] * 3,
         out_shape=[
-            jax.ShapeDtypeStruct((CLIPS * 8, SENT + E), bf16),
+            jax.ShapeDtypeStruct((CLIPS * 8, SENT + PIECE), bf16),
             jax.ShapeDtypeStruct((8, E), f32),
             jax.ShapeDtypeStruct((8, 1), f32),
         ],
@@ -190,7 +193,7 @@
     arrived_ref, proj_ref, emb_ref, hat_ref, norm_ref, send_ref, text_ref, target_ref
 ):
     rows = CLIPS * 8
-    text_ref[...] = arrived_ref[:, SENT : SENT + E]
+    text_ref[...] = arrived_ref[:, SENT : SENT + PIECE]
     tails = arrived_ref[:, TAIL : TAIL + HD]
     pick = jnp.where(iota((8, HD), 1) - 64 == iota((8, HD), 0), 1.0, 0.0).astype(bf16)
     hot = dot(pick, tails, NT)
@@ -237,7 +240,7 @@
             jax.ShapeDtypeStruct((8, E), f32),
             jax.ShapeDtypeStruct((8, 1), f32),
             jax.ShapeDtypeStruct((32, 8, E), bf16),
-            jax.ShapeDtypeStruct((SET, E), bf16),
+            jax.ShapeDtypeStruct((SET, PIECE), bf16),
             jax.ShapeDtypeStruct((SET, 1), f32),
         ],
         compiler_params=pltpu.CompilerParams(vmem_limit_bytes=24 << 20),
@@ -252,24 +255,37 @@
     return xh, c, xl, z * 4 + y
 
 
-def rows_of(xh, c, k):
-    a, b = k // 2, k % 2
-    return (xh + a - 2 * a * xh) * 2 + (c + b - 2 * b * c)
-
-
-def score(videos, target, ref, row, own_ref, at, tile_scr, cols_ref, halves, positive, base):
+def other(a, flip):
+    return a + flip - 2 * flip * a
+
+
+def row_of(xh, c, k):
+    return other(xh, k // 2) * 2 + other(c, k % 2)
+
+
+def halves_of(ref, xl):
+    return (
+        ref[:, pl.ds(pl.multiple_of(xl * PIECE, 128), PIECE)],
+        ref[:, pl.ds(pl.multiple_of((1 - xl) * PIECE, 128), PIECE)],
+    )
+
+
+def score(videos, target, pieces, row, own_ref, at, tile_scr, cols_ref, sums, positive, base):
     lane = iota((1, TILE), 1).astype(f32)
     for t in range(2):
         tile = row * 2 + t
-        logits = SCALE * dot(videos, ref[t * TILE : (t + 1) * TILE, :], NT)
+        rows = slice(t * TILE, (t + 1) * TILE)
+        logits = SCALE * (
+            dot(videos[0], pieces[0][rows, :], NT) + dot(videos[1], pieces[1][rows, :], NT)
+        )
         ex = jnp.exp(logits)
         tile_scr[...] = ex
         cols_ref[pl.ds(tile, 1), :] = jnp.sum(ex, axis=0, keepdims=True)
-        halves += ex[:, 0:128] + ex[:, 128:TILE]
+        sums += ex[:, 0:128] + ex[:, 128:TILE]
         hit = target == (tile * TILE).astype(f32) + lane
         positive += jnp.sum(jnp.where(hit, logits, 0.0), axis=0, keepdims=True)
         own_ref[:, at + t * TILE : at + (t + 1) * TILE] = tile_scr[pl.ds(base, 8), :]
-    return halves, positive
+    return sums, positive
 
 
 def plane_rows(target_ref, xl):
@@ -277,68 +293,76 @@
 
 
 def first_kernel(
-    video_ref, target_ref, set0_ref, set1_ref, set2_ref,
-    own_ref, cols_ref, halves_ref, positive_ref, tile_scr,
+    video_ref, target_ref, set0_ref, set0b_ref, set2_ref, set2b_ref,
+    own_ref, cols_ref, sums_ref, positive_ref, tile_scr,
 ):
     xh, c, xl, spot = position()
     target = plane_rows(target_ref, xl)
-    videos = video_ref[...]
+    videos = halves_of(video_ref, xl)
     base = pl.multiple_of(spot * 8, 8)
     cols_ref[...] = jnp.zeros_like(cols_ref)
-    halves, positive = jnp.zeros((PLANE_ROWS, 128), f32), jnp.zeros((1, TILE), f32)
-    for k, ref in enumerate((set0_ref, set1_ref, set2_ref)):
-        halves, positive = score(
-            videos, target, ref, rows_of(xh, c, k), own_ref, k * SET, tile_scr, cols_ref,
-            halves, positive, base,
+    sums, positive = jnp.zeros((PLANE_ROWS, 128), f32), jnp.zeros((1, TILE), f32)
+    for n, pieces in enumerate(((set0_ref, set0b_ref), (set2_ref, set2b_ref))):
+        sums, positive = score(
+            videos, target, pieces, row_of(xh, c, 2 * n), own_ref, n * SET, tile_scr, cols_ref,
+            sums, positive, base,
         )
-    halves_ref[...] = halves
+    sums_ref[...] = sums
     positive_ref[...] = positive
 
 
 def second_kernel(
-    video_ref, target_ref, set0_ref, set1_ref, set2_ref, set3_ref, cols_ref, halves_ref, positive_ref,
+    video_ref, target_ref, set0_ref, set0b_ref, set2_ref, set2b_ref, set1_ref, set1b_ref, set3_ref,
+    set3b_ref, cols_ref, sums_ref, positive_ref,
     keep_ref, send_ref, own_ref, tile_scr, col_scr,
 ):
     xh, c, xl, spot = position()
     target = plane_rows(target_ref, xl)
-    videos = video_ref[...]
+    videos = halves_of(video_ref, xl)
     base = pl.multiple_of(spot * 8, 8)
-    sets = (set0_ref, set1_ref, set2_ref, set3_ref)
+    sets = (
+        (set0_ref, set0b_ref), (set1_ref, set1b_ref), (set2_ref, set2b_ref), (set3_ref, set3b_ref)
+    )
+    col_scr[...] = cols_ref[...]
+    sums, positive = sums_ref[...], positive_ref[...]
+    for n, k in enumerate((1, 3)):
+        sums, positive = score(
+            videos, target, sets[k], row_of(xh, c, k), own_ref, n * SET, tile_scr, col_scr,
+            sums, positive, base,
+        )
     odd = spot % 2 == 1
-    near, groups = [], []
-    for k, ref in enumerate(sets):
-        for half in range(2):
-            at = pl.multiple_of(half * PLANE_ROWS + spot // 2 * 16, 16)
-            pair = ref[pl.ds(at, 16), :].astype(f32)
-            near.append(jnp.where(odd, pair[8:16], pair[0:8]))
-            groups.append(rows_of(xh, c, k) * 2 + half)
-    near = jnp.concatenate(near, axis=0).astype(bf16)
-    near = jnp.exp(SCALE * dot(videos, near, NT))
-    col_scr[...] = cols_ref[...]
-    halves, positive = score(
-        videos, target, set3_ref, rows_of(xh, c, 3), own_ref, 0, tile_scr, col_scr,
-        halves_ref[...], positive_ref[...], base,
-    )
-    rowsum = jnp.sum(halves, axis=1, keepdims=True)
+    logits, groups = 0.0, []
+    for part in range(2):
+        near = []
+        for k in range(4):
+            for half in range(2):
+                at = pl.multiple_of(half * PLANE_ROWS + spot // 2 * 16, 16)
+                pair = sets[k][part][pl.ds(at, 16), :].astype(f32)
+                near.append(jnp.where(odd, pair[8:16], pair[0:8]))
+        near = jnp.concatenate(near, axis=0).astype(bf16)
+        logits += dot(videos[part], near, NT)
+    near = jnp.exp(SCALE * logits)
+    rowsum = jnp.sum(sums, axis=1, keepdims=True)
     total = jnp.sum(jnp.log(rowsum), axis=0, keepdims=True) - 2.0 * jnp.sum(
         positive, axis=1, keepdims=True
     )
     slot = iota((1, 64), 1)
-    group = sum(jnp.where(slot // 8 == n, g, 0) for n, g in enumerate(groups))
+    group = sum(
+        jnp.where(slot // 8 == n, row_of(xh, c, n // 2) * 2 + n % 2, 0) for n in range(8)
+    )
     text = ((group * 32 + spot) * 8 + slot % 8).astype(f32)
     first = near / rowsum - jnp.where(target == text, 2.0, 0.0)
     first_hi = first.astype(bf16).astype(f32)
     near_hi = near.astype(bf16).astype(f32)
     terms = jnp.concatenate([first_hi, first - first_hi, near_hi, near - near_hi], axis=1)
-    sums = dot(terms.astype(bf16), videos, TN)
+    sums = dot(terms.astype(bf16), video_ref[...], TN)
     first, second = sums[0:64] + sums[64:128], sums[128:192] + sums[192:256]
     cols = col_scr[...]
     total = jnp.broadcast_to(total, (8, 128))
     for k in range(4):
         for half in range(2):
             n = k * 2 + half
-            there = (xh + k // 2 - 2 * (k // 2) * xh) * 2 + half
-            step = (there - (xh * 2 + xl) + 4) % 4
+            step = k // 2 * 2 + other(xl, half)
             out_ref = send_ref if k % 2 else keep_ref
             out_ref[step, :, 0:E] = first[n * 8 : (n + 1) * 8]
             out_ref[step, :, E : 2 * E] = second[n * 8 : (n + 1) * 8]
@@ -346,13 +370,13 @@
             out_ref[step, :, 2 * E + TILE :] = total
 
 
-def first_logits(videos, target, *sets):
+def first_logits(*args):
     return pl.pallas_call(
         first_kernel,
-        in_specs=[VMEM] * 5,
+        in_specs=[VMEM] * 6,
         out_specs=[VMEM] * 4,
         out_shape=[
-            jax.ShapeDtypeStruct((8, 3 * SET), f32),
+            jax.ShapeDtypeStruct((8, 2 * SET), f32),
             jax.ShapeDtypeStruct((8, TILE), f32),
             jax.ShapeDtypeStruct((PLANE_ROWS, 128), f32),
             jax.ShapeDtypeStruct((1, TILE), f32),
@@ -360,25 +384,25 @@
         scratch_shapes=[pltpu.VMEM((PLANE_ROWS, TILE), f32)],
         compiler_params=pltpu.CompilerParams(vmem_limit_bytes=24 << 20),
         cost_estimate=pl.CostEstimate(
-            flops=2 * PLANE_ROWS * 1536 * E, bytes_accessed=3 << 20, transcendentals=3 << 17
+            flops=2 * PLANE_ROWS * 1024 * E, bytes_accessed=2 << 20, transcendentals=1 << 18
         ),
-    )(videos, target, *sets)
+    )(*args)
 
 
 def second_logits(*args):
     return pl.pallas_call(
         second_kernel,
-        in_specs=[VMEM] * 9,
+        in_specs=[VMEM] * 13,
         out_specs=[VMEM] * 3,
         out_shape=[
             jax.ShapeDtypeStruct((4, 8, SUMS), f32),
             jax.ShapeDtypeStruct((4, 8, SUMS), f32),
-            jax.ShapeDtypeStruct((8, SET), f32),
+            jax.ShapeDtypeStruct((8, 2 * SET), f32),
         ],
         scratch_shapes=[pltpu.VMEM((PLANE_ROWS, TILE), f32), pltpu.VMEM((8, TILE), f32)],
         compiler_params=pltpu.CompilerParams(vmem_limit_bytes=24 << 20),
         cost_estimate=pl.CostEstimate(
-            flops=2 * PLANE_ROWS * 1024 * E, bytes_accessed=3 << 20, transcendentals=1 << 17
+            flops=2 * PLANE_ROWS * 1536 * E, bytes_accessed=4 << 20, transcendentals=1 << 18
         ),
     )(*args)
 
@@ -401,8 +425,8 @@
 
 def grad_kernel(
     part0_ref, part1_ref, part2_ref, part3_ref, own_ref, last_ref, target_ref,
-    set0_ref, set1_ref, set2_ref, set3_ref, video_hat_ref, video_norm_ref,
-    text_hat_ref, text_norm_ref, loss_ref, video_grad_ref, text_grad_ref, col_scr,
+    set0_ref, set0b_ref, set2_ref, set2b_ref, set1_ref, set1b_ref, set3_ref, set3b_ref,
+    video_hat_ref, video_norm_ref, text_hat_ref, text_norm_ref, loss_ref, video_grad_ref, text_grad_ref, col_scr,
 ):
     xh, c, xl, spot = position()
     got = (part0_ref[...] + part1_ref[...]) + (part2_ref[...] + part3_ref[...])
@@ -425,23 +449,36 @@
     rowsum = jnp.sum(rows, axis=1, keepdims=True)
     target = target_ref[pl.ds(pl.multiple_of((xl * 32 + spot) * 8, 8), 8), :]
     lane = iota((8, TILE), 1).astype(f32)
-    direction = jnp.zeros((8, E), f32)
-    for k, ref in enumerate((set0_ref, set1_ref, set2_ref, set3_ref)):
-        row = rows_of(xh, c, k)
+    direction = [jnp.zeros((8, PIECE), f32)] * 2
+    sets = ((set0_ref, set0b_ref), (set2_ref, set2b_ref), (set1_ref, set1b_ref), (set3_ref, set3b_ref))
+    for n, k in enumerate((0, 2, 1, 3)):
+        row = row_of(xh, c, k)
         for t in range(2):
             tile = row * 2 + t
-            at = k * SET + t * TILE
+            at = n * SET + t * TILE
             ex = rows[:, at : at + TILE]
             hot = jnp.where(target == (tile * TILE).astype(f32) + lane, 2.0, 0.0)
             probe = ex / rowsum + ex / col_scr[pl.ds(tile, 1), :] - hot
-            direction += dot(probe.astype(bf16), ref[t * TILE : (t + 1) * TILE, :])
+            probe = probe.astype(bf16)
+            direction = [
+                total + dot(probe, ref[t * TILE : (t + 1) * TILE, :])
+                for total, ref in zip(direction, sets[n])
+            ]
+    low = xl == 0
+    direction = jnp.concatenate(
+        [
+            jnp.where(low, direction[0], direction[1]),
+            jnp.where(low, direction[1], direction[0]),
+        ],
+        axis=1,
+    )
     video_grad_ref[...] = project(SCALE * direction, video_hat_ref[...], video_norm_ref[...])
 
 
 def gradients(*args):
     return pl.pallas_call(
         grad_kernel,
-        in_specs=[VMEM] * 15,
+        in_specs=[VMEM] * 19,
         out_specs=[VMEM] * 3,
         out_shape=[
             jax.ShapeDtypeStruct((1, 1), f32),
@@ -464,32 +501,29 @@
     return lax.ppermute(x, "c", [(0, 1), (1, 0)])
 
 
-def turn(x, step):
-    return lax.ppermute(x, ("xh", "xl"), [(k, (k + step) % 4) for k in range(4)])
-
-
-def cross(x):
-    return lax.ppermute(x, ("xh", "xl"), [(0, 3), (3, 0), (1, 2), (2, 1)])
+def along(x, step):
+    return lax.ppermute(x, ("xh", "xl"), [(k, k ^ step) for k in range(4)])
 
 
 def body(clip_tokens, clip_video, pool_vectors, out_proj, text_embed, pair_text):
     outgoing, text_hat, text_norm = clip_sums(
         clip_tokens, clip_video, pool_vectors, text_embed, pair_text
     )
-    arrived = exchange(outgoing.reshape(CLIPS, 8, SENT + E), ROW)
+    arrived = exchange(outgoing.reshape(CLIPS, 8, SENT + PIECE), ROW)
     video_embed, video_hat, video_norm, send, texts, target = embed(
-        arrived.reshape(CLIPS * 8, SENT + E), out_proj
-    )
-    crossed = cross(texts)
-    videos, crossed = lax.optimization_barrier((exchange(send, PLANE), crossed))
+        arrived.reshape(CLIPS * 8, SENT + PIECE), out_proj
+    )
+    moved = [along(texts, step) for step in (2, 3, 1)]
+    videos, *moved = lax.optimization_barrier((exchange(send, PLANE), *moved))
     videos = videos.reshape(PLANE_ROWS, E)
-    sets = (texts, swap(texts), crossed, swap(crossed))
-    own, cols, halves, positive = first_logits(videos, target, *sets[0:3])
-    keep, send, last = second_logits(videos, target, *sets, cols, halves, positive)
+    mine = (texts, moved[2], moved[0], moved[1])
+    theirs = tuple(swap(x) for x in mine)
+    own, cols, sums, positive = first_logits(videos, target, *mine)
+    keep, send, last = second_logits(videos, target, *mine, *theirs, cols, sums, positive)
     parts = add_parts(keep, swap(send))
-    parts = [parts[0], turn(parts[1], 1), turn(parts[3], 3), turn(parts[2], 2)]
+    parts = [parts[0]] + [along(parts[step], step) for step in (2, 3, 1)]
     loss, video_grad, text_grad = gradients(
-        *parts, own, last, target, *sets, video_hat, video_norm, text_hat, text_norm
+        *parts, own, last, target, *mine, *theirs, video_hat, video_norm, text_hat, text_norm
     )
     return video_embed, video_grad, text_grad, loss.reshape(())
 

time: 101 us -> 96.4 us (0.954)
  blocking collectives: 53.2 us -> 45.6 us
  starting transfers between devices: 17.8 us -> 19.8 us
    ppermute x4 -> x6, waiting for transfers between devices: 4.53 us -> 15.7 us  [along(): return lax.ppermute(x, ('xh', 'xl'), [(k, k ^ step) for k in range(4)])]
    all_to_all x1, waiting for transfers between devices: 10.4 us -> 0.01 us  [exchange(): return lax.all_to_all(x, axes, 0, 0, tiled=True)]
    all_to_all x1, blocking collectives: 53.2 us -> 45.6 us  [exchange(): return lax.all_to_all(x, axes, 0, 0, tiled=True)]
    ppermute x4 -> x6, starting transfers between devices: 4.24 us -> 6.6 us  [along(): return lax.ppermute(x, ('xh', 'xl'), [(k, k ^ step) for k in range(4)])]
    ppermute x3 -> x5, starting transfers between devices: 6.32 us -> 6.72 us  [swap(): return lax.ppermute(x, 'c', [(0, 1), (1, 0)])]
    ppermute x3 -> x5, waiting for transfers between devices: 2.08 us -> 2.22 us  [swap(): return lax.ppermute(x, 'c', [(0, 1), (1, 0)])]
  transfers between devices with their start and end apart: 8 -> 12, of which waited for: 5 -> 9; matrix products, arithmetic and copies ran while one was open for 0% -> 0% of each run, Pallas kernels for 1% -> 1%
where the time goes in v5:
time: 96.4 us; the launch traced here: 96.1 us
  blocking collectives  45.6 us (47%)
  starting transfers between devices  19.8 us (21%)
  waiting for transfers between devices  17.9 us (19%)
  Pallas kernels  12.1 us (13%)
    all_to_all x1, blocking collectives, exchange(): return lax.all_to_all(x, axes, 0, 0, tiled=True)  45.6 us
    ppermute x6, waiting for transfers between devices, along(): return lax.ppermute(x, ('xh', 'xl'), [(k, k ^ step) for k in range(4)])  15.7 us
    ppermute x5, starting transfers between devices, swap(): return lax.ppermute(x, 'c', [(0, 1), (1, 0)])  6.72 us
    ppermute x6, starting transfers between devices, along(): return lax.ppermute(x, ('xh', 'xl'), [(k, k ^ step) for k in range(4)])  6.6 us
    all_to_all x1, starting transfers between devices, exchange(): return lax.all_to_all(x, axes, 0, 0, tiled=True)  6.51 us
    pallas_call x1, Pallas kernels, clip_sums(): pl.pallas_call(clip_kernel, in_specs=[pl.BlockSpec(memory_space=pltpu.HBM...  6.02 us
    pallas_call x1, Pallas kernels, embed(): pl.pallas_call(embed_kernel, in_specs=[VMEM, VMEM], out_specs=[VMEM] * 6,...  2.53 us
    ppermute x5, waiting for transfers between devices, swap(): return lax.ppermute(x, 'c', [(0, 1), (1, 0)])  2.22 us
  transfers between devices with their start and end apart: 12, of which 9 were waited for; matrix products, arithmetic and copies ran while one was open for 0% of the time, Pallas kernels for 1%

profile of v5, /device:TPU:1, one launch (start us, length us, event | category | flops | bytes accessed | tf_op | source)
XLA Modules:
  0.0 96.1 jit_solution(4373660364156376505)
XLA Ops:
  0.6 0.0 slice-start
  0.6 0.0 slice-start.1
  0.7 6.0 %shard_map.93 = (bf16[512,1280]{1,0:T(8,128)(2,1)S(1)}, f32[8,768]{1,0:T(8,128)S(1)}, f32[8,1]{1,0:T(8,128)S(1)}) custom-call(s32[1,64]{1,0:T(1,128)} %bitcast.14, bf16[1024,3200]{1,0:T(8,128)(2,1)} %bitcast.13, bf16[25,3200]{1,0:T(8,128)(2,1)} %pool_hbm.1, bf16[8,768]{1,0:T(8,128)(2,1)} %text_hbm.1, s32[1,8]{1,0:T(1,128)} %bitcast.15), custom_call_target="tpu_custom_call" | custom-call | flops 419430400 | bytes 8388608 | tf_op jit(solution)/shard_map/pallas_call | solution.py:170
  6.7 45.6 %all_to_all.10 = bf16[64,8,1280]{2,1,0:T(8,128)(2,1)S(1)} all-to-all(bf16[64,8,1280]{2,1,0:T(8,128)(2,1)S(1)} %bitcast.12), channel_id=1, replica_groups=mesh['xh'=2,'c'=2,'xl'=2,'z'=8,'y'=4] {'xl','z','y'}, dimensions={0} | all-to-all | bytes 2621440 | tf_op jit(solution)/shard_map/all_to_all | solution.py:497
  52.3 2.5 %shard_map.94 = (bf16[8,768]{1,0:T(8,128)(2,1)}, f32[8,768]{1,0:T(8,128)S(1)}, f32[8,1]{1,0:T(8,128)S(1)}, bf16[32,8,768]{2,1,0:T(8,128)(2,1)}, bf16[512,384]{1,0:T(8,128)(2,1)S(1)}, /*index=5*/f32[512,1]{1,0:T(8,128)S(1)}) custom-call(bf16[512,1280]{1,0:T(8,128)(2,1)S(1)} %bitcast.7, bf16[3200,768]{1,0:T(8,128)(2,1)S(1)} %bitcast.9), custom_call_target="tpu_custom_call" | custom-call | flops 117964800 | bytes 6291456 | tf_op jit(solution)/shard_map/pallas_call | solution.py:234
  54.8 6.5 %all-to-all-start.1 = ((bf16[32,8,768]{2,1,0:T(8,128)(2,1)}), bf16[32,8,768]{2,1,0:T(8,128)(2,1)S(1)}, u32[]{:S(2)}, u32[]{:S(2)}) async-start(bf16[32,8,768]{2,1,0:T(8,128)(2,1)} %get-tuple-element.33), calls=%async_computation.1 | async-start | bytes 786432 | tf_op jit(solution)/shard_map/all_to_all | solution.py:497
  61.3 0.2 collective-permute-start.2
  61.6 2.6 %collective-permute-start.1 = (bf16[512,384]{1,0:T(8,128)(2,1)S(1)}, bf16[512,384]{1,0:T(8,128)(2,1)S(1)}, u32[]{:S(2)}, u32[]{:S(2)}) collective-permute-start(bf16[512,384]{1,0:T(8,128)(2,1)S(1)} %get-tuple-element.34.set0_ref), channel_id=1, source_target_pairs={{0,160},{32,128},{128,32},{160,0},{1,161},{33,129},{129,33},{161,1... | collective-permute-start | bytes 1179656 | tf_op jit(solution)/shard_map/ppermute | solution.py:505
  64.2 0.5 collective-permute-start
  64.7 2.8 %collective-permute-start.3 = (bf16[512,384]{1,0:T(8,128)(2,1)S(1)}, bf16[512,384]{1,0:T(8,128)(2,1)S(1)}, u32[]{:S(2)}, u32[]{:S(2)}) collective-permute-start(bf16[512,384]{1,0:T(8,128)(2,1)S(1)} %get-tuple-element.34.set0_ref), channel_id=1, source_target_pairs={{0,64},{64,0},{1,65},{65,1},{2,66},{66,2},{3,67},{67,3},{4,68},{68... | collective-permute-start | bytes 1179656 | tf_op jit(solution)/shard_map/ppermute | solution.py:501
  67.5 2.6 %collective-permute-done.2.set0b_ref = bf16[512,384]{1,0:T(8,128)(2,1)S(1)} collective-permute-done((bf16[512,384]{1,0:T(8,128)(2,1)S(1)}, bf16[512,384]{1,0:T(8,128)(2,1)S(1)}, u32[]{:S(2)}, u32[]{:S(2)}) %collective-permute-start.2) | collective-permute-done | bytes 393248 | tf_op jit(solution)/shard_map/ppermute | solution.py:505
  70.1 1.1 %collective-permute-done.1.set2b_ref = bf16[512,384]{1,0:T(8,128)(2,1)S(1)} collective-permute-done((bf16[512,384]{1,0:T(8,128)(2,1)S(1)}, bf16[512,384]{1,0:T(8,128)(2,1)S(1)}, u32[]{:S(2)}, u32[]{:S(2)}) %collective-permute-start.1) | collective-permute-done | bytes 393248 | tf_op jit(solution)/shard_map/ppermute | solution.py:505
  71.2 8.5 %collective-permute-done.set2_ref = bf16[512,384]{1,0:T(8,128)(2,1)S(1)} collective-permute-done((bf16[512,384]{1,0:T(8,128)(2,1)S(1)}, bf16[512,384]{1,0:T(8,128)(2,1)S(1)}, u32[]{:S(2)}, u32[]{:S(2)}) %collective-permute-start) | collective-permute-done | bytes 393248 | tf_op jit(solution)/shard_map/ppermute | solution.py:505
  79.8 0.0 all-to-all-done.1
  79.8 3.0 %collective-permute-start.4 = (bf16[512,384]{1,0:T(8,128)(2,1)S(1)}, bf16[512,384]{1,0:T(8,128)(2,1)S(1)}, u32[]{:S(2)}, u32[]{:S(2)}) collective-permute-start(bf16[512,384]{1,0:T(8,128)(2,1)S(1)} %collective-permute-done.2.set0b_ref), channel_id=1, source_target_pairs={{0,64},{64,0},{1,65},{65,1},{2,66},{66,2},{3,67},{67,3},{4,68},{68... | collective-permute-start | bytes 1179656 | tf_op jit(solution)/shard_map/ppermute | solution.py:501
  82.7 0.1 collective-permute-start.5
  82.8 0.4 collective-permute-start.6
  83.3 0.9 shard_map.95
  84.1 0.0 collective-permute-done.3.set1_ref
  84.1 0.0 collective-permute-done.4.set1b_ref
  84.1 0.5 collective-permute-done.5.set3_ref
  84.7 0.6 collective-permute-done.6.set3b_ref
  85.2 1.3 %shard_map.96 = (f32[4,8,1920]{2,1,0:T(8,128)S(1)}, f32[4,8,1920]{2,1,0:T(8,128)S(1)}, f32[8,1024]{1,0:T(8,128)S(1)}) custom-call(bf16[256,768]{1,0:T(8,128)(2,1)S(1)} %bitcast.11, f32[512,1]{1,0:T(8,128)S(1)} %get-tuple-element.36.target_ref, bf16[512,384]{1,0:T(8,128)(2,1)S(1)} %get-tuple-element.34.set0_ref, ...), custom_call_target="tpu_custom_call" | custom-call | flops 603979776 | bytes 4194304 | tf_op jit(solution)/shard_map/pallas_call | solution.py:393
  86.5 0.5 collective-permute-start.7
  87.0 1.1 %collective-permute-done.7.got_ref = f32[4,8,1920]{2,1,0:T(8,128)S(1)} collective-permute-done((f32[4,8,1920]{2,1,0:T(8,128)S(1)}, f32[4,8,1920]{2,1,0:T(8,128)S(1)}, u32[]{:S(2)}, u32[]{:S(2)}) %collective-permute-start.7) | collective-permute-done | bytes 245792 | tf_op jit(solution)/shard_map/ppermute | solution.py:501
  88.2 1.3 %collective-permute-start.8 = (f32[8,1920]{1,0:T(8,128)S(1)}, f32[8,1920]{1,0:T(8,128)S(1)}, u32[]{:S(2)}, u32[]{:S(2)}) collective-permute-start(f32[8,1920]{1,0:T(8,128)S(1)} %get-tuple-element.46), channel_id=1, source_target_pairs={{0,128},{32,160},{128,0},{160,32},{1,129},{33,161},{129,1},{161,33... | collective-permute-start | bytes 184328 | tf_op jit(solution)/shard_map/ppermute | solution.py:505
  89.5 1.6 %collective-permute-start.9 = (f32[8,1920]{1,0:T(8,128)S(1)}, f32[8,1920]{1,0:T(8,128)S(1)}, u32[]{:S(2)}, u32[]{:S(2)}) collective-permute-start(f32[8,1920]{1,0:T(8,128)S(1)} %get-tuple-element.47), channel_id=1, source_target_pairs={{0,160},{32,128},{128,32},{160,0},{1,161},{33,129},{129,33},{161,1... | collective-permute-start | bytes 184328 | tf_op jit(solution)/shard_map/ppermute | solution.py:505
  91.1 0.3 collective-permute-start.10
  91.4 1.4 %collective-permute-done.8.part1_ref = f32[8,1920]{1,0:T(8,128)S(1)} collective-permute-done((f32[8,1920]{1,0:T(8,128)S(1)}, f32[8,1920]{1,0:T(8,128)S(1)}, u32[]{:S(2)}, u32[]{:S(2)}) %collective-permute-start.8) | collective-permute-done | bytes 61472 | tf_op jit(solution)/shard_map/ppermute | solution.py:505
  92.8 1.9 %collective-permute-done.9.part2_ref = f32[8,1920]{1,0:T(8,128)S(1)} collective-permute-done((f32[8,1920]{1,0:T(8,128)S(1)}, f32[8,1920]{1,0:T(8,128)S(1)}, u32[]{:S(2)}, u32[]{:S(2)}) %collective-permute-start.9) | collective-permute-done | bytes 61472 | tf_op jit(solution)/shard_map/ppermute | solution.py:505
  94.7 0.1 collective-permute-done.10.part3_ref
  94.8 1.3 %shard_map.98 = (f32[1,1]{1,0:T(1,128)}, f32[8,768]{1,0:T(8,128)}, f32[8,768]{1,0:T(8,128)}) custom-call(f32[8,1920]{1,0:T(8,128)S(1)} %get-tuple-element.45.part0_ref, f32[8,1920]{1,0:T(8,128)S(1)} %collective-permute-done.8.part1_ref, f32[8,1920]{1,0:T(8,128)S(1)} %collective-permute-done.9.part2_ref, f32[8,1920]{1,0:T(8,128)S(1)} %collective-permute-done.10.part3_ref, ...), custom_call_target="tpu_custom_call" | custom-call | flops 25165824 | bytes 5242880 | tf_op jit(solution)/shard_map/pallas_call | solution.py:479
  (4 shorter events, 0.0 us)
Async XLA Ops:
  0.6 51.7 %slice-start = ((s8[4915200]{0:T(1024)(128)(4,1)}), s8[4194304]{0:T(1024)(128)(4,1)S(1)}, s32[]{:S(2)}) async-start(s8[4915200]{0:T(1024)(128)(4,1)} %bitcast.8), calls=%async_computation.2 | async-start | bytes 8388608
  0.6 51.6 %slice-start.1 = ((s8[4915200]{0:T(1024)(128)(4,1)}), s8[720896]{0:T(1024)(128)(4,1)S(1)}, s32[]{:S(2)}) async-start(s8[4915200]{0:T(1024)(128)(4,1)} %bitcast.8), calls=%async_computation.3 | async-start | bytes 1441792
  54.8 24.9 %all-to-all-start.1 = ((bf16[32,8,768]{2,1,0:T(8,128)(2,1)}), bf16[32,8,768]{2,1,0:T(8,128)(2,1)S(1)}, u32[]{:S(2)}, u32[]{:S(2)}) async-start(bf16[32,8,768]{2,1,0:T(8,128)(2,1)} %get-tuple-element.33), calls=%async_computation.1 | async-start | bytes 786432 | tf_op jit(solution)/shard_map/all_to_all | solution.py:497
  61.3 8.8 %collective-permute-start.2 = (bf16[512,384]{1,0:T(8,128)(2,1)S(1)}, bf16[512,384]{1,0:T(8,128)(2,1)S(1)}, u32[]{:S(2)}, u32[]{:S(2)}) collective-permute-start(bf16[512,384]{1,0:T(8,128)(2,1)S(1)} %get-tuple-element.34.set0_ref), channel_id=1, source_target_pairs={{0,32},{32,0},{128,160},{160,128},{1,33},{33,1},{129,161},{161,129... | collective-permute-start | bytes 1179656 | tf_op jit(solution)/shard_map/ppermute | solution.py:505
  61.6 9.7 %collective-permute-start.1 = (bf16[512,384]{1,0:T(8,128)(2,1)S(1)}, bf16[512,384]{1,0:T(8,128)(2,1)S(1)}, u32[]{:S(2)}, u32[]{:S(2)}) collective-permute-start(bf16[512,384]{1,0:T(8,128)(2,1)S(1)} %get-tuple-element.34.set0_ref), channel_id=1, source_target_pairs={{0,160},{32,128},{128,32},{160,0},{1,161},{33,129},{129,33},{161,1... | collective-permute-start | bytes 1179656 | tf_op jit(solution)/shard_map/ppermute | solution.py:505
  64.2 15.6 %collective-permute-start = (bf16[512,384]{1,0:T(8,128)(2,1)S(1)}, bf16[512,384]{1,0:T(8,128)(2,1)S(1)}, u32[]{:S(2)}, u32[]{:S(2)}) collective-permute-start(bf16[512,384]{1,0:T(8,128)(2,1)S(1)} %get-tuple-element.34.set0_ref), channel_id=1, source_target_pairs={{0,128},{32,160},{128,0},{160,32},{1,129},{33,161},{129,1},{161,33... | collective-permute-start | bytes 1179656 | tf_op jit(solution)/shard_map/ppermute | solution.py:505
  64.7 19.4 %collective-permute-start.3 = (bf16[512,384]{1,0:T(8,128)(2,1)S(1)}, bf16[512,384]{1,0:T(8,128)(2,1)S(1)}, u32[]{:S(2)}, u32[]{:S(2)}) collective-permute-start(bf16[512,384]{1,0:T(8,128)(2,1)S(1)} %get-tuple-element.34.set0_ref), channel_id=1, source_target_pairs={{0,64},{64,0},{1,65},{65,1},{2,66},{66,2},{3,67},{67,3},{4,68},{68... | collective-permute-start | bytes 1179656 | tf_op jit(solution)/shard_map/ppermute | solution.py:501
  79.8 4.4 %collective-permute-start.4 = (bf16[512,384]{1,0:T(8,128)(2,1)S(1)}, bf16[512,384]{1,0:T(8,128)(2,1)S(1)}, u32[]{:S(2)}, u32[]{:S(2)}) collective-permute-start(bf16[512,384]{1,0:T(8,128)(2,1)S(1)} %collective-permute-done.2.set0b_ref), channel_id=1, source_target_pairs={{0,64},{64,0},{1,65},{65,1},{2,66},{66,2},{3,67},{67,3},{4,68},{68... | collective-permute-start | bytes 1179656 | tf_op jit(solution)/shard_map/ppermute | solution.py:501
  82.7 1.9 %collective-permute-start.5 = (bf16[512,384]{1,0:T(8,128)(2,1)S(1)}, bf16[512,384]{1,0:T(8,128)(2,1)S(1)}, u32[]{:S(2)}, u32[]{:S(2)}) collective-permute-start(bf16[512,384]{1,0:T(8,128)(2,1)S(1)} %collective-permute-done.set2_ref), channel_id=1, source_target_pairs={{0,64},{64,0},{1,65},{65,1},{2,66},{66,2},{3,67},{67,3},{4,68},{68... | collective-permute-start | bytes 1179656 | tf_op jit(solution)/shard_map/ppermute | solution.py:501
  82.8 2.4 %collective-permute-start.6 = (bf16[512,384]{1,0:T(8,128)(2,1)S(1)}, bf16[512,384]{1,0:T(8,128)(2,1)S(1)}, u32[]{:S(2)}, u32[]{:S(2)}) collective-permute-start(bf16[512,384]{1,0:T(8,128)(2,1)S(1)} %collective-permute-done.1.set2b_ref), channel_id=1, source_target_pairs={{0,64},{64,0},{1,65},{65,1},{2,66},{66,2},{3,67},{67,3},{4,68},{68... | collective-permute-start | bytes 1179656 | tf_op jit(solution)/shard_map/ppermute | solution.py:501
  86.5 1.6 %collective-permute-start.7 = (f32[4,8,1920]{2,1,0:T(8,128)S(1)}, f32[4,8,1920]{2,1,0:T(8,128)S(1)}, u32[]{:S(2)}, u32[]{:S(2)}) collective-permute-start(f32[4,8,1920]{2,1,0:T(8,128)S(1)} %get-tuple-element.44), channel_id=1, source_target_pairs={{0,64},{64,0},{1,65},{65,1},{2,66},{66,2},{3,67},{67,3},{4,68},{68... | collective-permute-start | bytes 737288 | tf_op jit(solution)/shard_map/ppermute | solution.py:501
  88.2 4.7 %collective-permute-start.8 = (f32[8,1920]{1,0:T(8,128)S(1)}, f32[8,1920]{1,0:T(8,128)S(1)}, u32[]{:S(2)}, u32[]{:S(2)}) collective-permute-start(f32[8,1920]{1,0:T(8,128)S(1)} %get-tuple-element.46), channel_id=1, source_target_pairs={{0,128},{32,160},{128,0},{160,32},{1,129},{33,161},{129,1},{161,33... | collective-permute-start | bytes 184328 | tf_op jit(solution)/shard_map/ppermute | solution.py:505
  89.5 5.2 %collective-permute-start.9 = (f32[8,1920]{1,0:T(8,128)S(1)}, f32[8,1920]{1,0:T(8,128)S(1)}, u32[]{:S(2)}, u32[]{:S(2)}) collective-permute-start(f32[8,1920]{1,0:T(8,128)S(1)} %get-tuple-element.47), channel_id=1, source_target_pairs={{0,160},{32,128},{128,32},{160,0},{1,161},{33,129},{129,33},{161,1... | collective-permute-start | bytes 184328 | tf_op jit(solution)/shard_map/ppermute | solution.py:505
  91.1 3.7 %collective-permute-start.10 = (f32[8,1920]{1,0:T(8,128)S(1)}, f32[8,1920]{1,0:T(8,128)S(1)}, u32[]{:S(2)}, u32[]{:S(2)}) collective-permute-start(f32[8,1920]{1,0:T(8,128)S(1)} %get-tuple-element.48), channel_id=1, source_target_pairs={{0,32},{32,0},{128,160},{160,128},{1,33},{33,1},{129,161},{161,129... | collective-permute-start | bytes 184328 | tf_op jit(solution)/shard_map/ppermute | solution.py:505

commit v6 on v5

--- a/solution.py
+++ b/solution.py
@@ -190,10 +190,9 @@
 
 
 def embed_kernel(
-    arrived_ref, proj_ref, emb_ref, hat_ref, norm_ref, send_ref, text_ref, target_ref
+    arrived_ref, proj_ref, emb_ref, hat_ref, norm_ref, send_ref, target_ref
 ):
     rows = CLIPS * 8
-    text_ref[...] = arrived_ref[:, SENT : SENT + PIECE]
     tails = arrived_ref[:, TAIL : TAIL + HD]
     pick = jnp.where(iota((8, HD), 1) - 64 == iota((8, HD), 0), 1.0, 0.0).astype(bf16)
     hot = dot(pick, tails, NT)
@@ -234,13 +233,12 @@
     return pl.pallas_call(
         embed_kernel,
         in_specs=[VMEM, VMEM],
-        out_specs=[VMEM] * 6,
+        out_specs=[VMEM] * 5,
         out_shape=[
             jax.ShapeDtypeStruct((8, E), bf16),
             jax.ShapeDtypeStruct((8, E), f32),
             jax.ShapeDtypeStruct((8, 1), f32),
             jax.ShapeDtypeStruct((32, 8, E), bf16),
-            jax.ShapeDtypeStruct((SET, PIECE), bf16),
             jax.ShapeDtypeStruct((SET, 1), f32),
         ],
         compiler_params=pltpu.CompilerParams(vmem_limit_bytes=24 << 20),
@@ -248,6 +246,21 @@
             flops=2 * 24 * D * E, bytes_accessed=6 << 20, transcendentals=0
         ),
     )(arrived, out_proj)
+
+
+def text_kernel(arrived_ref, text_ref):
+    text_ref[...] = arrived_ref[:, SENT : SENT + PIECE]
+
+
+def text_piece(arrived):
+    return pl.pallas_call(
+        text_kernel,
+        in_specs=[VMEM],
+        out_specs=VMEM,
+        out_shape=jax.ShapeDtypeStruct((SET, PIECE), bf16),
+        compiler_params=pltpu.CompilerParams(vmem_limit_bytes=16 << 20),
+        cost_estimate=pl.CostEstimate(flops=0, bytes_accessed=1 << 20, transcendentals=0),
+    )(arrived)
 
 
 def position():
@@ -510,10 +523,10 @@
         clip_tokens, clip_video, pool_vectors, text_embed, pair_text
     )
     arrived = exchange(outgoing.reshape(CLIPS, 8, SENT + PIECE), ROW)
-    video_embed, video_hat, video_norm, send, texts, target = embed(
-        arrived.reshape(CLIPS * 8, SENT + PIECE), out_proj
-    )
+    arrived = arrived.reshape(CLIPS * 8, SENT + PIECE)
+    texts = text_piece(arrived)
     moved = [along(texts, step) for step in (2, 3, 1)]
+    video_embed, video_hat, video_norm, send, target = embed(arrived, out_proj)
     videos, *moved = lax.optimization_barrier((exchange(send, PLANE), *moved))
     videos = videos.reshape(PLANE_ROWS, E)
     mine = (texts, moved[2], moved[0], moved[1])

time: 96.4 us -> 96.3 us (level)
    pallas_call x1 -> x2, Pallas kernels: 2.53 us -> 2.53 us  [the longest x1 2.5 us: embed(): pl.pallas_call(embed_kernel, in_specs=[VMEM, VMEM], out_specs=[VMEM] * 5,...]
where the time goes in v6:
time: 96.3 us; the launch traced here: 96.1 us
  blocking collectives  45.6 us (47%)
  starting transfers between devices  19.8 us (21%)
  waiting for transfers between devices  17.9 us (19%)
  Pallas kernels  12.1 us (13%)
    all_to_all x1, blocking collectives, exchange(): return lax.all_to_all(x, axes, 0, 0, tiled=True)  45.6 us
    ppermute x6, waiting for transfers between devices, along(): return lax.ppermute(x, ('xh', 'xl'), [(k, k ^ step) for k in range(4)])  15.7 us
    ppermute x5, starting transfers between devices, swap(): return lax.ppermute(x, 'c', [(0, 1), (1, 0)])  6.72 us
    ppermute x6, starting transfers between devices, along(): return lax.ppermute(x, ('xh', 'xl'), [(k, k ^ step) for k in range(4)])  6.6 us
    all_to_all x1, starting transfers between devices, exchange(): return lax.all_to_all(x, axes, 0, 0, tiled=True)  6.51 us
    pallas_call x1, Pallas kernels, clip_sums(): pl.pallas_call(clip_kernel, in_specs=[pl.BlockSpec(memory_space=pltpu.HBM...  6.02 us
    pallas_call x1, Pallas kernels, embed(): pl.pallas_call(embed_kernel, in_specs=[VMEM, VMEM], out_specs=[VMEM] * 5,...  2.5 us
    ppermute x5, waiting for transfers between devices, swap(): return lax.ppermute(x, 'c', [(0, 1), (1, 0)])  2.23 us
  transfers between devices with their start and end apart: 12, of which 9 were waited for; matrix products, arithmetic and copies ran while one was open for 0% of the time, Pallas kernels for 1%

profile of v6, /device:TPU:1, one launch (start us, length us, event | category | flops | bytes accessed | tf_op | source)
XLA Modules:
  0.0 96.1 jit_solution(3589434817553665033)
XLA Ops:
  0.6 0.0 slice-start
  0.6 0.0 slice-start.1
  0.7 6.0 %shard_map.93 = (bf16[512,1280]{1,0:T(8,128)(2,1)S(1)}, f32[8,768]{1,0:T(8,128)S(1)}, f32[8,1]{1,0:T(8,128)S(1)}) custom-call(s32[1,64]{1,0:T(1,128)} %bitcast.15, bf16[1024,3200]{1,0:T(8,128)(2,1)} %bitcast.14, bf16[25,3200]{1,0:T(8,128)(2,1)} %pool_hbm.1, bf16[8,768]{1,0:T(8,128)(2,1)} %text_hbm.1, s32[1,8]{1,0:T(1,128)} %bitcast.16), custom_call_target="tpu_custom_call" | custom-call | flops 419430400 | bytes 8388608 | tf_op jit(solution)/shard_map/pallas_call | solution.py:170
  6.7 45.6 %all_to_all.10 = bf16[64,8,1280]{2,1,0:T(8,128)(2,1)S(1)} all-to-all(bf16[64,8,1280]{2,1,0:T(8,128)(2,1)S(1)} %bitcast.13), channel_id=1, replica_groups=mesh['xh'=2,'c'=2,'xl'=2,'z'=8,'y'=4] {'xl','z','y'}, dimensions={0} | all-to-all | bytes 2621440 | tf_op jit(solution)/shard_map/all_to_all | solution.py:510
  52.3 2.5 %shard_map.94 = (bf16[8,768]{1,0:T(8,128)(2,1)}, f32[8,768]{1,0:T(8,128)S(1)}, f32[8,1]{1,0:T(8,128)S(1)}, bf16[32,8,768]{2,1,0:T(8,128)(2,1)}, f32[512,1]{1,0:T(8,128)S(1)}) custom-call(bf16[512,1280]{1,0:T(8,128)(2,1)S(1)} %bitcast.7, bf16[3200,768]{1,0:T(8,128)(2,1)S(1)} %bitcast.10), custom_call_target="tpu_custom_call" | custom-call | flops 117964800 | bytes 6291456 | tf_op jit(solution)/shard_map/pallas_call | solution.py:233
  54.8 6.5 %all-to-all-start.1 = ((bf16[32,8,768]{2,1,0:T(8,128)(2,1)}), bf16[32,8,768]{2,1,0:T(8,128)(2,1)S(1)}, u32[]{:S(2)}, u32[]{:S(2)}) async-start(bf16[32,8,768]{2,1,0:T(8,128)(2,1)} %get-tuple-element.32), calls=%async_computation.1 | async-start | bytes 786432 | tf_op jit(solution)/shard_map/all_to_all | solution.py:510
  61.3 0.2 collective-permute-start.2
  61.6 2.6 %collective-permute-start.1 = (bf16[512,384]{1,0:T(8,128)(2,1)S(1)}, bf16[512,384]{1,0:T(8,128)(2,1)S(1)}, u32[]{:S(2)}, u32[]{:S(2)}) collective-permute-start(bf16[512,384]{1,0:T(8,128)(2,1)S(1)} %shard_map.95.set0_ref), channel_id=1, source_target_pairs={{0,160},{32,128},{128,32},{160,0},{1,161},{33,129},{129,33},{161,1... | collective-permute-start | bytes 1179656 | tf_op jit(solution)/shard_map/ppermute | solution.py:518
  64.2 0.5 collective-permute-start
  64.7 2.8 %collective-permute-start.3 = (bf16[512,384]{1,0:T(8,128)(2,1)S(1)}, bf16[512,384]{1,0:T(8,128)(2,1)S(1)}, u32[]{:S(2)}, u32[]{:S(2)}) collective-permute-start(bf16[512,384]{1,0:T(8,128)(2,1)S(1)} %shard_map.95.set0_ref), channel_id=1, source_target_pairs={{0,64},{64,0},{1,65},{65,1},{2,66},{66,2},{3,67},{67,3},{4,68},{68... | collective-permute-start | bytes 1179656 | tf_op jit(solution)/shard_map/ppermute | solution.py:514
  67.5 2.6 %collective-permute-done.2.set0b_ref = bf16[512,384]{1,0:T(8,128)(2,1)S(1)} collective-permute-done((bf16[512,384]{1,0:T(8,128)(2,1)S(1)}, bf16[512,384]{1,0:T(8,128)(2,1)S(1)}, u32[]{:S(2)}, u32[]{:S(2)}) %collective-permute-start.2) | collective-permute-done | bytes 393248 | tf_op jit(solution)/shard_map/ppermute | solution.py:518
  70.1 1.1 %collective-permute-done.1.set2b_ref = bf16[512,384]{1,0:T(8,128)(2,1)S(1)} collective-permute-done((bf16[512,384]{1,0:T(8,128)(2,1)S(1)}, bf16[512,384]{1,0:T(8,128)(2,1)S(1)}, u32[]{:S(2)}, u32[]{:S(2)}) %collective-permute-start.1) | collective-permute-done | bytes 393248 | tf_op jit(solution)/shard_map/ppermute | solution.py:518
  71.2 8.5 %collective-permute-done.set2_ref = bf16[512,384]{1,0:T(8,128)(2,1)S(1)} collective-permute-done((bf16[512,384]{1,0:T(8,128)(2,1)S(1)}, bf16[512,384]{1,0:T(8,128)(2,1)S(1)}, u32[]{:S(2)}, u32[]{:S(2)}) %collective-permute-start) | collective-permute-done | bytes 393248 | tf_op jit(solution)/shard_map/ppermute | solution.py:518
  79.8 0.0 all-to-all-done.1
  79.8 3.0 %collective-permute-start.4 = (bf16[512,384]{1,0:T(8,128)(2,1)S(1)}, bf16[512,384]{1,0:T(8,128)(2,1)S(1)}, u32[]{:S(2)}, u32[]{:S(2)}) collective-permute-start(bf16[512,384]{1,0:T(8,128)(2,1)S(1)} %collective-permute-done.2.set0b_ref), channel_id=1, source_target_pairs={{0,64},{64,0},{1,65},{65,1},{2,66},{66,2},{3,67},{67,3},{4,68},{68... | collective-permute-start | bytes 1179656 | tf_op jit(solution)/shard_map/ppermute | solution.py:514
  82.8 0.1 collective-permute-start.5
  82.8 0.4 collective-permute-start.6
  83.3 0.9 shard_map.96
  84.1 0.0 collective-permute-done.3.set1_ref
  84.1 0.0 collective-permute-done.4.set1b_ref
  84.1 0.5 collective-permute-done.5.set3_ref
  84.7 0.6 collective-permute-done.6.set3b_ref
  85.2 1.3 %shard_map.97 = (f32[4,8,1920]{2,1,0:T(8,128)S(1)}, f32[4,8,1920]{2,1,0:T(8,128)S(1)}, f32[8,1024]{1,0:T(8,128)S(1)}) custom-call(bf16[256,768]{1,0:T(8,128)(2,1)S(1)} %bitcast.12, f32[512,1]{1,0:T(8,128)S(1)} %get-tuple-element.34.target_ref, bf16[512,384]{1,0:T(8,128)(2,1)S(1)} %shard_map.95.set0_ref, ...), custom_call_target="tpu_custom_call" | custom-call | flops 603979776 | bytes 4194304 | tf_op jit(solution)/shard_map/pallas_call | solution.py:406
  86.5 0.5 collective-permute-start.7
  87.0 1.1 %collective-permute-done.7.got_ref = f32[4,8,1920]{2,1,0:T(8,128)S(1)} collective-permute-done((f32[4,8,1920]{2,1,0:T(8,128)S(1)}, f32[4,8,1920]{2,1,0:T(8,128)S(1)}, u32[]{:S(2)}, u32[]{:S(2)}) %collective-permute-start.7) | collective-permute-done | bytes 245792 | tf_op jit(solution)/shard_map/ppermute | solution.py:514
  88.2 1.3 %collective-permute-start.8 = (f32[8,1920]{1,0:T(8,128)S(1)}, f32[8,1920]{1,0:T(8,128)S(1)}, u32[]{:S(2)}, u32[]{:S(2)}) collective-permute-start(f32[8,1920]{1,0:T(8,128)S(1)} %get-tuple-element.44), channel_id=1, source_target_pairs={{0,128},{32,160},{128,0},{160,32},{1,129},{33,161},{129,1},{161,33... | collective-permute-start | bytes 184328 | tf_op jit(solution)/shard_map/ppermute | solution.py:518
  89.5 1.6 %collective-permute-start.9 = (f32[8,1920]{1,0:T(8,128)S(1)}, f32[8,1920]{1,0:T(8,128)S(1)}, u32[]{:S(2)}, u32[]{:S(2)}) collective-permute-start(f32[8,1920]{1,0:T(8,128)S(1)} %get-tuple-element.45), channel_id=1, source_target_pairs={{0,160},{32,128},{128,32},{160,0},{1,161},{33,129},{129,33},{161,1... | collective-permute-start | bytes 184328 | tf_op jit(solution)/shard_map/ppermute | solution.py:518
  91.1 0.3 collective-permute-start.10
  91.4 1.4 %collective-permute-done.8.part1_ref = f32[8,1920]{1,0:T(8,128)S(1)} collective-permute-done((f32[8,1920]{1,0:T(8,128)S(1)}, f32[8,1920]{1,0:T(8,128)S(1)}, u32[]{:S(2)}, u32[]{:S(2)}) %collective-permute-start.8) | collective-permute-done | bytes 61472 | tf_op jit(solution)/shard_map/ppermute | solution.py:518
  92.8 1.9 %collective-permute-done.9.part2_ref = f32[8,1920]{1,0:T(8,128)S(1)} collective-permute-done((f32[8,1920]{1,0:T(8,128)S(1)}, f32[8,1920]{1,0:T(8,128)S(1)}, u32[]{:S(2)}, u32[]{:S(2)}) %collective-permute-start.9) | collective-permute-done | bytes 61472 | tf_op jit(solution)/shard_map/ppermute | solution.py:518
  94.7 0.1 collective-permute-done.10.part3_ref
  94.8 1.3 %shard_map.99 = (f32[1,1]{1,0:T(1,128)}, f32[8,768]{1,0:T(8,128)}, f32[8,768]{1,0:T(8,128)}) custom-call(f32[8,1920]{1,0:T(8,128)S(1)} %get-tuple-element.43.part0_ref, f32[8,1920]{1,0:T(8,128)S(1)} %collective-permute-done.8.part1_ref, f32[8,1920]{1,0:T(8,128)S(1)} %collective-permute-done.9.part2_ref, f32[8,1920]{1,0:T(8,128)S(1)} %collective-permute-done.10.part3_ref, ...), custom_call_target="tpu_custom_call" | custom-call | flops 25165824 | bytes 5242880 | tf_op jit(solution)/shard_map/pallas_call | solution.py:492
  (5 shorter events, 0.1 us)
Async XLA Ops:
  0.6 51.7 %slice-start = ((s8[4915200]{0:T(1024)(128)(4,1)}), s8[4194304]{0:T(1024)(128)(4,1)S(1)}, s32[]{:S(2)}) async-start(s8[4915200]{0:T(1024)(128)(4,1)} %bitcast.9), calls=%async_computation.2 | async-start | bytes 8388608
  0.6 51.6 %slice-start.1 = ((s8[4915200]{0:T(1024)(128)(4,1)}), s8[720896]{0:T(1024)(128)(4,1)S(1)}, s32[]{:S(2)}) async-start(s8[4915200]{0:T(1024)(128)(4,1)} %bitcast.9), calls=%async_computation.3 | async-start | bytes 1441792
  54.8 25.0 %all-to-all-start.1 = ((bf16[32,8,768]{2,1,0:T(8,128)(2,1)}), bf16[32,8,768]{2,1,0:T(8,128)(2,1)S(1)}, u32[]{:S(2)}, u32[]{:S(2)}) async-start(bf16[32,8,768]{2,1,0:T(8,128)(2,1)} %get-tuple-element.32), calls=%async_computation.1 | async-start | bytes 786432 | tf_op jit(solution)/shard_map/all_to_all | solution.py:510
  61.3 8.8 %collective-permute-start.2 = (bf16[512,384]{1,0:T(8,128)(2,1)S(1)}, bf16[512,384]{1,0:T(8,128)(2,1)S(1)}, u32[]{:S(2)}, u32[]{:S(2)}) collective-permute-start(bf16[512,384]{1,0:T(8,128)(2,1)S(1)} %shard_map.95.set0_ref), channel_id=1, source_target_pairs={{0,32},{32,0},{128,160},{160,128},{1,33},{33,1},{129,161},{161,129... | collective-permute-start | bytes 1179656 | tf_op jit(solution)/shard_map/ppermute | solution.py:518
  61.6 9.7 %collective-permute-start.1 = (bf16[512,384]{1,0:T(8,128)(2,1)S(1)}, bf16[512,384]{1,0:T(8,128)(2,1)S(1)}, u32[]{:S(2)}, u32[]{:S(2)}) collective-permute-start(bf16[512,384]{1,0:T(8,128)(2,1)S(1)} %shard_map.95.set0_ref), channel_id=1, source_target_pairs={{0,160},{32,128},{128,32},{160,0},{1,161},{33,129},{129,33},{161,1... | collective-permute-start | bytes 1179656 | tf_op jit(solution)/shard_map/ppermute | solution.py:518
  64.2 15.6 %collective-permute-start = (bf16[512,384]{1,0:T(8,128)(2,1)S(1)}, bf16[512,384]{1,0:T(8,128)(2,1)S(1)}, u32[]{:S(2)}, u32[]{:S(2)}) collective-permute-start(bf16[512,384]{1,0:T(8,128)(2,1)S(1)} %shard_map.95.set0_ref), channel_id=1, source_target_pairs={{0,128},{32,160},{128,0},{160,32},{1,129},{33,161},{129,1},{161,33... | collective-permute-start | bytes 1179656 | tf_op jit(solution)/shard_map/ppermute | solution.py:518
  64.7 19.4 %collective-permute-start.3 = (bf16[512,384]{1,0:T(8,128)(2,1)S(1)}, bf16[512,384]{1,0:T(8,128)(2,1)S(1)}, u32[]{:S(2)}, u32[]{:S(2)}) collective-permute-start(bf16[512,384]{1,0:T(8,128)(2,1)S(1)} %shard_map.95.set0_ref), channel_id=1, source_target_pairs={{0,64},{64,0},{1,65},{65,1},{2,66},{66,2},{3,67},{67,3},{4,68},{68... | collective-permute-start | bytes 1179656 | tf_op jit(solution)/shard_map/ppermute | solution.py:514
  79.8 4.4 %collective-permute-start.4 = (bf16[512,384]{1,0:T(8,128)(2,1)S(1)}, bf16[512,384]{1,0:T(8,128)(2,1)S(1)}, u32[]{:S(2)}, u32[]{:S(2)}) collective-permute-start(bf16[512,384]{1,0:T(8,128)(2,1)S(1)} %collective-permute-done.2.set0b_ref), channel_id=1, source_target_pairs={{0,64},{64,0},{1,65},{65,1},{2,66},{66,2},{3,67},{67,3},{4,68},{68... | collective-permute-start | bytes 1179656 | tf_op jit(solution)/shard_map/ppermute | solution.py:514
  82.8 1.9 %collective-permute-start.5 = (bf16[512,384]{1,0:T(8,128)(2,1)S(1)}, bf16[512,384]{1,0:T(8,128)(2,1)S(1)}, u32[]{:S(2)}, u32[]{:S(2)}) collective-permute-start(bf16[512,384]{1,0:T(8,128)(2,1)S(1)} %collective-permute-done.set2_ref), channel_id=1, source_target_pairs={{0,64},{64,0},{1,65},{65,1},{2,66},{66,2},{3,67},{67,3},{4,68},{68... | collective-permute-start | bytes 1179656 | tf_op jit(solution)/shard_map/ppermute | solution.py:514
  82.8 2.4 %collective-permute-start.6 = (bf16[512,384]{1,0:T(8,128)(2,1)S(1)}, bf16[512,384]{1,0:T(8,128)(2,1)S(1)}, u32[]{:S(2)}, u32[]{:S(2)}) collective-permute-start(bf16[512,384]{1,0:T(8,128)(2,1)S(1)} %collective-permute-done.1.set2b_ref), channel_id=1, source_target_pairs={{0,64},{64,0},{1,65},{65,1},{2,66},{66,2},{3,67},{67,3},{4,68},{68... | collective-permute-start | bytes 1179656 | tf_op jit(solution)/shard_map/ppermute | solution.py:514
  86.5 1.6 %collective-permute-start.7 = (f32[4,8,1920]{2,1,0:T(8,128)S(1)}, f32[4,8,1920]{2,1,0:T(8,128)S(1)}, u32[]{:S(2)}, u32[]{:S(2)}) collective-permute-start(f32[4,8,1920]{2,1,0:T(8,128)S(1)} %get-tuple-element.42), channel_id=1, source_target_pairs={{0,64},{64,0},{1,65},{65,1},{2,66},{66,2},{3,67},{67,3},{4,68},{68... | collective-permute-start | bytes 737288 | tf_op jit(solution)/shard_map/ppermute | solution.py:514
  88.2 4.7 %collective-permute-start.8 = (f32[8,1920]{1,0:T(8,128)S(1)}, f32[8,1920]{1,0:T(8,128)S(1)}, u32[]{:S(2)}, u32[]{:S(2)}) collective-permute-start(f32[8,1920]{1,0:T(8,128)S(1)} %get-tuple-element.44), channel_id=1, source_target_pairs={{0,128},{32,160},{128,0},{160,32},{1,129},{33,161},{129,1},{161,33... | collective-permute-start | bytes 184328 | tf_op jit(solution)/shard_map/ppermute | solution.py:518
  89.5 5.2 %collective-permute-start.9 = (f32[8,1920]{1,0:T(8,128)S(1)}, f32[8,1920]{1,0:T(8,128)S(1)}, u32[]{:S(2)}, u32[]{:S(2)}) collective-permute-start(f32[8,1920]{1,0:T(8,128)S(1)} %get-tuple-element.45), channel_id=1, source_target_pairs={{0,160},{32,128},{128,32},{160,0},{1,161},{33,129},{129,33},{161,1... | collective-permute-start | bytes 184328 | tf_op jit(solution)/shard_map/ppermute | solution.py:518
  91.1 3.7 %collective-permute-start.10 = (f32[8,1920]{1,0:T(8,128)S(1)}, f32[8,1920]{1,0:T(8,128)S(1)}, u32[]{:S(2)}, u32[]{:S(2)}) collective-permute-start(f32[8,1920]{1,0:T(8,128)S(1)} %get-tuple-element.46), channel_id=1, source_target_pairs={{0,32},{32,0},{128,160},{160,128},{1,33},{33,1},{129,161},{161,129... | collective-permute-start | bytes 184328 | tf_op jit(solution)/shard_map/ppermute | solution.py:518

commit v7 on v6

--- a/solution.py
+++ b/solution.py
@@ -25,7 +25,7 @@
 SENT = WIDE * HD
 TAIL = 4 * HD
 TILE = 256
-SET = 512
+SET = CLIPS * 8
 PLANE_ROWS = 256
 SUMS = 2 * E + TILE + 128
 PIECE = E // 2
@@ -55,10 +55,14 @@
     return values / norms, norms
 
 
+def label_of(xh, xl, y):
+    return (2 * xh + xl + 2 * y) % 4
+
+
 def clip_kernel(
     video_hbm, token_hbm, pool_hbm, text_hbm, pair_hbm,
-    out_ref, hat_ref, norm_ref,
-    video_ref, token_ref, pool_ref, text_ref, pair_ref, weight_scr, num_scr, sems,
+    num_ref, slot_ref, code_ref, hat_ref, norm_ref,
+    video_ref, token_ref, pool_ref, text_ref, pair_ref, weight_scr, sems,
 ):
     small = ((pool_hbm, pool_ref), (video_hbm, video_ref), (text_hbm, text_ref), (pair_hbm, pair_ref))
     chunks = [pl.ds(i * TOKS, TOKS) for i in range(STEPS)]
@@ -74,7 +78,7 @@
     for copy in early[1:] + loads[1:]:
         copy.start()
     weight_scr[...] = jnp.zeros_like(weight_scr)
-    num_scr[...] = jnp.zeros_like(num_scr)
+    num_ref[...] = jnp.zeros_like(num_ref)
     mine = iota((CHUNK, TOKS), 1) // TOK == iota((CHUNK, TOKS), 0)
     ones = mine.astype(f32).astype(bf16)
     lane = iota((CHUNK, HD), 1)
@@ -84,16 +88,12 @@
     hat, norm = unit_rows(text_ref[...].astype(f32))
     hat_ref[...] = hat
     norm_ref[...] = norm
-    for k in range(2):
-        texts = hat[None, :, k * PIECE : (k + 1) * PIECE]
-        texts = jnp.broadcast_to(texts, (CLIPS // 2, 8, PIECE)).reshape(CLIPS * 4, PIECE)
-        out_ref[k * CLIPS * 4 : (k + 1) * CLIPS * 4, SENT : SENT + PIECE] = texts.astype(bf16)
     early[0].wait()
     pool = pool_ref[...]
 
     def put(step, j, value):
         at = j // WIDE * CLIPS + step * CHUNK
-        num_scr[at : at + CHUNK, j % WIDE * HD : (j % WIDE + 1) * HD] = value.astype(bf16)
+        num_ref[at : at + CHUNK, j % WIDE * HD : (j % WIDE + 1) * HD] = value.astype(bf16)
 
     def weigh(step):
         loads[step].wait()
@@ -136,13 +136,9 @@
     before = (column_of(owner) == owner) & (iota((CLIPS, CLIPS), 0) < iota((CLIPS, CLIPS), 1))
     rank = jnp.sum(jnp.where(before, 1.0, 0.0), axis=0, keepdims=True)
     slot = owner * 2.0 + rank
-    slots = jnp.concatenate([slot] * PARTS, axis=1).astype(jnp.int32)
-    shape = (CLIPS * 8, PARTS * CLIPS)
-    row, col = iota(shape, 0), iota(shape, 1)
-    place = (row // PARTS == slots) & (row % PARTS == col // CLIPS)
-    out = dot(jnp.where(place, 1.0, 0.0).astype(bf16), num_scr[...])
+    slot_ref[...] = jnp.concatenate([slot] * PARTS, axis=1)
     pair = pair_ref[...]
-    codes = jnp.concatenate(
+    code_ref[...] = jnp.concatenate(
         [
             jnp.zeros((1, 72), f32),
             (pair // 64).astype(f32),
@@ -151,12 +147,46 @@
         ],
         axis=1,
     )
+
+
+def pack_kernel(num_ref, slot_ref, code_ref, hat_ref, far_ref, out_ref):
+    xh = lax.axis_index("xh")
+    shape = (CLIPS * 8, PARTS * CLIPS)
+    row, col = iota(shape, 0), iota(shape, 1)
+    place = (row // PARTS == slot_ref[...].astype(jnp.int32)) & (row % PARTS == col // CLIPS)
+    out = dot(jnp.where(place, 1.0, 0.0).astype(bf16), num_ref[...])
     last = iota((CLIPS * 8, HD), 0) % PARTS == PARTS - 1
     out_ref[:, 0:TAIL] = out[:, 0:TAIL].astype(bf16)
     out_ref[:, TAIL : TAIL + HD] = (
-        out[:, TAIL : TAIL + HD] + jnp.where(last, codes, 0.0)
+        out[:, TAIL : TAIL + HD] + jnp.where(last, code_ref[...], 0.0)
     ).astype(bf16)
     out_ref[:, TAIL + HD : SENT] = out[:, TAIL + HD : SENT].astype(bf16)
+    near = hat_ref[...]
+    far, _ = unit_rows(far_ref[...].astype(f32))
+    low = xh == 0
+    texts = jnp.concatenate([jnp.where(low, near, far), jnp.where(low, far, near)], axis=0)
+    row, col = iota((CLIPS * 8, 16), 0), iota((CLIPS * 8, 16), 1)
+    dest = row // 8
+    label = label_of(xh, dest // 32, dest % 4)
+    pick = row % 4 // 2 * 8 + 2 * label + row % 2 == col
+    texts = dot(jnp.where(pick, 1.0, 0.0).astype(bf16), texts.astype(bf16))
+    upper = iota((CLIPS * 8, PIECE), 0) % 8 < 4
+    out_ref[:, SENT : SENT + PIECE] = jnp.where(
+        upper, texts[:, 0:PIECE], texts[:, PIECE:E]
+    ).astype(bf16)
+
+
+def pack(*args):
+    return pl.pallas_call(
+        pack_kernel,
+        in_specs=[VMEM] * 5,
+        out_specs=VMEM,
+        out_shape=jax.ShapeDtypeStruct((CLIPS * 8, SENT + PIECE), bf16),
+        compiler_params=pltpu.CompilerParams(vmem_limit_bytes=24 << 20),
+        cost_estimate=pl.CostEstimate(
+            flops=2 * 512 * 256 * SENT, bytes_accessed=2 << 20, transcendentals=0
+        ),
+    )(*args)
 
 
 def clip_sums(clip_tokens, clip_video, pool_vectors, text_embed, pair_text):
@@ -170,16 +200,17 @@
     return pl.pallas_call(
         clip_kernel,
         in_specs=[pl.BlockSpec(memory_space=pltpu.HBM)] * 5,
-        out_specs=[VMEM] * 3,
+        out_specs=[VMEM] * 5,
         out_shape=[
-            jax.ShapeDtypeStruct((CLIPS * 8, SENT + PIECE), bf16),
+            jax.ShapeDtypeStruct((PARTS * CLIPS, SENT), bf16),
+            jax.ShapeDtypeStruct((1, PARTS * CLIPS), f32),
+            jax.ShapeDtypeStruct((1, HD), f32),
             jax.ShapeDtypeStruct((8, E), f32),
             jax.ShapeDtypeStruct((8, 1), f32),
         ],
         scratch_shapes=[pltpu.VMEM(x.shape, x.dtype) for x in args]
         + [
             pltpu.VMEM((STEPS, 128, TOKS), f32),
-            pltpu.VMEM((PARTS * CLIPS, SENT), bf16),
             pltpu.SemaphoreType.DMA((STEPS + 4,)),
         ],
         compiler_params=pltpu.CompilerParams(vmem_limit_bytes=24 << 20),
@@ -249,7 +280,12 @@
 
 
 def text_kernel(arrived_ref, text_ref):
-    text_ref[...] = arrived_ref[:, SENT : SENT + PIECE]
+    halves = arrived_ref[:, SENT : SENT + PIECE]
+    row, col = iota((TILE, CLIPS * 8), 0), iota((TILE, CLIPS * 8), 1)
+    for part in range(2):
+        pick = row // 4 * 8 + part * 4 + row % 4 == col
+        texts = dot(jnp.where(pick, 1.0, 0.0).astype(bf16), halves)
+        text_ref[:, part * PIECE : (part + 1) * PIECE] = texts.astype(bf16)
 
 
 def text_piece(arrived):
@@ -257,9 +293,11 @@
         text_kernel,
         in_specs=[VMEM],
         out_specs=VMEM,
-        out_shape=jax.ShapeDtypeStruct((SET, PIECE), bf16),
+        out_shape=jax.ShapeDtypeStruct((TILE, E), bf16),
         compiler_params=pltpu.CompilerParams(vmem_limit_bytes=16 << 20),
-        cost_estimate=pl.CostEstimate(flops=0, bytes_accessed=1 << 20, transcendentals=0),
+        cost_estimate=pl.CostEstimate(
+            flops=4 * 256 * 512 * PIECE, bytes_accessed=1 << 20, transcendentals=0
+        ),
     )(arrived)
 
 
@@ -276,28 +314,32 @@
     return other(xh, k // 2) * 2 + other(c, k % 2)
 
 
-def halves_of(ref, xl):
-    return (
-        ref[:, pl.ds(pl.multiple_of(xl * PIECE, 128), PIECE)],
-        ref[:, pl.ds(pl.multiple_of((1 - xl) * PIECE, 128), PIECE)],
-    )
-
-
-def score(videos, target, pieces, row, own_ref, at, tile_scr, cols_ref, sums, positive, base):
-    lane = iota((1, TILE), 1).astype(f32)
-    for t in range(2):
-        tile = row * 2 + t
-        rows = slice(t * TILE, (t + 1) * TILE)
-        logits = SCALE * (
-            dot(videos[0], pieces[0][rows, :], NT) + dot(videos[1], pieces[1][rows, :], NT)
-        )
+def tile_of(xh, c, xl, spot, k):
+    y = spot % 4
+    label = (
+        label_of(xh, xl, y),
+        label_of(xh, 1 - xl, y),
+        label_of(1 - xh, 1 - xl, y),
+        label_of(xh, xl, y + 1),
+    )[k % 4]
+    return other(c, k // 4) * 4 + label
+
+
+def texts_of(tile, j):
+    row = j % 4 // 2 * 2 + tile // 4
+    return ((row * 64 + j // 4) * 8 + tile % 4 * 2 + j % 2).astype(f32)
+
+
+def score(videos, target, pieces, tiles, own_ref, tile_scr, cols_ref, sums, positive, base):
+    for n, (ref, tile) in enumerate(zip(pieces, tiles)):
+        logits = SCALE * dot(videos, ref[...], NT)
         ex = jnp.exp(logits)
         tile_scr[...] = ex
         cols_ref[pl.ds(tile, 1), :] = jnp.sum(ex, axis=0, keepdims=True)
         sums += ex[:, 0:128] + ex[:, 128:TILE]
-        hit = target == (tile * TILE).astype(f32) + lane
+        hit = target == texts_of(tile, iota((1, TILE), 1))
         positive += jnp.sum(jnp.where(hit, logits, 0.0), axis=0, keepdims=True)
-        own_ref[:, at + t * TILE : at + (t + 1) * TILE] = tile_scr[pl.ds(base, 8), :]
+        own_ref[:, n * TILE : (n + 1) * TILE] = tile_scr[pl.ds(base, 8), :]
     return sums, positive
 
 
@@ -306,69 +348,56 @@
 
 
 def first_kernel(
-    video_ref, target_ref, set0_ref, set0b_ref, set2_ref, set2b_ref,
+    video_ref, target_ref, set0_ref, set1_ref, set2_ref, set3_ref,
     own_ref, cols_ref, sums_ref, positive_ref, tile_scr,
 ):
     xh, c, xl, spot = position()
-    target = plane_rows(target_ref, xl)
-    videos = halves_of(video_ref, xl)
-    base = pl.multiple_of(spot * 8, 8)
     cols_ref[...] = jnp.zeros_like(cols_ref)
-    sums, positive = jnp.zeros((PLANE_ROWS, 128), f32), jnp.zeros((1, TILE), f32)
-    for n, pieces in enumerate(((set0_ref, set0b_ref), (set2_ref, set2b_ref))):
-        sums, positive = score(
-            videos, target, pieces, row_of(xh, c, 2 * n), own_ref, n * SET, tile_scr, cols_ref,
-            sums, positive, base,
-        )
-    sums_ref[...] = sums
-    positive_ref[...] = positive
+    sums_ref[...], positive_ref[...] = score(
+        video_ref[...], plane_rows(target_ref, xl), (set0_ref, set1_ref, set2_ref, set3_ref),
+        [tile_of(xh, c, xl, spot, k) for k in range(4)], own_ref, tile_scr, cols_ref,
+        jnp.zeros((PLANE_ROWS, 128), f32), jnp.zeros((1, TILE), f32), pl.multiple_of(spot * 8, 8),
+    )
 
 
 def second_kernel(
-    video_ref, target_ref, set0_ref, set0b_ref, set2_ref, set2b_ref, set1_ref, set1b_ref, set3_ref,
-    set3b_ref, cols_ref, sums_ref, positive_ref,
+    video_ref, target_ref, set0_ref, set1_ref, set2_ref, set3_ref, set4_ref, set5_ref, set6_ref,
+    set7_ref, cols_ref, sums_ref, positive_ref,
     keep_ref, send_ref, own_ref, tile_scr, col_scr,
 ):
     xh, c, xl, spot = position()
     target = plane_rows(target_ref, xl)
-    videos = halves_of(video_ref, xl)
-    base = pl.multiple_of(spot * 8, 8)
-    sets = (
-        (set0_ref, set0b_ref), (set1_ref, set1b_ref), (set2_ref, set2b_ref), (set3_ref, set3b_ref)
-    )
+    videos = video_ref[...]
+    pieces = (set0_ref, set1_ref, set2_ref, set3_ref, set4_ref, set5_ref, set6_ref, set7_ref)
+    tiles = [tile_of(xh, c, xl, spot, k) for k in range(8)]
     col_scr[...] = cols_ref[...]
-    sums, positive = sums_ref[...], positive_ref[...]
-    for n, k in enumerate((1, 3)):
-        sums, positive = score(
-            videos, target, sets[k], row_of(xh, c, k), own_ref, n * SET, tile_scr, col_scr,
-            sums, positive, base,
+    sums, positive = score(
+        videos, target, pieces[4:8], tiles[4:8], own_ref, tile_scr, col_scr,
+        sums_ref[...], positive_ref[...], pl.multiple_of(spot * 8, 8),
+    )
+
+    def near_texts(slot):
+        group = sum(
+            jnp.where(slot // 8 == n, row_of(xh, c, n // 2) * 2 + n % 2, 0) for n in range(8)
         )
-    odd = spot % 2 == 1
-    logits, groups = 0.0, []
-    for part in range(2):
-        near = []
-        for k in range(4):
-            for half in range(2):
-                at = pl.multiple_of(half * PLANE_ROWS + spot // 2 * 16, 16)
-                pair = sets[k][part][pl.ds(at, 16), :].astype(f32)
-                near.append(jnp.where(odd, pair[8:16], pair[0:8]))
-        near = jnp.concatenate(near, axis=0).astype(bf16)
-        logits += dot(videos[part], near, NT)
-    near = jnp.exp(SCALE * logits)
+        return ((group * 32 + spot) * 8 + slot % 8).astype(f32)
+
+    column = near_texts(iota((64, 1), 0))
+    near = jnp.zeros((64, E), f32)
+    for ref, tile in zip(pieces, tiles):
+        pick = column == texts_of(tile, iota((1, TILE), 1))
+        near += dot(jnp.where(pick, 1.0, 0.0).astype(bf16), ref[...])
+    near = jnp.exp(SCALE * dot(videos, near.astype(bf16), NT))
     rowsum = jnp.sum(sums, axis=1, keepdims=True)
     total = jnp.sum(jnp.log(rowsum), axis=0, keepdims=True) - 2.0 * jnp.sum(
         positive, axis=1, keepdims=True
     )
-    slot = iota((1, 64), 1)
-    group = sum(
-        jnp.where(slot // 8 == n, row_of(xh, c, n // 2) * 2 + n % 2, 0) for n in range(8)
-    )
-    text = ((group * 32 + spot) * 8 + slot % 8).astype(f32)
+    text = near_texts(iota((1, 64), 1))
     first = near / rowsum - jnp.where(target == text, 2.0, 0.0)
     first_hi = first.astype(bf16).astype(f32)
     near_hi = near.astype(bf16).astype(f32)
     terms = jnp.concatenate([first_hi, first - first_hi, near_hi, near - near_hi], axis=1)
-    sums = dot(terms.astype(bf16), video_ref[...], TN)
+    sums = dot(terms.astype(bf16), videos, TN)
     first, second = sums[0:64] + sums[64:128], sums[128:192] + sums[192:256]
     cols = col_scr[...]
     total = jnp.broadcast_to(total, (8, 128))
@@ -438,7 +467,7 @@
 
 def grad_kernel(
     part0_ref, part1_ref, part2_ref, part3_ref, own_ref, last_ref, target_ref,
-    set0_ref, set0b_ref, set2_ref, set2b_ref, set1_ref, set1b_ref, set3_ref, set3b_ref,
+    set0_ref, set1_ref, set2_ref, set3_ref, set4_ref, set5_ref, set6_ref, set7_ref,
     video_hat_ref, video_norm_ref, text_hat_ref, text_norm_ref, loss_ref, video_grad_ref, text_grad_ref, col_scr,
 ):
     xh, c, xl, spot = position()
@@ -451,40 +480,28 @@
     def project(direction, hat, norm):
         return (direction - jnp.sum(direction * hat, axis=1, keepdims=True) * hat) / norm
 
-    group = (xh * 2 + c) * 2 + xl
-    mine = jnp.broadcast_to(col_scr[pl.ds(group, 1), :], (8, TILE))
-    here = iota((8, TILE), 1) == spot * 8 + iota((8, TILE), 0)
-    mine = jnp.sum(jnp.where(here, mine, 0.0), axis=1, keepdims=True)
+    at = (xl * 32 + spot) * 4 + xh * 2
+    lane = iota((4, TILE), 1) - at
+    mine = jnp.where(c == 0, cols[0:4], cols[4:8])
+    pair = [jnp.sum(jnp.where(lane == n, mine, 0.0), axis=1, keepdims=True) for n in range(2)]
+    row = iota((8, 1), 0)
+    mine = sum(
+        jnp.where(row == n, pair[n % 2][n // 2 : n // 2 + 1], 0.0) for n in range(8)
+    )
     text_dir = SCALE * (got[:, 0:E] + got[:, E : 2 * E] / mine)
     text_grad_ref[...] = project(text_dir, text_hat_ref[...], text_norm_ref[...])
 
     rows = jnp.concatenate([own_ref[...], last_ref[...]], axis=1)
     rowsum = jnp.sum(rows, axis=1, keepdims=True)
     target = target_ref[pl.ds(pl.multiple_of((xl * 32 + spot) * 8, 8), 8), :]
-    lane = iota((8, TILE), 1).astype(f32)
-    direction = [jnp.zeros((8, PIECE), f32)] * 2
-    sets = ((set0_ref, set0b_ref), (set2_ref, set2b_ref), (set1_ref, set1b_ref), (set3_ref, set3b_ref))
-    for n, k in enumerate((0, 2, 1, 3)):
-        row = row_of(xh, c, k)
-        for t in range(2):
-            tile = row * 2 + t
-            at = n * SET + t * TILE
-            ex = rows[:, at : at + TILE]
-            hot = jnp.where(target == (tile * TILE).astype(f32) + lane, 2.0, 0.0)
-            probe = ex / rowsum + ex / col_scr[pl.ds(tile, 1), :] - hot
-            probe = probe.astype(bf16)
-            direction = [
-                total + dot(probe, ref[t * TILE : (t + 1) * TILE, :])
-                for total, ref in zip(direction, sets[n])
-            ]
-    low = xl == 0
-    direction = jnp.concatenate(
-        [
-            jnp.where(low, direction[0], direction[1]),
-            jnp.where(low, direction[1], direction[0]),
-        ],
-        axis=1,
-    )
+    direction = jnp.zeros((8, E), f32)
+    pieces = (set0_ref, set1_ref, set2_ref, set3_ref, set4_ref, set5_ref, set6_ref, set7_ref)
+    for k, ref in enumerate(pieces):
+        tile = tile_of(xh, c, xl, spot, k)
+        ex = rows[:, k * TILE : (k + 1) * TILE]
+        hot = jnp.where(target == texts_of(tile, iota((1, TILE), 1)), 2.0, 0.0)
+        probe = ex / rowsum + ex / col_scr[pl.ds(tile, 1), :] - hot
+        direction += dot(probe.astype(bf16), ref[...])
     video_grad_ref[...] = project(SCALE * direction, video_hat_ref[...], video_norm_ref[...])
 
 
@@ -518,18 +535,24 @@
     return lax.ppermute(x, ("xh", "xl"), [(k, k ^ step) for k in range(4)])
 
 
+def turn_y(x):
+    return lax.ppermute(x, "y", [(k, k ^ 1) for k in range(4)])
+
+
 def body(clip_tokens, clip_video, pool_vectors, out_proj, text_embed, pair_text):
-    outgoing, text_hat, text_norm = clip_sums(
+    far_text = along(text_embed, 2)
+    *sums, text_hat, text_norm = clip_sums(
         clip_tokens, clip_video, pool_vectors, text_embed, pair_text
     )
+    outgoing = pack(*sums, text_hat, far_text)
     arrived = exchange(outgoing.reshape(CLIPS, 8, SENT + PIECE), ROW)
     arrived = arrived.reshape(CLIPS * 8, SENT + PIECE)
     texts = text_piece(arrived)
-    moved = [along(texts, step) for step in (2, 3, 1)]
+    moved = [turn_y(texts), along(texts, 3), along(texts, 1)]
     video_embed, video_hat, video_norm, send, target = embed(arrived, out_proj)
-    videos, *moved = lax.optimization_barrier((exchange(send, PLANE), *moved))
+    videos, moved[0] = lax.optimization_barrier((exchange(send, PLANE), moved[0]))
     videos = videos.reshape(PLANE_ROWS, E)
-    mine = (texts, moved[2], moved[0], moved[1])
+    mine = (texts, moved[2], moved[1], moved[0])
     theirs = tuple(swap(x) for x in mine)
     own, cols, sums, positive = first_logits(videos, target, *mine)
     keep, send, last = second_logits(videos, target, *mine, *theirs, cols, sums, positive)

time: 96.3 us -> 94.6 us (0.982)
  waiting for transfers between devices: 17.9 us -> 10.8 us
  starting transfers between devices: 19.8 us -> 24.9 us
  blocking collectives: 45.6 us -> 43.8 us
  Pallas kernels: 12.1 us -> 13.4 us
    ppermute x6, waiting for transfers between devices: 15.7 us -> 7.33 us  [along(): return lax.ppermute(x, ('xh', 'xl'), [(k, k ^ step) for k in range(4)])]
    ppermute x5, starting transfers between devices: 6.72 us -> 9.14 us  [swap(): return lax.ppermute(x, 'c', [(0, 1), (1, 0)])]
    all_to_all x1, blocking collectives: 45.6 us -> 43.8 us  [exchange(): return lax.all_to_all(x, axes, 0, 0, tiled=True)]
    ppermute x0 -> x1, waiting for transfers between devices: none -> 1.73 us  [turn_y(): return lax.ppermute(x, 'y', [(k, k ^ 1) for k in range(4)])]
    ppermute x6, starting transfers between devices: 6.6 us -> 8.13 us  [along(): return lax.ppermute(x, ('xh', 'xl'), [(k, k ^ step) for k in range(4)])]
    ppermute x0 -> x1, starting transfers between devices: none -> 1.23 us  [turn_y(): return lax.ppermute(x, 'y', [(k, k ^ 1) for k in range(4)])]
  transfers between devices with their start and end apart: 12 -> 13, of which waited for: 9 -> 6; matrix products, arithmetic and copies ran while one was open for 0% -> 0% of each run, Pallas kernels for 1% -> 7%
where the time goes in v7:
time: 94.6 us; the launch traced here: 94.3 us
  blocking collectives  43.8 us (46%)
  starting transfers between devices  24.9 us (26%)
  Pallas kernels  13.4 us (14%)
  waiting for transfers between devices  10.8 us (11%)
    all_to_all x1, blocking collectives, exchange(): return lax.all_to_all(x, axes, 0, 0, tiled=True)  43.8 us
    ppermute x5, starting transfers between devices, swap(): return lax.ppermute(x, 'c', [(0, 1), (1, 0)])  9.14 us
    ppermute x6, starting transfers between devices, along(): return lax.ppermute(x, ('xh', 'xl'), [(k, k ^ step) for k in range(4)])  8.13 us
    ppermute x6, waiting for transfers between devices, along(): return lax.ppermute(x, ('xh', 'xl'), [(k, k ^ step) for k in range(4)])  7.33 us
    all_to_all x1, starting transfers between devices, exchange(): return lax.all_to_all(x, axes, 0, 0, tiled=True)  6.38 us
    pallas_call x1, Pallas kernels, clip_sums(): pl.pallas_call(clip_kernel, in_specs=[pl.BlockSpec(memory_space=pltpu.HBM...  5.59 us
    pallas_call x1, Pallas kernels, embed(): pl.pallas_call(embed_kernel, in_specs=[VMEM, VMEM], out_specs=[VMEM] * 5,...  2.49 us
    pallas_call x1, Pallas kernels, second_logits(): pl.pallas_call(second_kernel, in_specs=[VMEM] * 13, out_specs=[VMEM] * 3,...  2 us
  transfers between devices with their start and end apart: 13, of which 6 were waited for; matrix products, arithmetic and copies ran while one was open for 0% of the time, Pallas kernels for 7%

profile of v7, /device:TPU:1, one launch (start us, length us, event | category | flops | bytes accessed | tf_op | source)
XLA Modules:
  0.0 94.3 jit_solution(174822166538439928)
XLA Ops:
  0.6 3.7 %collective-permute-start = (bf16[8,768]{1,0:T(8,128)(2,1)}, bf16[8,768]{1,0:T(8,128)(2,1)S(1)}, u32[]{:S(2)}, u32[]{:S(2)}) collective-permute-start(bf16[8,768]{1,0:T(8,128)(2,1)} %text_hbm.1), channel_id=1, source_target_pairs={{0,128},{32,160},{128,0},{160,32},{1,129},{33,161},{129,1},{161,33... | collective-permute-start | bytes 36872 | tf_op jit(solution)/shard_map/ppermute | solution.py:535
  4.3 5.6 %shard_map.93 = (bf16[256,896]{1,0:T(8,128)(2,1)S(1)}, f32[1,256]{1,0:T(1,128)S(1)}, f32[1,128]{1,0:T(1,128)S(1)}, f32[8,768]{1,0:T(8,128)S(1)}, f32[8,1]{1,0:T(8,128)S(1)}) custom-call(s32[1,64]{1,0:T(1,128)} %bitcast.15, bf16[1024,3200]{1,0:T(8,128)(2,1)} %bitcast.14, bf16[25,3200]{1,0:T(8,128)(2,1)} %pool_hbm.1, bf16[8,768]{1,0:T(8,128)(2,1)} %text_hbm.1, ...), custom_call_target="tpu_custom_call" | custom-call | flops 419430400 | bytes 8388608 | tf_op jit(solution)/shard_map/pallas_call | solution.py:200
  9.9 0.0 copy-start
  9.9 0.0 collective-permute-done.far_ref
  9.9 0.8 shard_map.94
  10.7 43.8 %all_to_all.10 = bf16[64,8,1280]{2,1,0:T(8,128)(2,1)S(1)} all-to-all(bf16[64,8,1280]{2,1,0:T(8,128)(2,1)S(1)} %bitcast.9), channel_id=1, replica_groups=mesh['xh'=2,'c'=2,'xl'=2,'z'=8,'y'=4] {'xl','z','y'}, dimensions={0} | all-to-all | bytes 2621440 | tf_op jit(solution)/shard_map/all_to_all | solution.py:527
  54.6 2.5 %shard_map.95 = (bf16[8,768]{1,0:T(8,128)(2,1)}, f32[8,768]{1,0:T(8,128)S(1)}, f32[8,1]{1,0:T(8,128)S(1)}, bf16[32,8,768]{2,1,0:T(8,128)(2,1)}, f32[512,1]{1,0:T(8,128)S(1)}) custom-call(bf16[512,1280]{1,0:T(8,128)(2,1)S(1)} %bitcast.7, bf16[3200,768]{1,0:T(8,128)(2,1)S(1)} %bitcast.11), custom_call_target="tpu_custom_call" | custom-call | flops 117964800 | bytes 6291456 | tf_op jit(solution)/shard_map/pallas_call | solution.py:264
  57.1 0.6 copy-done.2
  57.7 6.4 %all-to-all-start.1 = ((bf16[32,8,768]{2,1,0:T(8,128)(2,1)}), bf16[32,8,768]{2,1,0:T(8,128)(2,1)S(1)}, u32[]{:S(2)}, u32[]{:S(2)}) async-start(bf16[32,8,768]{2,1,0:T(8,128)(2,1)} %get-tuple-element.35), calls=%async_computation.1 | async-start | bytes 786432 | tf_op jit(solution)/shard_map/all_to_all | solution.py:527
  64.1 0.4 shard_map.96.set0_ref
  64.5 0.9 collective-permute-start.3
  65.4 0.6 collective-permute-start.2
  66.0 1.2 %collective-permute-start.1 = (bf16[256,768]{1,0:T(8,128)(2,1)S(1)}, bf16[256,768]{1,0:T(8,128)(2,1)S(1)}, u32[]{:S(2)}, u32[]{:S(2)}) collective-permute-start(bf16[256,768]{1,0:T(8,128)(2,1)S(1)} %shard_map.96.set0_ref), channel_id=1, source_target_pairs={{0,1},{1,0},{2,3},{3,2},{4,5},{5,4},{6,7},{7,6},{8,9},{9,8},{10,11... | collective-permute-start | bytes 1179656 | tf_op jit(solution)/shard_map/ppermute | solution.py:539
  67.2 3.2 %collective-permute-start.4 = (bf16[256,768]{1,0:T(8,128)(2,1)S(1)}, bf16[256,768]{1,0:T(8,128)(2,1)S(1)}, u32[]{:S(2)}, u32[]{:S(2)}) collective-permute-start(bf16[256,768]{1,0:T(8,128)(2,1)S(1)} %shard_map.96.set0_ref), channel_id=1, source_target_pairs={{0,64},{64,0},{1,65},{65,1},{2,66},{66,2},{3,67},{67,3},{4,68},{68... | collective-permute-start | bytes 1179656 | tf_op jit(solution)/shard_map/ppermute | solution.py:531
  70.5 3.8 %collective-permute-done.3.set2_ref = bf16[256,768]{1,0:T(8,128)(2,1)S(1)} collective-permute-done((bf16[256,768]{1,0:T(8,128)(2,1)S(1)}, bf16[256,768]{1,0:T(8,128)(2,1)S(1)}, u32[]{:S(2)}, u32[]{:S(2)}) %collective-permute-start.3) | collective-permute-done | bytes 393248 | tf_op jit(solution)/shard_map/ppermute | solution.py:535
  74.3 3.0 %collective-permute-start.6 = (bf16[256,768]{1,0:T(8,128)(2,1)S(1)}, bf16[256,768]{1,0:T(8,128)(2,1)S(1)}, u32[]{:S(2)}, u32[]{:S(2)}) collective-permute-start(bf16[256,768]{1,0:T(8,128)(2,1)S(1)} %collective-permute-done.3.set2_ref), channel_id=1, source_target_pairs={{0,64},{64,0},{1,65},{65,1},{2,66},{66,2},{3,67},{67,3},{4,68},{68... | collective-permute-start | bytes 1179656 | tf_op jit(solution)/shard_map/ppermute | solution.py:531
  77.3 0.0 collective-permute-start.5
  77.4 1.7 %collective-permute-done.1.set3_ref = bf16[256,768]{1,0:T(8,128)(2,1)S(1)} collective-permute-done((bf16[256,768]{1,0:T(8,128)(2,1)S(1)}, bf16[256,768]{1,0:T(8,128)(2,1)S(1)}, u32[]{:S(2)}, u32[]{:S(2)}) %collective-permute-start.1) | collective-permute-done | bytes 393248 | tf_op jit(solution)/shard_map/ppermute | solution.py:539
  79.1 2.4 %collective-permute-start.7 = (bf16[256,768]{1,0:T(8,128)(2,1)S(1)}, bf16[256,768]{1,0:T(8,128)(2,1)S(1)}, u32[]{:S(2)}, u32[]{:S(2)}) collective-permute-start(bf16[256,768]{1,0:T(8,128)(2,1)S(1)} %collective-permute-done.1.set3_ref), channel_id=1, source_target_pairs={{0,64},{64,0},{1,65},{65,1},{2,66},{66,2},{3,67},{67,3},{4,68},{68... | collective-permute-start | bytes 1179656 | tf_op jit(solution)/shard_map/ppermute | solution.py:531
  81.5 0.7 shard_map.97
  82.2 0.0 collective-permute-done.6.set6_ref
  82.2 0.0 collective-permute-done.5.set5_ref
  82.3 0.6 collective-permute-done.7.set7_ref
  82.8 2.0 %shard_map.98 = (f32[4,8,1920]{2,1,0:T(8,128)S(1)}, f32[4,8,1920]{2,1,0:T(8,128)S(1)}, f32[8,1024]{1,0:T(8,128)S(1)}) custom-call(bf16[256,768]{1,0:T(8,128)(2,1)S(1)} %bitcast.13, f32[512,1]{1,0:T(8,128)S(1)} %get-tuple-element.37.target_ref, bf16[256,768]{1,0:T(8,128)(2,1)S(1)} %shard_map.96.set0_ref, ...), custom_call_target="tpu_custom_call" | custom-call | flops 603979776 | bytes 4194304 | tf_op jit(solution)/shard_map/pallas_call | solution.py:435
  84.9 0.5 collective-permute-start.8
  85.3 1.1 %collective-permute-done.8.got_ref = f32[4,8,1920]{2,1,0:T(8,128)S(1)} collective-permute-done((f32[4,8,1920]{2,1,0:T(8,128)S(1)}, f32[4,8,1920]{2,1,0:T(8,128)S(1)}, u32[]{:S(2)}, u32[]{:S(2)}) %collective-permute-start.8) | collective-permute-done | bytes 245792 | tf_op jit(solution)/shard_map/ppermute | solution.py:531
  86.5 2.2 %collective-permute-start.9 = (f32[8,1920]{1,0:T(8,128)S(1)}, f32[8,1920]{1,0:T(8,128)S(1)}, u32[]{:S(2)}, u32[]{:S(2)}) collective-permute-start(f32[8,1920]{1,0:T(8,128)S(1)} %get-tuple-element.45), channel_id=1, source_target_pairs={{0,128},{32,160},{128,0},{160,32},{1,129},{33,161},{129,1},{161,33... | collective-permute-start | bytes 184328 | tf_op jit(solution)/shard_map/ppermute | solution.py:535
  88.7 0.8 collective-permute-start.10
  89.5 1.7 %collective-permute-done.9.part1_ref = f32[8,1920]{1,0:T(8,128)S(1)} collective-permute-done((f32[8,1920]{1,0:T(8,128)S(1)}, f32[8,1920]{1,0:T(8,128)S(1)}, u32[]{:S(2)}, u32[]{:S(2)}) %collective-permute-start.9) | collective-permute-done | bytes 61472 | tf_op jit(solution)/shard_map/ppermute | solution.py:535
  91.2 1.8 %collective-permute-done.10.part2_ref = f32[8,1920]{1,0:T(8,128)S(1)} collective-permute-done((f32[8,1920]{1,0:T(8,128)S(1)}, f32[8,1920]{1,0:T(8,128)S(1)}, u32[]{:S(2)}, u32[]{:S(2)}) %collective-permute-start.10) | collective-permute-done | bytes 61472 | tf_op jit(solution)/shard_map/ppermute | solution.py:535
  93.0 0.0 collective-permute-done.11.part3_ref
  93.0 1.3 %shard_map.100 = (f32[1,1]{1,0:T(1,128)}, f32[8,768]{1,0:T(8,128)}, f32[8,768]{1,0:T(8,128)}) custom-call(f32[8,1920]{1,0:T(8,128)S(1)} %get-tuple-element.44.part0_ref, f32[8,1920]{1,0:T(8,128)S(1)} %collective-permute-done.9.part1_ref, f32[8,1920]{1,0:T(8,128)S(1)} %collective-permute-done.10.part2_ref, f32[8,1920]{1,0:T(8,128)S(1)} %collective-permute-done.11.part3_ref, ...), custom_call_target="tpu_custom_call" | custom-call | flops 25165824 | bytes 5242880 | tf_op jit(solution)/shard_map/pallas_call | solution.py:509
  (16 shorter events, 0.1 us)
Async XLA Ops:
  0.6 9.3 %collective-permute-start = (bf16[8,768]{1,0:T(8,128)(2,1)}, bf16[8,768]{1,0:T(8,128)(2,1)S(1)}, u32[]{:S(2)}, u32[]{:S(2)}) collective-permute-start(bf16[8,768]{1,0:T(8,128)(2,1)} %text_hbm.1), channel_id=1, source_target_pairs={{0,128},{32,160},{128,0},{160,32},{1,129},{33,161},{129,1},{161,33... | collective-permute-start | bytes 36872 | tf_op jit(solution)/shard_map/ppermute | solution.py:535
  4.3 50.3 %slice-start = ((s8[4915200]{0:T(1024)(128)(4,1)}), s8[4194304]{0:T(1024)(128)(4,1)S(1)}, s32[]{:S(2)}) async-start(s8[4915200]{0:T(1024)(128)(4,1)} %bitcast.10), calls=%async_computation.2 | async-start | bytes 8388608
  4.3 50.3 %slice-start.1 = ((s8[4915200]{0:T(1024)(128)(4,1)}), s8[720896]{0:T(1024)(128)(4,1)S(1)}, s32[]{:S(2)}) async-start(s8[4915200]{0:T(1024)(128)(4,1)} %bitcast.10), calls=%async_computation.3 | async-start | bytes 1441792
  9.9 47.2 %copy-start = (f32[8,768]{1,0:T(8,128)}, f32[8,768]{1,0:T(8,128)S(1)}, u32[]{:S(2)}) copy-start(f32[8,768]{1,0:T(8,128)S(1)} %get-tuple-element.33.hat_ref.text_hat_ref) | copy-start | bytes 73732
  57.1 0.6 copy-start.2
  57.7 21.4 %all-to-all-start.1 = ((bf16[32,8,768]{2,1,0:T(8,128)(2,1)}), bf16[32,8,768]{2,1,0:T(8,128)(2,1)S(1)}, u32[]{:S(2)}, u32[]{:S(2)}) async-start(bf16[32,8,768]{2,1,0:T(8,128)(2,1)} %get-tuple-element.35), calls=%async_computation.1 | async-start | bytes 786432 | tf_op jit(solution)/shard_map/all_to_all | solution.py:527
  64.5 9.8 %collective-permute-start.3 = (bf16[256,768]{1,0:T(8,128)(2,1)S(1)}, bf16[256,768]{1,0:T(8,128)(2,1)S(1)}, u32[]{:S(2)}, u32[]{:S(2)}) collective-permute-start(bf16[256,768]{1,0:T(8,128)(2,1)S(1)} %shard_map.96.set0_ref), channel_id=1, source_target_pairs={{0,160},{32,128},{128,32},{160,0},{1,161},{33,129},{129,33},{161,1... | collective-permute-start | bytes 1179656 | tf_op jit(solution)/shard_map/ppermute | solution.py:535
  65.4 11.9 %collective-permute-start.2 = (bf16[256,768]{1,0:T(8,128)(2,1)S(1)}, bf16[256,768]{1,0:T(8,128)(2,1)S(1)}, u32[]{:S(2)}, u32[]{:S(2)}) collective-permute-start(bf16[256,768]{1,0:T(8,128)(2,1)S(1)} %shard_map.96.set0_ref), channel_id=1, source_target_pairs={{0,32},{32,0},{128,160},{160,128},{1,33},{33,1},{129,161},{161,129... | collective-permute-start | bytes 1179656 | tf_op jit(solution)/shard_map/ppermute | solution.py:535
  66.0 13.1 %collective-permute-start.1 = (bf16[256,768]{1,0:T(8,128)(2,1)S(1)}, bf16[256,768]{1,0:T(8,128)(2,1)S(1)}, u32[]{:S(2)}, u32[]{:S(2)}) collective-permute-start(bf16[256,768]{1,0:T(8,128)(2,1)S(1)} %shard_map.96.set0_ref), channel_id=1, source_target_pairs={{0,1},{1,0},{2,3},{3,2},{4,5},{5,4},{6,7},{7,6},{8,9},{9,8},{10,11... | collective-permute-start | bytes 1179656 | tf_op jit(solution)/shard_map/ppermute | solution.py:539
  67.2 15.0 %collective-permute-start.4 = (bf16[256,768]{1,0:T(8,128)(2,1)S(1)}, bf16[256,768]{1,0:T(8,128)(2,1)S(1)}, u32[]{:S(2)}, u32[]{:S(2)}) collective-permute-start(bf16[256,768]{1,0:T(8,128)(2,1)S(1)} %shard_map.96.set0_ref), channel_id=1, source_target_pairs={{0,64},{64,0},{1,65},{65,1},{2,66},{66,2},{3,67},{67,3},{4,68},{68... | collective-permute-start | bytes 1179656 | tf_op jit(solution)/shard_map/ppermute | solution.py:531
  74.3 7.9 %collective-permute-start.6 = (bf16[256,768]{1,0:T(8,128)(2,1)S(1)}, bf16[256,768]{1,0:T(8,128)(2,1)S(1)}, u32[]{:S(2)}, u32[]{:S(2)}) collective-permute-start(bf16[256,768]{1,0:T(8,128)(2,1)S(1)} %collective-permute-done.3.set2_ref), channel_id=1, source_target_pairs={{0,64},{64,0},{1,65},{65,1},{2,66},{66,2},{3,67},{67,3},{4,68},{68... | collective-permute-start | bytes 1179656 | tf_op jit(solution)/shard_map/ppermute | solution.py:531
  77.3 4.9 %collective-permute-start.5 = (bf16[256,768]{1,0:T(8,128)(2,1)S(1)}, bf16[256,768]{1,0:T(8,128)(2,1)S(1)}, u32[]{:S(2)}, u32[]{:S(2)}) collective-permute-start(bf16[256,768]{1,0:T(8,128)(2,1)S(1)} %collective-permute-done.2.set1_ref), channel_id=1, source_target_pairs={{0,64},{64,0},{1,65},{65,1},{2,66},{66,2},{3,67},{67,3},{4,68},{68... | collective-permute-start | bytes 1179656 | tf_op jit(solution)/shard_map/ppermute | solution.py:531
  79.1 13.9 %copy-start.1 = (f32[8,768]{1,0:T(8,128)S(1)}, f32[8,768]{1,0:T(8,128)}, u32[]{:S(2)}) copy-start(f32[8,768]{1,0:T(8,128)} %copy-done) | copy-start | bytes 73732
  79.1 13.9 %copy-start.3 = (f32[8,768]{1,0:T(8,128)S(1)}, f32[8,768]{1,0:T(8,128)}, u32[]{:S(2)}) copy-start(f32[8,768]{1,0:T(8,128)} %copy-done.2) | copy-start | bytes 73732
  79.1 3.8 %collective-permute-start.7 = (bf16[256,768]{1,0:T(8,128)(2,1)S(1)}, bf16[256,768]{1,0:T(8,128)(2,1)S(1)}, u32[]{:S(2)}, u32[]{:S(2)}) collective-permute-start(bf16[256,768]{1,0:T(8,128)(2,1)S(1)} %collective-permute-done.1.set3_ref), channel_id=1, source_target_pairs={{0,64},{64,0},{1,65},{65,1},{2,66},{66,2},{3,67},{67,3},{4,68},{68... | collective-permute-start | bytes 1179656 | tf_op jit(solution)/shard_map/ppermute | solution.py:531
  84.9 1.6 %collective-permute-start.8 = (f32[4,8,1920]{2,1,0:T(8,128)S(1)}, f32[4,8,1920]{2,1,0:T(8,128)S(1)}, u32[]{:S(2)}, u32[]{:S(2)}) collective-permute-start(f32[4,8,1920]{2,1,0:T(8,128)S(1)} %get-tuple-element.43), channel_id=1, source_target_pairs={{0,64},{64,0},{1,65},{65,1},{2,66},{66,2},{3,67},{67,3},{4,68},{68... | collective-permute-start | bytes 737288 | tf_op jit(solution)/shard_map/ppermute | solution.py:531
  86.5 4.7 %collective-permute-start.9 = (f32[8,1920]{1,0:T(8,128)S(1)}, f32[8,1920]{1,0:T(8,128)S(1)}, u32[]{:S(2)}, u32[]{:S(2)}) collective-permute-start(f32[8,1920]{1,0:T(8,128)S(1)} %get-tuple-element.45), channel_id=1, source_target_pairs={{0,128},{32,160},{128,0},{160,32},{1,129},{33,161},{129,1},{161,33... | collective-permute-start | bytes 184328 | tf_op jit(solution)/shard_map/ppermute | solution.py:535
  88.7 4.3 %collective-permute-start.10 = (f32[8,1920]{1,0:T(8,128)S(1)}, f32[8,1920]{1,0:T(8,128)S(1)}, u32[]{:S(2)}, u32[]{:S(2)}) collective-permute-start(f32[8,1920]{1,0:T(8,128)S(1)} %get-tuple-element.46), channel_id=1, source_target_pairs={{0,160},{32,128},{128,32},{160,0},{1,161},{33,129},{129,33},{161,1... | collective-permute-start | bytes 184328 | tf_op jit(solution)/shard_map/ppermute | solution.py:535
  89.5 3.5 %collective-permute-start.11 = (f32[8,1920]{1,0:T(8,128)S(1)}, f32[8,1920]{1,0:T(8,128)S(1)}, u32[]{:S(2)}, u32[]{:S(2)}) collective-permute-start(f32[8,1920]{1,0:T(8,128)S(1)} %get-tuple-element.47), channel_id=1, source_target_pairs={{0,32},{32,0},{128,160},{160,128},{1,33},{33,1},{129,161},{161,129... | collective-permute-start | bytes 184328 | tf_op jit(solution)/shard_map/ppermute | solution.py:535

commit v8 on v7

--- a/solution.py
+++ b/solution.py
@@ -61,7 +61,7 @@
 
 def clip_kernel(
     video_hbm, token_hbm, pool_hbm, text_hbm, pair_hbm,
-    num_ref, slot_ref, code_ref, hat_ref, norm_ref,
+    num_ref, slot_ref, code_ref, hat_ref,
     video_ref, token_ref, pool_ref, text_ref, pair_ref, weight_scr, sems,
 ):
     small = ((pool_hbm, pool_ref), (video_hbm, video_ref), (text_hbm, text_ref), (pair_hbm, pair_ref))
@@ -85,9 +85,7 @@
     for copy in early[1:]:
         copy.wait()
     videos = video_ref[...].astype(f32)
-    hat, norm = unit_rows(text_ref[...].astype(f32))
-    hat_ref[...] = hat
-    norm_ref[...] = norm
+    hat_ref[...], _ = unit_rows(text_ref[...].astype(f32))
     early[0].wait()
     pool = pool_ref[...]
 
@@ -182,7 +180,7 @@
         in_specs=[VMEM] * 5,
         out_specs=VMEM,
         out_shape=jax.ShapeDtypeStruct((CLIPS * 8, SENT + PIECE), bf16),
-        compiler_params=pltpu.CompilerParams(vmem_limit_bytes=24 << 20),
+        compiler_params=pltpu.CompilerParams(vmem_limit_bytes=16 << 20),
         cost_estimate=pl.CostEstimate(
             flops=2 * 512 * 256 * SENT, bytes_accessed=2 << 20, transcendentals=0
         ),
@@ -200,20 +198,19 @@
     return pl.pallas_call(
         clip_kernel,
         in_specs=[pl.BlockSpec(memory_space=pltpu.HBM)] * 5,
-        out_specs=[VMEM] * 5,
+        out_specs=[VMEM] * 4,
         out_shape=[
             jax.ShapeDtypeStruct((PARTS * CLIPS, SENT), bf16),
             jax.ShapeDtypeStruct((1, PARTS * CLIPS), f32),
             jax.ShapeDtypeStruct((1, HD), f32),
             jax.ShapeDtypeStruct((8, E), f32),
-            jax.ShapeDtypeStruct((8, 1), f32),
         ],
         scratch_shapes=[pltpu.VMEM(x.shape, x.dtype) for x in args]
         + [
             pltpu.VMEM((STEPS, 128, TOKS), f32),
             pltpu.SemaphoreType.DMA((STEPS + 4,)),
         ],
-        compiler_params=pltpu.CompilerParams(vmem_limit_bytes=24 << 20),
+        compiler_params=pltpu.CompilerParams(vmem_limit_bytes=16 << 20),
         cost_estimate=pl.CostEstimate(
             flops=2 * 1024 * D * 64, bytes_accessed=8 << 20, transcendentals=1 << 17
         ),
@@ -221,7 +218,7 @@
 
 
 def embed_kernel(
-    arrived_ref, proj_ref, emb_ref, hat_ref, norm_ref, send_ref, target_ref
+    arrived_ref, proj_ref, emb_ref, hat_ref, norm_ref, send_ref
 ):
     rows = CLIPS * 8
     tails = arrived_ref[:, TAIL : TAIL + HD]
@@ -253,52 +250,59 @@
     hat_low = hat.astype(bf16)
     for k in range(32):
         send_ref[k] = hat_low
-    code = tails.astype(f32).reshape(CLIPS, 8, HD)[:, 3:4, :]
-    code = jnp.broadcast_to(code, (CLIPS, 8, HD)).reshape(rows, HD)
-    lane, own = iota((rows, HD), 1), iota((rows, HD), 0) % 8
-    code = jnp.where(lane - 72 == own, 64.0 * code, jnp.where(lane - 80 == own, code, 0.0))
-    target_ref[...] = jnp.sum(code, axis=1, keepdims=True)
 
 
 def embed(arrived, out_proj):
     return pl.pallas_call(
         embed_kernel,
         in_specs=[VMEM, VMEM],
-        out_specs=[VMEM] * 5,
+        out_specs=[VMEM] * 4,
         out_shape=[
             jax.ShapeDtypeStruct((8, E), bf16),
             jax.ShapeDtypeStruct((8, E), f32),
             jax.ShapeDtypeStruct((8, 1), f32),
             jax.ShapeDtypeStruct((32, 8, E), bf16),
-            jax.ShapeDtypeStruct((SET, 1), f32),
-        ],
-        compiler_params=pltpu.CompilerParams(vmem_limit_bytes=24 << 20),
+        ],
+        compiler_params=pltpu.CompilerParams(vmem_limit_bytes=16 << 20),
         cost_estimate=pl.CostEstimate(
             flops=2 * 24 * D * E, bytes_accessed=6 << 20, transcendentals=0
         ),
     )(arrived, out_proj)
 
 
-def text_kernel(arrived_ref, text_ref):
+def text_kernel(arrived_ref, hat_ref, norm_ref, text_ref, target_ref, hat_out, norm_out):
+    hat_out[...] = hat_ref[...]
+    norm_out[...] = norm_ref[...]
     halves = arrived_ref[:, SENT : SENT + PIECE]
     row, col = iota((TILE, CLIPS * 8), 0), iota((TILE, CLIPS * 8), 1)
     for part in range(2):
         pick = row // 4 * 8 + part * 4 + row % 4 == col
         texts = dot(jnp.where(pick, 1.0, 0.0).astype(bf16), halves)
         text_ref[:, part * PIECE : (part + 1) * PIECE] = texts.astype(bf16)
-
-
-def text_piece(arrived):
+    rows = CLIPS * 8
+    code = arrived_ref[:, TAIL : TAIL + HD].astype(f32).reshape(CLIPS, 8, HD)[:, 3:4, :]
+    code = jnp.broadcast_to(code, (CLIPS, 8, HD)).reshape(rows, HD)
+    lane, own = iota((rows, HD), 1), iota((rows, HD), 0) % 8
+    code = jnp.where(lane - 72 == own, 64.0 * code, jnp.where(lane - 80 == own, code, 0.0))
+    target_ref[...] = jnp.sum(code, axis=1, keepdims=True)
+
+
+def text_piece(*args):
     return pl.pallas_call(
         text_kernel,
-        in_specs=[VMEM],
-        out_specs=VMEM,
-        out_shape=jax.ShapeDtypeStruct((TILE, E), bf16),
+        in_specs=[VMEM] * 3,
+        out_specs=[VMEM] * 4,
+        out_shape=[
+            jax.ShapeDtypeStruct((TILE, E), bf16),
+            jax.ShapeDtypeStruct((SET, 1), f32),
+            jax.ShapeDtypeStruct((8, E), f32),
+            jax.ShapeDtypeStruct((8, 1), f32),
+        ],
         compiler_params=pltpu.CompilerParams(vmem_limit_bytes=16 << 20),
         cost_estimate=pl.CostEstimate(
             flops=4 * 256 * 512 * PIECE, bytes_accessed=1 << 20, transcendentals=0
         ),
-    )(arrived)
+    )(*args)
 
 
 def position():
@@ -348,10 +352,12 @@
 
 
 def first_kernel(
-    video_ref, target_ref, set0_ref, set1_ref, set2_ref, set3_ref,
-    own_ref, cols_ref, sums_ref, positive_ref, tile_scr,
+    video_ref, target_ref, set0_ref, set1_ref, set2_ref, set3_ref, hat_ref, norm_ref,
+    own_ref, cols_ref, sums_ref, positive_ref, hat_out, norm_out, tile_scr,
 ):
     xh, c, xl, spot = position()
+    hat_out[...] = hat_ref[...]
+    norm_out[...] = norm_ref[...]
     cols_ref[...] = jnp.zeros_like(cols_ref)
     sums_ref[...], positive_ref[...] = score(
         video_ref[...], plane_rows(target_ref, xl), (set0_ref, set1_ref, set2_ref, set3_ref),
@@ -382,11 +388,16 @@
         )
         return ((group * 32 + spot) * 8 + slot % 8).astype(f32)
 
-    column = near_texts(iota((64, 1), 0))
-    near = jnp.zeros((64, E), f32)
-    for ref, tile in zip(pieces, tiles):
-        pick = column == texts_of(tile, iota((1, TILE), 1))
-        near += dot(jnp.where(pick, 1.0, 0.0).astype(bf16), ref[...])
+    blocks = [
+        ref[pl.ds(pl.multiple_of(half * 128 + spot // 4 * 16, 16), 16), :]
+        for ref in pieces
+        for half in range(2)
+    ]
+    col = iota((1, TILE), 1)
+    tile = sum(jnp.where(col // 32 == k, tiles[k], 0) for k in range(8))
+    held = texts_of(tile, col % 32 // 16 * 128 + spot // 4 * 16 + col % 16)
+    pick = near_texts(iota((64, 1), 0)) == held
+    near = dot(jnp.where(pick, 1.0, 0.0).astype(bf16), jnp.concatenate(blocks, axis=0))
     near = jnp.exp(SCALE * dot(videos, near.astype(bf16), NT))
     rowsum = jnp.sum(sums, axis=1, keepdims=True)
     total = jnp.sum(jnp.log(rowsum), axis=0, keepdims=True) - 2.0 * jnp.sum(
@@ -415,16 +426,18 @@
 def first_logits(*args):
     return pl.pallas_call(
         first_kernel,
-        in_specs=[VMEM] * 6,
-        out_specs=[VMEM] * 4,
+        in_specs=[VMEM] * 8,
+        out_specs=[VMEM] * 6,
         out_shape=[
             jax.ShapeDtypeStruct((8, 2 * SET), f32),
             jax.ShapeDtypeStruct((8, TILE), f32),
             jax.ShapeDtypeStruct((PLANE_ROWS, 128), f32),
             jax.ShapeDtypeStruct((1, TILE), f32),
+            jax.ShapeDtypeStruct((8, E), f32),
+            jax.ShapeDtypeStruct((8, 1), f32),
         ],
         scratch_shapes=[pltpu.VMEM((PLANE_ROWS, TILE), f32)],
-        compiler_params=pltpu.CompilerParams(vmem_limit_bytes=24 << 20),
+        compiler_params=pltpu.CompilerParams(vmem_limit_bytes=16 << 20),
         cost_estimate=pl.CostEstimate(
             flops=2 * PLANE_ROWS * 1024 * E, bytes_accessed=2 << 20, transcendentals=1 << 18
         ),
@@ -442,7 +455,7 @@
             jax.ShapeDtypeStruct((8, 2 * SET), f32),
         ],
         scratch_shapes=[pltpu.VMEM((PLANE_ROWS, TILE), f32), pltpu.VMEM((8, TILE), f32)],
-        compiler_params=pltpu.CompilerParams(vmem_limit_bytes=24 << 20),
+        compiler_params=pltpu.CompilerParams(vmem_limit_bytes=16 << 20),
         cost_estimate=pl.CostEstimate(
             flops=2 * PLANE_ROWS * 1536 * E, bytes_accessed=4 << 20, transcendentals=1 << 18
         ),
@@ -468,7 +481,7 @@
 def grad_kernel(
     part0_ref, part1_ref, part2_ref, part3_ref, own_ref, last_ref, target_ref,
     set0_ref, set1_ref, set2_ref, set3_ref, set4_ref, set5_ref, set6_ref, set7_ref,
-    video_hat_ref, video_norm_ref, text_hat_ref, text_norm_ref, loss_ref, video_grad_ref, text_grad_ref, col_scr,
+    video_hat_ref, video_norm_ref, text_ref, loss_ref, video_grad_ref, text_grad_ref, col_scr,
 ):
     xh, c, xl, spot = position()
     got = (part0_ref[...] + part1_ref[...]) + (part2_ref[...] + part3_ref[...])
@@ -489,7 +502,7 @@
         jnp.where(row == n, pair[n % 2][n // 2 : n // 2 + 1], 0.0) for n in range(8)
     )
     text_dir = SCALE * (got[:, 0:E] + got[:, E : 2 * E] / mine)
-    text_grad_ref[...] = project(text_dir, text_hat_ref[...], text_norm_ref[...])
+    text_grad_ref[...] = project(text_dir, *unit_rows(text_ref[...].astype(f32)))
 
     rows = jnp.concatenate([own_ref[...], last_ref[...]], axis=1)
     rowsum = jnp.sum(rows, axis=1, keepdims=True)
@@ -508,7 +521,7 @@
 def gradients(*args):
     return pl.pallas_call(
         grad_kernel,
-        in_specs=[VMEM] * 19,
+        in_specs=[VMEM] * 18,
         out_specs=[VMEM] * 3,
         out_shape=[
             jax.ShapeDtypeStruct((1, 1), f32),
@@ -516,7 +529,7 @@
             jax.ShapeDtypeStruct((8, E), f32),
         ],
         scratch_shapes=[pltpu.VMEM((8, TILE), f32)],
-        compiler_params=pltpu.CompilerParams(vmem_limit_bytes=32 << 20),
+        compiler_params=pltpu.CompilerParams(vmem_limit_bytes=12 << 20),
         cost_estimate=pl.CostEstimate(
             flops=2 * 8 * 2048 * E, bytes_accessed=5 << 20, transcendentals=2048
         ),
@@ -541,25 +554,27 @@
 
 def body(clip_tokens, clip_video, pool_vectors, out_proj, text_embed, pair_text):
     far_text = along(text_embed, 2)
-    *sums, text_hat, text_norm = clip_sums(
+    *sums, text_hat = clip_sums(
         clip_tokens, clip_video, pool_vectors, text_embed, pair_text
     )
     outgoing = pack(*sums, text_hat, far_text)
     arrived = exchange(outgoing.reshape(CLIPS, 8, SENT + PIECE), ROW)
     arrived = arrived.reshape(CLIPS * 8, SENT + PIECE)
-    texts = text_piece(arrived)
+    video_embed, video_hat, video_norm, send = embed(arrived, out_proj)
+    texts, target, video_hat, video_norm = text_piece(arrived, video_hat, video_norm)
     moved = [turn_y(texts), along(texts, 3), along(texts, 1)]
-    video_embed, video_hat, video_norm, send, target = embed(arrived, out_proj)
     videos, moved[0] = lax.optimization_barrier((exchange(send, PLANE), moved[0]))
     videos = videos.reshape(PLANE_ROWS, E)
     mine = (texts, moved[2], moved[1], moved[0])
     theirs = tuple(swap(x) for x in mine)
-    own, cols, sums, positive = first_logits(videos, target, *mine)
+    own, cols, sums, positive, video_hat, video_norm = first_logits(
+        videos, target, *mine, video_hat, video_norm
+    )
     keep, send, last = second_logits(videos, target, *mine, *theirs, cols, sums, positive)
     parts = add_parts(keep, swap(send))
     parts = [parts[0]] + [along(parts[step], step) for step in (2, 3, 1)]
     loss, video_grad, text_grad = gradients(
-        *parts, own, last, target, *mine, *theirs, video_hat, video_norm, text_hat, text_norm
+        *parts, own, last, target, *mine, *theirs, video_hat, video_norm, text_embed
     )
     return video_embed, video_grad, text_grad, loss.reshape(())
 

time: 94.6 us -> 93.9 us (level)
  transfers between devices with their start and end apart: 13 -> 13, of which waited for: 6 -> 5; matrix products, arithmetic and copies ran while one was open for 0% -> 0% of each run, Pallas kernels for 7% -> 7%
where the time goes in v8:
time: 93.9 us; the launch traced here: 93.6 us
  blocking collectives  43.8 us (47%)
  starting transfers between devices  24.7 us (26%)
  Pallas kernels  12.9 us (14%)
  waiting for transfers between devices  10.1 us (11%)
  local copies, waits for them, and re-layouts  1.35 us (1%)
    all_to_all x1, blocking collectives, exchange(): return lax.all_to_all(x, axes, 0, 0, tiled=True)  43.8 us
    ppermute x5, starting transfers between devices, swap(): return lax.ppermute(x, 'c', [(0, 1), (1, 0)])  8.85 us
    ppermute x6, starting transfers between devices, along(): return lax.ppermute(x, ('xh', 'xl'), [(k, k ^ step) for k in range(4)])  8.07 us
    ppermute x6, waiting for transfers between devices, along(): return lax.ppermute(x, ('xh', 'xl'), [(k, k ^ step) for k in range(4)])  7.23 us
    all_to_all x1, starting transfers between devices, exchange(): return lax.all_to_all(x, axes, 0, 0, tiled=True)  6.5 us
    pallas_call x1, Pallas kernels, clip_sums(): pl.pallas_call(clip_kernel, in_specs=[pl.BlockSpec(memory_space=pltpu.HBM...  5.59 us
    pallas_call x1, Pallas kernels, embed(): pl.pallas_call(embed_kernel, in_specs=[VMEM, VMEM], out_specs=[VMEM] * 4,...  2.49 us
  transfers between devices with their start and end apart: 13, of which 5 were waited for; matrix products, arithmetic and copies ran while one was open for 0% of the time, Pallas kernels for 7%

profile of v8, /device:TPU:1, one launch (start us, length us, event | category | flops | bytes accessed | tf_op | source)
XLA Modules:
  0.0 93.6 jit_solution(3214753584074005234)
XLA Ops:
  0.6 3.7 %collective-permute-start = (bf16[8,768]{1,0:T(8,128)(2,1)}, bf16[8,768]{1,0:T(8,128)(2,1)S(1)}, u32[]{:S(2)}, u32[]{:S(2)}) collective-permute-start(bf16[8,768]{1,0:T(8,128)(2,1)} %text_ref.1), channel_id=1, source_target_pairs={{0,128},{32,160},{128,0},{160,32},{1,129},{33,161},{129,1},{161,33... | collective-permute-start | bytes 36872 | tf_op jit(solution)/shard_map/ppermute | solution.py:548
  4.3 5.6 %shard_map.93 = (bf16[256,896]{1,0:T(8,128)(2,1)S(1)}, f32[1,256]{1,0:T(1,128)S(1)}, f32[1,128]{1,0:T(1,128)S(1)}, f32[8,768]{1,0:T(8,128)S(1)}) custom-call(s32[1,64]{1,0:T(1,128)} %bitcast.15, bf16[1024,3200]{1,0:T(8,128)(2,1)} %bitcast.14, bf16[25,3200]{1,0:T(8,128)(2,1)} %pool_hbm.1, bf16[8,768]{1,0:T(8,128)(2,1)} %text_ref.1, s32[1,8]{1,0:T(1,128)} %bitcast.16), custom_call_target="tpu_custom_call" | custom-call | flops 419430400 | bytes 8388608 | tf_op jit(solution)/shard_map/pallas_call | solution.py:198
  9.9 0.8 shard_map.94
  10.7 43.8 %all_to_all.10 = bf16[64,8,1280]{2,1,0:T(8,128)(2,1)S(1)} all-to-all(bf16[64,8,1280]{2,1,0:T(8,128)(2,1)S(1)} %bitcast.9), channel_id=1, replica_groups=mesh['xh'=2,'c'=2,'xl'=2,'z'=8,'y'=4] {'xl','z','y'}, dimensions={0} | all-to-all | bytes 2621440 | tf_op jit(solution)/shard_map/all_to_all | solution.py:540
  54.6 2.5 %shard_map.95 = (bf16[8,768]{1,0:T(8,128)(2,1)}, f32[8,768]{1,0:T(8,128)S(1)}, f32[8,1]{1,0:T(8,128)S(1)}, bf16[32,8,768]{2,1,0:T(8,128)(2,1)}) custom-call(bf16[512,1280]{1,0:T(8,128)(2,1)S(1)} %bitcast.7, bf16[3200,768]{1,0:T(8,128)(2,1)S(1)} %bitcast.11), custom_call_target="tpu_custom_call" | custom-call | flops 117964800 | bytes 6291456 | tf_op jit(solution)/shard_map/pallas_call | solution.py:256
  57.1 6.5 %all-to-all-start.1 = ((bf16[32,8,768]{2,1,0:T(8,128)(2,1)}), bf16[32,8,768]{2,1,0:T(8,128)(2,1)S(1)}, u32[]{:S(2)}, u32[]{:S(2)}) async-start(bf16[32,8,768]{2,1,0:T(8,128)(2,1)} %get-tuple-element.39), calls=%async_computation.1 | async-start | bytes 786432 | tf_op jit(solution)/shard_map/all_to_all | solution.py:540
  63.6 0.5 shard_map.96
  64.1 0.0 copy-start.1
  64.1 0.6 copy-done.1
  64.7 0.8 collective-permute-start.3
  65.5 0.6 collective-permute-start.2
  66.1 1.2 %collective-permute-start.1 = (bf16[256,768]{1,0:T(8,128)(2,1)S(1)}, bf16[256,768]{1,0:T(8,128)(2,1)S(1)}, u32[]{:S(2)}, u32[]{:S(2)}) collective-permute-start(bf16[256,768]{1,0:T(8,128)(2,1)S(1)} %get-tuple-element.42.set0_ref), channel_id=1, source_target_pairs={{0,1},{1,0},{2,3},{3,2},{4,5},{5,4},{6,7},{7,6},{8,9},{9,8},{10,11... | collective-permute-start | bytes 1179656 | tf_op jit(solution)/shard_map/ppermute | solution.py:552
  67.3 3.2 %collective-permute-start.4 = (bf16[256,768]{1,0:T(8,128)(2,1)S(1)}, bf16[256,768]{1,0:T(8,128)(2,1)S(1)}, u32[]{:S(2)}, u32[]{:S(2)}) collective-permute-start(bf16[256,768]{1,0:T(8,128)(2,1)S(1)} %get-tuple-element.42.set0_ref), channel_id=1, source_target_pairs={{0,64},{64,0},{1,65},{65,1},{2,66},{66,2},{3,67},{67,3},{4,68},{68... | collective-permute-start | bytes 1179656 | tf_op jit(solution)/shard_map/ppermute | solution.py:544
  70.6 3.9 %collective-permute-done.3.set2_ref = bf16[256,768]{1,0:T(8,128)(2,1)S(1)} collective-permute-done((bf16[256,768]{1,0:T(8,128)(2,1)S(1)}, bf16[256,768]{1,0:T(8,128)(2,1)S(1)}, u32[]{:S(2)}, u32[]{:S(2)}) %collective-permute-start.3) | collective-permute-done | bytes 393248 | tf_op jit(solution)/shard_map/ppermute | solution.py:548
  74.4 3.0 %collective-permute-start.6 = (bf16[256,768]{1,0:T(8,128)(2,1)S(1)}, bf16[256,768]{1,0:T(8,128)(2,1)S(1)}, u32[]{:S(2)}, u32[]{:S(2)}) collective-permute-start(bf16[256,768]{1,0:T(8,128)(2,1)S(1)} %collective-permute-done.3.set2_ref), channel_id=1, source_target_pairs={{0,64},{64,0},{1,65},{65,1},{2,66},{66,2},{3,67},{67,3},{4,68},{68... | collective-permute-start | bytes 1179656 | tf_op jit(solution)/shard_map/ppermute | solution.py:544
  77.4 0.0 collective-permute-done.2.set1_ref
  77.4 0.0 collective-permute-start.5
  77.4 1.6 %collective-permute-done.1.set3_ref = bf16[256,768]{1,0:T(8,128)(2,1)S(1)} collective-permute-done((bf16[256,768]{1,0:T(8,128)(2,1)S(1)}, bf16[256,768]{1,0:T(8,128)(2,1)S(1)}, u32[]{:S(2)}, u32[]{:S(2)}) %collective-permute-start.1) | collective-permute-done | bytes 393248 | tf_op jit(solution)/shard_map/ppermute | solution.py:552
  79.0 0.0 all-to-all-done.1
  79.0 2.1 %collective-permute-start.7 = (bf16[256,768]{1,0:T(8,128)(2,1)S(1)}, bf16[256,768]{1,0:T(8,128)(2,1)S(1)}, u32[]{:S(2)}, u32[]{:S(2)}) collective-permute-start(bf16[256,768]{1,0:T(8,128)(2,1)S(1)} %collective-permute-done.1.set3_ref), channel_id=1, source_target_pairs={{0,64},{64,0},{1,65},{65,1},{2,66},{66,2},{3,67},{67,3},{4,68},{68... | collective-permute-start | bytes 1179656 | tf_op jit(solution)/shard_map/ppermute | solution.py:544
  81.1 0.7 copy-done.2
  81.8 0.7 shard_map.97
  82.6 0.0 collective-permute-done.6.set6_ref
  82.6 0.0 collective-permute-done.5.set5_ref
  82.6 1.5 %shard_map.98 = (f32[4,8,1920]{2,1,0:T(8,128)S(1)}, f32[4,8,1920]{2,1,0:T(8,128)S(1)}, f32[8,1024]{1,0:T(8,128)S(1)}) custom-call(bf16[256,768]{1,0:T(8,128)(2,1)S(1)} %bitcast.13, f32[512,1]{1,0:T(8,128)S(1)} %get-tuple-element.44.target_ref, bf16[256,768]{1,0:T(8,128)(2,1)S(1)} %get-tuple-element.42.set0_ref, ...), custom_call_target="tpu_custom_call" | custom-call | flops 603979776 | bytes 4194304 | tf_op jit(solution)/shard_map/pallas_call | solution.py:448
  84.1 0.5 collective-permute-start.8
  84.6 1.3 %collective-permute-done.8.got_ref = f32[4,8,1920]{2,1,0:T(8,128)S(1)} collective-permute-done((f32[4,8,1920]{2,1,0:T(8,128)S(1)}, f32[4,8,1920]{2,1,0:T(8,128)S(1)}, u32[]{:S(2)}, u32[]{:S(2)}) %collective-permute-start.8) | collective-permute-done | bytes 245792 | tf_op jit(solution)/shard_map/ppermute | solution.py:544
  85.9 2.1 %collective-permute-start.9 = (f32[8,1920]{1,0:T(8,128)S(1)}, f32[8,1920]{1,0:T(8,128)S(1)}, u32[]{:S(2)}, u32[]{:S(2)}) collective-permute-start(f32[8,1920]{1,0:T(8,128)S(1)} %get-tuple-element.54), channel_id=1, source_target_pairs={{0,128},{32,160},{128,0},{160,32},{1,129},{33,161},{129,1},{161,33... | collective-permute-start | bytes 184328 | tf_op jit(solution)/shard_map/ppermute | solution.py:548
  88.0 0.9 collective-permute-start.10
  88.9 1.6 %collective-permute-done.9.part1_ref = f32[8,1920]{1,0:T(8,128)S(1)} collective-permute-done((f32[8,1920]{1,0:T(8,128)S(1)}, f32[8,1920]{1,0:T(8,128)S(1)}, u32[]{:S(2)}, u32[]{:S(2)}) %collective-permute-start.9) | collective-permute-done | bytes 61472 | tf_op jit(solution)/shard_map/ppermute | solution.py:548
  90.6 1.7 %collective-permute-done.10.part2_ref = f32[8,1920]{1,0:T(8,128)S(1)} collective-permute-done((f32[8,1920]{1,0:T(8,128)S(1)}, f32[8,1920]{1,0:T(8,128)S(1)}, u32[]{:S(2)}, u32[]{:S(2)}) %collective-permute-start.10) | collective-permute-done | bytes 61472 | tf_op jit(solution)/shard_map/ppermute | solution.py:548
  92.3 1.3 %shard_map.100 = (f32[1,1]{1,0:T(1,128)}, f32[8,768]{1,0:T(8,128)}, f32[8,768]{1,0:T(8,128)}) custom-call(f32[8,1920]{1,0:T(8,128)S(1)} %get-tuple-element.53.part0_ref, f32[8,1920]{1,0:T(8,128)S(1)} %collective-permute-done.9.part1_ref, f32[8,1920]{1,0:T(8,128)S(1)} %collective-permute-done.10.part2_ref, f32[8,1920]{1,0:T(8,128)S(1)} %collective-permute-done.11.part3_ref, ...), custom_call_target="tpu_custom_call" | custom-call | flops 25165824 | bytes 5242880 | tf_op jit(solution)/shard_map/pallas_call | solution.py:522
  (14 shorter events, 0.1 us)
Async XLA Ops:
  0.6 9.3 %collective-permute-start = (bf16[8,768]{1,0:T(8,128)(2,1)}, bf16[8,768]{1,0:T(8,128)(2,1)S(1)}, u32[]{:S(2)}, u32[]{:S(2)}) collective-permute-start(bf16[8,768]{1,0:T(8,128)(2,1)} %text_ref.1), channel_id=1, source_target_pairs={{0,128},{32,160},{128,0},{160,32},{1,129},{33,161},{129,1},{161,33... | collective-permute-start | bytes 36872 | tf_op jit(solution)/shard_map/ppermute | solution.py:548
  4.3 50.3 %slice-start = ((s8[4915200]{0:T(1024)(128)(4,1)}), s8[4194304]{0:T(1024)(128)(4,1)S(1)}, s32[]{:S(2)}) async-start(s8[4915200]{0:T(1024)(128)(4,1)} %bitcast.10), calls=%async_computation.2 | async-start | bytes 8388608
  4.3 50.3 %slice-start.1 = ((s8[4915200]{0:T(1024)(128)(4,1)}), s8[720896]{0:T(1024)(128)(4,1)S(1)}, s32[]{:S(2)}) async-start(s8[4915200]{0:T(1024)(128)(4,1)} %bitcast.10), calls=%async_computation.3 | async-start | bytes 1441792
  57.1 35.2 %copy-start = (bf16[8,768]{1,0:T(8,128)(2,1)S(1)}, bf16[8,768]{1,0:T(8,128)(2,1)}, u32[]{:S(2)}) copy-start(bf16[8,768]{1,0:T(8,128)(2,1)} %text_ref.1) | copy-start | bytes 36868
  57.1 21.9 %all-to-all-start.1 = ((bf16[32,8,768]{2,1,0:T(8,128)(2,1)}), bf16[32,8,768]{2,1,0:T(8,128)(2,1)S(1)}, u32[]{:S(2)}, u32[]{:S(2)}) async-start(bf16[32,8,768]{2,1,0:T(8,128)(2,1)} %get-tuple-element.39), calls=%async_computation.1 | async-start | bytes 786432 | tf_op jit(solution)/shard_map/all_to_all | solution.py:540
  64.1 0.6 copy-start.1
  64.7 9.7 %collective-permute-start.3 = (bf16[256,768]{1,0:T(8,128)(2,1)S(1)}, bf16[256,768]{1,0:T(8,128)(2,1)S(1)}, u32[]{:S(2)}, u32[]{:S(2)}) collective-permute-start(bf16[256,768]{1,0:T(8,128)(2,1)S(1)} %get-tuple-element.42.set0_ref), channel_id=1, source_target_pairs={{0,160},{32,128},{128,32},{160,0},{1,161},{33,129},{129,33},{161,1... | collective-permute-start | bytes 1179656 | tf_op jit(solution)/shard_map/ppermute | solution.py:548
  65.5 11.9 %collective-permute-start.2 = (bf16[256,768]{1,0:T(8,128)(2,1)S(1)}, bf16[256,768]{1,0:T(8,128)(2,1)S(1)}, u32[]{:S(2)}, u32[]{:S(2)}) collective-permute-start(bf16[256,768]{1,0:T(8,128)(2,1)S(1)} %get-tuple-element.42.set0_ref), channel_id=1, source_target_pairs={{0,32},{32,0},{128,160},{160,128},{1,33},{33,1},{129,161},{161,129... | collective-permute-start | bytes 1179656 | tf_op jit(solution)/shard_map/ppermute | solution.py:548
  66.1 12.9 %collective-permute-start.1 = (bf16[256,768]{1,0:T(8,128)(2,1)S(1)}, bf16[256,768]{1,0:T(8,128)(2,1)S(1)}, u32[]{:S(2)}, u32[]{:S(2)}) collective-permute-start(bf16[256,768]{1,0:T(8,128)(2,1)S(1)} %get-tuple-element.42.set0_ref), channel_id=1, source_target_pairs={{0,1},{1,0},{2,3},{3,2},{4,5},{5,4},{6,7},{7,6},{8,9},{9,8},{10,11... | collective-permute-start | bytes 1179656 | tf_op jit(solution)/shard_map/ppermute | solution.py:552
  67.3 15.2 %collective-permute-start.4 = (bf16[256,768]{1,0:T(8,128)(2,1)S(1)}, bf16[256,768]{1,0:T(8,128)(2,1)S(1)}, u32[]{:S(2)}, u32[]{:S(2)}) collective-permute-start(bf16[256,768]{1,0:T(8,128)(2,1)S(1)} %get-tuple-element.42.set0_ref), channel_id=1, source_target_pairs={{0,64},{64,0},{1,65},{65,1},{2,66},{66,2},{3,67},{67,3},{4,68},{68... | collective-permute-start | bytes 1179656 | tf_op jit(solution)/shard_map/ppermute | solution.py:544
  74.4 8.2 %collective-permute-start.6 = (bf16[256,768]{1,0:T(8,128)(2,1)S(1)}, bf16[256,768]{1,0:T(8,128)(2,1)S(1)}, u32[]{:S(2)}, u32[]{:S(2)}) collective-permute-start(bf16[256,768]{1,0:T(8,128)(2,1)S(1)} %collective-permute-done.3.set2_ref), channel_id=1, source_target_pairs={{0,64},{64,0},{1,65},{65,1},{2,66},{66,2},{3,67},{67,3},{4,68},{68... | collective-permute-start | bytes 1179656 | tf_op jit(solution)/shard_map/ppermute | solution.py:544
  77.4 5.1 %collective-permute-start.5 = (bf16[256,768]{1,0:T(8,128)(2,1)S(1)}, bf16[256,768]{1,0:T(8,128)(2,1)S(1)}, u32[]{:S(2)}, u32[]{:S(2)}) collective-permute-start(bf16[256,768]{1,0:T(8,128)(2,1)S(1)} %collective-permute-done.2.set1_ref), channel_id=1, source_target_pairs={{0,64},{64,0},{1,65},{65,1},{2,66},{66,2},{3,67},{67,3},{4,68},{68... | collective-permute-start | bytes 1179656 | tf_op jit(solution)/shard_map/ppermute | solution.py:544
  79.0 3.6 %collective-permute-start.7 = (bf16[256,768]{1,0:T(8,128)(2,1)S(1)}, bf16[256,768]{1,0:T(8,128)(2,1)S(1)}, u32[]{:S(2)}, u32[]{:S(2)}) collective-permute-start(bf16[256,768]{1,0:T(8,128)(2,1)S(1)} %collective-permute-done.1.set3_ref), channel_id=1, source_target_pairs={{0,64},{64,0},{1,65},{65,1},{2,66},{66,2},{3,67},{67,3},{4,68},{68... | collective-permute-start | bytes 1179656 | tf_op jit(solution)/shard_map/ppermute | solution.py:544
  81.1 0.7 copy-start.2
  84.1 1.8 %collective-permute-start.8 = (f32[4,8,1920]{2,1,0:T(8,128)S(1)}, f32[4,8,1920]{2,1,0:T(8,128)S(1)}, u32[]{:S(2)}, u32[]{:S(2)}) collective-permute-start(f32[4,8,1920]{2,1,0:T(8,128)S(1)} %get-tuple-element.52), channel_id=1, source_target_pairs={{0,64},{64,0},{1,65},{65,1},{2,66},{66,2},{3,67},{67,3},{4,68},{68... | collective-permute-start | bytes 737288 | tf_op jit(solution)/shard_map/ppermute | solution.py:544
  85.9 4.7 %collective-permute-start.9 = (f32[8,1920]{1,0:T(8,128)S(1)}, f32[8,1920]{1,0:T(8,128)S(1)}, u32[]{:S(2)}, u32[]{:S(2)}) collective-permute-start(f32[8,1920]{1,0:T(8,128)S(1)} %get-tuple-element.54), channel_id=1, source_target_pairs={{0,128},{32,160},{128,0},{160,32},{1,129},{33,161},{129,1},{161,33... | collective-permute-start | bytes 184328 | tf_op jit(solution)/shard_map/ppermute | solution.py:548
  88.0 4.3 %collective-permute-start.10 = (f32[8,1920]{1,0:T(8,128)S(1)}, f32[8,1920]{1,0:T(8,128)S(1)}, u32[]{:S(2)}, u32[]{:S(2)}) collective-permute-start(f32[8,1920]{1,0:T(8,128)S(1)} %get-tuple-element.55), channel_id=1, source_target_pairs={{0,160},{32,128},{128,32},{160,0},{1,161},{33,129},{129,33},{161,1... | collective-permute-start | bytes 184328 | tf_op jit(solution)/shard_map/ppermute | solution.py:548
  88.9 3.4 %collective-permute-start.11 = (f32[8,1920]{1,0:T(8,128)S(1)}, f32[8,1920]{1,0:T(8,128)S(1)}, u32[]{:S(2)}, u32[]{:S(2)}) collective-permute-start(f32[8,1920]{1,0:T(8,128)S(1)} %get-tuple-element.56), channel_id=1, source_target_pairs={{0,32},{32,0},{128,160},{160,128},{1,33},{33,1},{129,161},{161,129... | collective-permute-start | bytes 184328 | tf_op jit(solution)/shard_map/ppermute | solution.py:548

commit v9 on v8

--- a/solution.py
+++ b/solution.py
@@ -351,90 +351,118 @@
     return target_ref[pl.ds(pl.multiple_of(xl * PLANE_ROWS, PLANE_ROWS), PLANE_ROWS), :]
 
 
-def first_kernel(
-    video_ref, target_ref, set0_ref, set1_ref, set2_ref, set3_ref, hat_ref, norm_ref,
-    own_ref, cols_ref, sums_ref, positive_ref, hat_out, norm_out, tile_scr,
-):
-    xh, c, xl, spot = position()
-    hat_out[...] = hat_ref[...]
-    norm_out[...] = norm_ref[...]
-    cols_ref[...] = jnp.zeros_like(cols_ref)
-    sums_ref[...], positive_ref[...] = score(
-        video_ref[...], plane_rows(target_ref, xl), (set0_ref, set1_ref, set2_ref, set3_ref),
-        [tile_of(xh, c, xl, spot, k) for k in range(4)], own_ref, tile_scr, cols_ref,
-        jnp.zeros((PLANE_ROWS, 128), f32), jnp.zeros((1, TILE), f32), pl.multiple_of(spot * 8, 8),
-    )
-
-
-def second_kernel(
-    video_ref, target_ref, set0_ref, set1_ref, set2_ref, set3_ref, set4_ref, set5_ref, set6_ref,
-    set7_ref, cols_ref, sums_ref, positive_ref,
-    keep_ref, send_ref, own_ref, tile_scr, col_scr,
-):
-    xh, c, xl, spot = position()
-    target = plane_rows(target_ref, xl)
-    videos = video_ref[...]
-    pieces = (set0_ref, set1_ref, set2_ref, set3_ref, set4_ref, set5_ref, set6_ref, set7_ref)
-    tiles = [tile_of(xh, c, xl, spot, k) for k in range(8)]
-    col_scr[...] = cols_ref[...]
-    sums, positive = score(
-        videos, target, pieces[4:8], tiles[4:8], own_ref, tile_scr, col_scr,
-        sums_ref[...], positive_ref[...], pl.multiple_of(spot * 8, 8),
-    )
-
-    def near_texts(slot):
-        group = sum(
-            jnp.where(slot // 8 == n, row_of(xh, c, n // 2) * 2 + n % 2, 0) for n in range(8)
-        )
-        return ((group * 32 + spot) * 8 + slot % 8).astype(f32)
-
+def near_texts(slot, flip):
+    xh, c, _, spot = position()
+    group = sum(
+        jnp.where(slot // 8 == n, row_of(xh, c, n // 2 * 2 + flip) * 2 + n % 2, 0)
+        for n in range(4)
+    )
+    return ((group * 32 + spot) * 8 + slot % 8).astype(f32)
+
+
+def near_exps(videos, pieces, tiles, flip):
+    spot = position()[3]
     blocks = [
         ref[pl.ds(pl.multiple_of(half * 128 + spot // 4 * 16, 16), 16), :]
         for ref in pieces
         for half in range(2)
     ]
-    col = iota((1, TILE), 1)
-    tile = sum(jnp.where(col // 32 == k, tiles[k], 0) for k in range(8))
+    col = iota((1, 128), 1)
+    tile = sum(jnp.where(col // 32 == k, tiles[k], 0) for k in range(4))
     held = texts_of(tile, col % 32 // 16 * 128 + spot // 4 * 16 + col % 16)
-    pick = near_texts(iota((64, 1), 0)) == held
+    pick = near_texts(iota((32, 1), 0), flip) == held
     near = dot(jnp.where(pick, 1.0, 0.0).astype(bf16), jnp.concatenate(blocks, axis=0))
-    near = jnp.exp(SCALE * dot(videos, near.astype(bf16), NT))
-    rowsum = jnp.sum(sums, axis=1, keepdims=True)
-    total = jnp.sum(jnp.log(rowsum), axis=0, keepdims=True) - 2.0 * jnp.sum(
-        positive, axis=1, keepdims=True
-    )
-    text = near_texts(iota((1, 64), 1))
-    first = near / rowsum - jnp.where(target == text, 2.0, 0.0)
+    return jnp.exp(SCALE * dot(videos, near.astype(bf16), NT))
+
+
+def near_sums(near, rowsum, target, videos, flip, cols, total, out_ref):
+    first = near / rowsum - jnp.where(target == near_texts(iota((1, 32), 1), flip), 2.0, 0.0)
     first_hi = first.astype(bf16).astype(f32)
     near_hi = near.astype(bf16).astype(f32)
     terms = jnp.concatenate([first_hi, first - first_hi, near_hi, near - near_hi], axis=1)
     sums = dot(terms.astype(bf16), videos, TN)
-    first, second = sums[0:64] + sums[64:128], sums[128:192] + sums[192:256]
-    cols = col_scr[...]
-    total = jnp.broadcast_to(total, (8, 128))
-    for k in range(4):
-        for half in range(2):
-            n = k * 2 + half
-            step = k // 2 * 2 + other(xl, half)
-            out_ref = send_ref if k % 2 else keep_ref
-            out_ref[step, :, 0:E] = first[n * 8 : (n + 1) * 8]
-            out_ref[step, :, E : 2 * E] = second[n * 8 : (n + 1) * 8]
-            out_ref[step, :, 2 * E : 2 * E + TILE] = cols
-            out_ref[step, :, 2 * E + TILE :] = total
+    first, second = sums[0:32] + sums[32:64], sums[64:96] + sums[96:128]
+    xl = position()[2]
+    for n in range(4):
+        step = n // 2 * 2 + other(xl, n % 2)
+        out_ref[step, :, 0:E] = first[n * 8 : (n + 1) * 8]
+        out_ref[step, :, E : 2 * E] = second[n * 8 : (n + 1) * 8]
+        out_ref[step, :, 2 * E : 2 * E + TILE] = cols
+        out_ref[step, :, 2 * E + TILE :] = total
+
+
+def first_kernel(
+    video_ref, target_ref, set0_ref, set1_ref, set2_ref, set3_ref,
+    own_ref, cols_ref, sums_ref, positive_ref, near_ref, tile_scr,
+):
+    xh, c, xl, spot = position()
+    cols_ref[...] = jnp.zeros_like(cols_ref)
+    videos = video_ref[...]
+    pieces = (set0_ref, set1_ref, set2_ref, set3_ref)
+    tiles = [tile_of(xh, c, xl, spot, k) for k in range(4)]
+    sums_ref[...], positive_ref[...] = score(
+        videos, plane_rows(target_ref, xl), pieces, tiles, own_ref, tile_scr, cols_ref,
+        jnp.zeros((PLANE_ROWS, 128), f32), jnp.zeros((1, TILE), f32), pl.multiple_of(spot * 8, 8),
+    )
+    near_ref[...] = near_exps(videos, pieces, tiles, 0)
+
+
+def second_kernel(
+    video_ref, target_ref, set4_ref, set5_ref, set6_ref, set7_ref, cols_ref, sums_ref, positive_ref,
+    send_ref, own_ref, rowsum_ref, cols_out, total_ref, tile_scr,
+):
+    xh, c, xl, spot = position()
+    target = plane_rows(target_ref, xl)
+    videos = video_ref[...]
+    pieces = (set4_ref, set5_ref, set6_ref, set7_ref)
+    tiles = [tile_of(xh, c, xl, spot, k) for k in range(4, 8)]
+    cols_out[...] = cols_ref[...]
+    sums, positive = score(
+        videos, target, pieces, tiles, own_ref, tile_scr, cols_out,
+        sums_ref[...], positive_ref[...], pl.multiple_of(spot * 8, 8),
+    )
+    near = near_exps(videos, pieces, tiles, 1)
+    rowsum = jnp.sum(sums, axis=1, keepdims=True)
+    rowsum_ref[...] = rowsum
+    total = jnp.sum(jnp.log(rowsum), axis=0, keepdims=True) - 2.0 * jnp.sum(
+        positive, axis=1, keepdims=True
+    )
+    total_ref[...] = jnp.broadcast_to(total, (8, 128))
+    near_sums(near, rowsum, target, videos, 1, cols_out[...], total_ref[...], send_ref)
+
+
+def keep_kernel(video_ref, target_ref, near_ref, rowsum_ref, cols_ref, total_ref, keep_ref):
+    target = plane_rows(target_ref, position()[2])
+    near_sums(
+        near_ref[...], rowsum_ref[...], target, video_ref[...], 0, cols_ref[...], total_ref[...],
+        keep_ref,
+    )
+
+
+def keep_sums(*args):
+    return pl.pallas_call(
+        keep_kernel,
+        in_specs=[VMEM] * 6,
+        out_specs=VMEM,
+        out_shape=jax.ShapeDtypeStruct((4, 8, SUMS), f32),
+        compiler_params=pltpu.CompilerParams(vmem_limit_bytes=16 << 20),
+        cost_estimate=pl.CostEstimate(
+            flops=2 * PLANE_ROWS * 128 * E, bytes_accessed=1 << 20, transcendentals=0
+        ),
+    )(*args)
 
 
 def first_logits(*args):
     return pl.pallas_call(
         first_kernel,
-        in_specs=[VMEM] * 8,
-        out_specs=[VMEM] * 6,
+        in_specs=[VMEM] * 6,
+        out_specs=[VMEM] * 5,
         out_shape=[
             jax.ShapeDtypeStruct((8, 2 * SET), f32),
             jax.ShapeDtypeStruct((8, TILE), f32),
             jax.ShapeDtypeStruct((PLANE_ROWS, 128), f32),
             jax.ShapeDtypeStruct((1, TILE), f32),
-            jax.ShapeDtypeStruct((8, E), f32),
-            jax.ShapeDtypeStruct((8, 1), f32),
+            jax.ShapeDtypeStruct((PLANE_ROWS, 32), f32),
         ],
         scratch_shapes=[pltpu.VMEM((PLANE_ROWS, TILE), f32)],
         compiler_params=pltpu.CompilerParams(vmem_limit_bytes=16 << 20),
@@ -447,14 +475,16 @@
 def second_logits(*args):
     return pl.pallas_call(
         second_kernel,
-        in_specs=[VMEM] * 13,
-        out_specs=[VMEM] * 3,
+        in_specs=[VMEM] * 9,
+        out_specs=[VMEM] * 5,
         out_shape=[
             jax.ShapeDtypeStruct((4, 8, SUMS), f32),
-            jax.ShapeDtypeStruct((4, 8, SUMS), f32),
             jax.ShapeDtypeStruct((8, 2 * SET), f32),
-        ],
-        scratch_shapes=[pltpu.VMEM((PLANE_ROWS, TILE), f32), pltpu.VMEM((8, TILE), f32)],
+            jax.ShapeDtypeStruct((PLANE_ROWS, 1), f32),
+            jax.ShapeDtypeStruct((8, TILE), f32),
+            jax.ShapeDtypeStruct((8, 128), f32),
+        ],
+        scratch_shapes=[pltpu.VMEM((PLANE_ROWS, TILE), f32)],
         compiler_params=pltpu.CompilerParams(vmem_limit_bytes=16 << 20),
         cost_estimate=pl.CostEstimate(
             flops=2 * PLANE_ROWS * 1536 * E, bytes_accessed=4 << 20, transcendentals=1 << 18
@@ -567,10 +597,9 @@
     videos = videos.reshape(PLANE_ROWS, E)
     mine = (texts, moved[2], moved[1], moved[0])
     theirs = tuple(swap(x) for x in mine)
-    own, cols, sums, positive, video_hat, video_norm = first_logits(
-        videos, target, *mine, video_hat, video_norm
-    )
-    keep, send, last = second_logits(videos, target, *mine, *theirs, cols, sums, positive)
+    own, cols, sums, positive, near = first_logits(videos, target, *mine)
+    send, last, rowsum, cols, total = second_logits(videos, target, *theirs, cols, sums, positive)
+    keep = keep_sums(videos, target, near, rowsum, cols, total)
     parts = add_parts(keep, swap(send))
     parts = [parts[0]] + [along(parts[step], step) for step in (2, 3, 1)]
     loss, video_grad, text_grad = gradients(

time: 93.9 us -> 93.6 us (level)
    pallas_call x2 -> x3, Pallas kernels: 2.18 us -> 2.85 us  [the longest x1 1.38 us: second_logits(): pl.pallas_call(second_kernel, in_specs=[VMEM] * 9, out_specs=[VMEM] * 5,...]
  transfers between devices with their start and end apart: 13 -> 13, of which waited for: 5 -> 6; matrix products, arithmetic and copies ran while one was open for 0% -> 0% of each run, Pallas kernels for 7% -> 8%
where the time goes in v9:
time: 93.6 us; the launch traced here: 93.4 us
  blocking collectives  43.8 us (47%)
  starting transfers between devices  24.8 us (26%)
  Pallas kernels  13.6 us (15%)
  waiting for transfers between devices  9.78 us (10%)
    all_to_all x1, blocking collectives, exchange(): return lax.all_to_all(x, axes, 0, 0, tiled=True)  43.8 us
    ppermute x5, starting transfers between devices, swap(): return lax.ppermute(x, 'c', [(0, 1), (1, 0)])  9 us
    ppermute x6, starting transfers between devices, along(): return lax.ppermute(x, ('xh', 'xl'), [(k, k ^ step) for k in range(4)])  8.06 us
    ppermute x6, waiting for transfers between devices, along(): return lax.ppermute(x, ('xh', 'xl'), [(k, k ^ step) for k in range(4)])  7.23 us
    all_to_all x1, starting transfers between devices, exchange(): return lax.all_to_all(x, axes, 0, 0, tiled=True)  6.5 us
    pallas_call x1, Pallas kernels, clip_sums(): pl.pallas_call(clip_kernel, in_specs=[pl.BlockSpec(memory_space=pltpu.HBM...  5.59 us
    pallas_call x1, Pallas kernels, embed(): pl.pallas_call(embed_kernel, in_specs=[VMEM, VMEM], out_specs=[VMEM] * 4,...  2.49 us
  transfers between devices with their start and end apart: 13, of which 6 were waited for; matrix products, arithmetic and copies ran while one was open for 0% of the time, Pallas kernels for 8%

profile of v9, /device:TPU:1, one launch (start us, length us, event | category | flops | bytes accessed | tf_op | source)
XLA Modules:
  0.0 93.4 jit_solution(12151204470084824449)
XLA Ops:
  0.6 3.7 %collective-permute-start = (bf16[8,768]{1,0:T(8,128)(2,1)}, bf16[8,768]{1,0:T(8,128)(2,1)S(1)}, u32[]{:S(2)}, u32[]{:S(2)}) collective-permute-start(bf16[8,768]{1,0:T(8,128)(2,1)} %text_ref.1), channel_id=1, source_target_pairs={{0,128},{32,160},{128,0},{160,32},{1,129},{33,161},{129,1},{161,33... | collective-permute-start | bytes 36872 | tf_op jit(solution)/shard_map/ppermute | solution.py:578
  4.3 5.6 %shard_map.93 = (bf16[256,896]{1,0:T(8,128)(2,1)S(1)}, f32[1,256]{1,0:T(1,128)S(1)}, f32[1,128]{1,0:T(1,128)S(1)}, f32[8,768]{1,0:T(8,128)S(1)}) custom-call(s32[1,64]{1,0:T(1,128)} %bitcast.16, bf16[1024,3200]{1,0:T(8,128)(2,1)} %bitcast.15, bf16[25,3200]{1,0:T(8,128)(2,1)} %pool_hbm.1, bf16[8,768]{1,0:T(8,128)(2,1)} %text_ref.1, s32[1,8]{1,0:T(1,128)} %bitcast.17), custom_call_target="tpu_custom_call" | custom-call | flops 419430400 | bytes 8388608 | tf_op jit(solution)/shard_map/pallas_call | solution.py:198
  9.9 0.8 shard_map.94
  10.7 43.8 %all_to_all.10 = bf16[64,8,1280]{2,1,0:T(8,128)(2,1)S(1)} all-to-all(bf16[64,8,1280]{2,1,0:T(8,128)(2,1)S(1)} %bitcast.12), channel_id=1, replica_groups=mesh['xh'=2,'c'=2,'xl'=2,'z'=8,'y'=4] {'xl','z','y'}, dimensions={0} | all-to-all | bytes 2621440 | tf_op jit(solution)/shard_map/all_to_all | solution.py:570
  54.6 2.5 %shard_map.95 = (bf16[8,768]{1,0:T(8,128)(2,1)}, f32[8,768]{1,0:T(8,128)S(1)}, f32[8,1]{1,0:T(8,128)S(1)}, bf16[32,8,768]{2,1,0:T(8,128)(2,1)}) custom-call(bf16[512,1280]{1,0:T(8,128)(2,1)S(1)} %bitcast.7, bf16[3200,768]{1,0:T(8,128)(2,1)S(1)} %bitcast.14), custom_call_target="tpu_custom_call" | custom-call | flops 117964800 | bytes 6291456 | tf_op jit(solution)/shard_map/pallas_call | solution.py:256
  57.1 6.5 %all-to-all-start.1 = ((bf16[32,8,768]{2,1,0:T(8,128)(2,1)}), bf16[32,8,768]{2,1,0:T(8,128)(2,1)S(1)}, u32[]{:S(2)}, u32[]{:S(2)}) async-start(bf16[32,8,768]{2,1,0:T(8,128)(2,1)} %get-tuple-element.40), calls=%async_computation.1 | async-start | bytes 786432 | tf_op jit(solution)/shard_map/all_to_all | solution.py:570
  63.6 0.5 shard_map.96
  64.1 0.0 copy-start.1
  64.1 0.6 copy-done.1
  64.7 0.8 collective-permute-start.3
  65.5 0.6 collective-permute-start.2
  66.1 1.2 %collective-permute-start.1 = (bf16[256,768]{1,0:T(8,128)(2,1)S(1)}, bf16[256,768]{1,0:T(8,128)(2,1)S(1)}, u32[]{:S(2)}, u32[]{:S(2)}) collective-permute-start(bf16[256,768]{1,0:T(8,128)(2,1)S(1)} %get-tuple-element.43.set0_ref), channel_id=1, source_target_pairs={{0,1},{1,0},{2,3},{3,2},{4,5},{5,4},{6,7},{7,6},{8,9},{9,8},{10,11... | collective-permute-start | bytes 1179656 | tf_op jit(solution)/shard_map/ppermute | solution.py:582
  67.3 3.2 %collective-permute-start.4 = (bf16[256,768]{1,0:T(8,128)(2,1)S(1)}, bf16[256,768]{1,0:T(8,128)(2,1)S(1)}, u32[]{:S(2)}, u32[]{:S(2)}) collective-permute-start(bf16[256,768]{1,0:T(8,128)(2,1)S(1)} %get-tuple-element.43.set0_ref), channel_id=1, source_target_pairs={{0,64},{64,0},{1,65},{65,1},{2,66},{66,2},{3,67},{67,3},{4,68},{68... | collective-permute-start | bytes 1179656 | tf_op jit(solution)/shard_map/ppermute | solution.py:574
  70.6 3.9 %collective-permute-done.3.set2_ref = bf16[256,768]{1,0:T(8,128)(2,1)S(1)} collective-permute-done((bf16[256,768]{1,0:T(8,128)(2,1)S(1)}, bf16[256,768]{1,0:T(8,128)(2,1)S(1)}, u32[]{:S(2)}, u32[]{:S(2)}) %collective-permute-start.3) | collective-permute-done | bytes 393248 | tf_op jit(solution)/shard_map/ppermute | solution.py:578
  74.4 3.0 %collective-permute-start.6 = (bf16[256,768]{1,0:T(8,128)(2,1)S(1)}, bf16[256,768]{1,0:T(8,128)(2,1)S(1)}, u32[]{:S(2)}, u32[]{:S(2)}) collective-permute-start(bf16[256,768]{1,0:T(8,128)(2,1)S(1)} %collective-permute-done.3.set2_ref), channel_id=1, source_target_pairs={{0,64},{64,0},{1,65},{65,1},{2,66},{66,2},{3,67},{67,3},{4,68},{68... | collective-permute-start | bytes 1179656 | tf_op jit(solution)/shard_map/ppermute | solution.py:574
  77.4 0.0 collective-permute-start.5
  77.4 1.6 %collective-permute-done.1.set3_ref = bf16[256,768]{1,0:T(8,128)(2,1)S(1)} collective-permute-done((bf16[256,768]{1,0:T(8,128)(2,1)S(1)}, bf16[256,768]{1,0:T(8,128)(2,1)S(1)}, u32[]{:S(2)}, u32[]{:S(2)}) %collective-permute-start.1) | collective-permute-done | bytes 393248 | tf_op jit(solution)/shard_map/ppermute | solution.py:582
  79.0 0.0 all-to-all-done.1
  79.0 2.1 %collective-permute-start.7 = (bf16[256,768]{1,0:T(8,128)(2,1)S(1)}, bf16[256,768]{1,0:T(8,128)(2,1)S(1)}, u32[]{:S(2)}, u32[]{:S(2)}) collective-permute-start(bf16[256,768]{1,0:T(8,128)(2,1)S(1)} %collective-permute-done.1.set3_ref), channel_id=1, source_target_pairs={{0,64},{64,0},{1,65},{65,1},{2,66},{66,2},{3,67},{67,3},{4,68},{68... | collective-permute-start | bytes 1179656 | tf_op jit(solution)/shard_map/ppermute | solution.py:574
  81.1 1.1 %shard_map.97 = (f32[8,1024]{1,0:T(8,128)S(1)}, f32[8,256]{1,0:T(8,128)S(1)}, f32[256,128]{1,0:T(8,128)S(1)}, f32[1,256]{1,0:T(1,128)S(1)}, f32[256,32]{1,0:T(8,128)S(1)}) custom-call(bf16[256,768]{1,0:T(8,128)(2,1)S(1)} %bitcast.9, f32[512,1]{1,0:T(8,128)S(1)} %get-tuple-element.45.target_ref, bf16[256,768]{1,0:T(8,128)(2,1)S(1)} %get-tuple-element.43.set0_ref, ...), custom_call_target="tpu_custom_call" | custom-call | flops 402653184 | bytes 2097152 | tf_op jit(solution)/shard_map/pallas_call | solution.py:456
  82.2 0.0 collective-permute-done.4.set4_ref
  82.2 0.0 collective-permute-done.6.set6_ref
  82.2 0.3 collective-permute-done.7.set7_ref
  82.5 1.4 %shard_map.98 = (f32[4,8,1920]{2,1,0:T(8,128)S(1)}, f32[8,1024]{1,0:T(8,128)S(1)}, f32[256,1]{1,0:T(8,128)S(1)}, f32[8,256]{1,0:T(8,128)S(1)}, f32[8,128]{1,0:T(8,128)S(1)}) custom-call(bf16[256,768]{1,0:T(8,128)(2,1)S(1)} %bitcast.10, f32[512,1]{1,0:T(8,128)S(1)} %get-tuple-element.45.target_ref, bf16[256,768]{1,0:T(8,128)(2,1)S(1)} %collective-permute-done.4.set4_ref, ...), custom_call_target="tpu_custom_call" | custom-call | flops 603979776 | bytes 4194304 | tf_op jit(solution)/shard_map/pallas_call | solution.py:476
  83.8 0.6 collective-permute-start.8
  84.5 0.4 shard_map.99.keep_ref
  84.9 0.7 collective-permute-done.8.got_ref
  85.7 2.1 %collective-permute-start.9 = (f32[8,1920]{1,0:T(8,128)S(1)}, f32[8,1920]{1,0:T(8,128)S(1)}, u32[]{:S(2)}, u32[]{:S(2)}) collective-permute-start(f32[8,1920]{1,0:T(8,128)S(1)} %get-tuple-element.56), channel_id=1, source_target_pairs={{0,128},{32,160},{128,0},{160,32},{1,129},{33,161},{129,1},{161,33... | collective-permute-start | bytes 184328 | tf_op jit(solution)/shard_map/ppermute | solution.py:578
  87.8 0.9 collective-permute-start.10
  88.7 1.7 %collective-permute-done.9.part1_ref = f32[8,1920]{1,0:T(8,128)S(1)} collective-permute-done((f32[8,1920]{1,0:T(8,128)S(1)}, f32[8,1920]{1,0:T(8,128)S(1)}, u32[]{:S(2)}, u32[]{:S(2)}) %collective-permute-start.9) | collective-permute-done | bytes 61472 | tf_op jit(solution)/shard_map/ppermute | solution.py:578
  90.3 1.7 %collective-permute-done.10.part2_ref = f32[8,1920]{1,0:T(8,128)S(1)} collective-permute-done((f32[8,1920]{1,0:T(8,128)S(1)}, f32[8,1920]{1,0:T(8,128)S(1)}, u32[]{:S(2)}, u32[]{:S(2)}) %collective-permute-start.10) | collective-permute-done | bytes 61472 | tf_op jit(solution)/shard_map/ppermute | solution.py:578
  92.1 1.3 %shard_map.101 = (f32[1,1]{1,0:T(1,128)}, f32[8,768]{1,0:T(8,128)}, f32[8,768]{1,0:T(8,128)}) custom-call(f32[8,1920]{1,0:T(8,128)S(1)} %get-tuple-element.55.part0_ref, f32[8,1920]{1,0:T(8,128)S(1)} %collective-permute-done.9.part1_ref, f32[8,1920]{1,0:T(8,128)S(1)} %collective-permute-done.10.part2_ref, f32[8,1920]{1,0:T(8,128)S(1)} %collective-permute-done.11.part3_ref, ...), custom_call_target="tpu_custom_call" | custom-call | flops 25165824 | bytes 5242880 | tf_op jit(solution)/shard_map/pallas_call | solution.py:552
  (15 shorter events, 0.1 us)
Async XLA Ops:
  0.6 9.3 %collective-permute-start = (bf16[8,768]{1,0:T(8,128)(2,1)}, bf16[8,768]{1,0:T(8,128)(2,1)S(1)}, u32[]{:S(2)}, u32[]{:S(2)}) collective-permute-start(bf16[8,768]{1,0:T(8,128)(2,1)} %text_ref.1), channel_id=1, source_target_pairs={{0,128},{32,160},{128,0},{160,32},{1,129},{33,161},{129,1},{161,33... | collective-permute-start | bytes 36872 | tf_op jit(solution)/shard_map/ppermute | solution.py:578
  4.3 50.3 %slice-start = ((s8[4915200]{0:T(1024)(128)(4,1)}), s8[4194304]{0:T(1024)(128)(4,1)S(1)}, s32[]{:S(2)}) async-start(s8[4915200]{0:T(1024)(128)(4,1)} %bitcast.13), calls=%async_computation.2 | async-start | bytes 8388608
  4.3 50.3 %slice-start.1 = ((s8[4915200]{0:T(1024)(128)(4,1)}), s8[720896]{0:T(1024)(128)(4,1)S(1)}, s32[]{:S(2)}) async-start(s8[4915200]{0:T(1024)(128)(4,1)} %bitcast.13), calls=%async_computation.3 | async-start | bytes 1441792
  57.1 35.0 %copy-start = (bf16[8,768]{1,0:T(8,128)(2,1)S(1)}, bf16[8,768]{1,0:T(8,128)(2,1)}, u32[]{:S(2)}) copy-start(bf16[8,768]{1,0:T(8,128)(2,1)} %text_ref.1) | copy-start | bytes 36868
  57.1 21.9 %all-to-all-start.1 = ((bf16[32,8,768]{2,1,0:T(8,128)(2,1)}), bf16[32,8,768]{2,1,0:T(8,128)(2,1)S(1)}, u32[]{:S(2)}, u32[]{:S(2)}) async-start(bf16[32,8,768]{2,1,0:T(8,128)(2,1)} %get-tuple-element.40), calls=%async_computation.1 | async-start | bytes 786432 | tf_op jit(solution)/shard_map/all_to_all | solution.py:570
  64.1 0.6 copy-start.1
  64.7 9.7 %collective-permute-start.3 = (bf16[256,768]{1,0:T(8,128)(2,1)S(1)}, bf16[256,768]{1,0:T(8,128)(2,1)S(1)}, u32[]{:S(2)}, u32[]{:S(2)}) collective-permute-start(bf16[256,768]{1,0:T(8,128)(2,1)S(1)} %get-tuple-element.43.set0_ref), channel_id=1, source_target_pairs={{0,160},{32,128},{128,32},{160,0},{1,161},{33,129},{129,33},{161,1... | collective-permute-start | bytes 1179656 | tf_op jit(solution)/shard_map/ppermute | solution.py:578
  65.5 11.9 %collective-permute-start.2 = (bf16[256,768]{1,0:T(8,128)(2,1)S(1)}, bf16[256,768]{1,0:T(8,128)(2,1)S(1)}, u32[]{:S(2)}, u32[]{:S(2)}) collective-permute-start(bf16[256,768]{1,0:T(8,128)(2,1)S(1)} %get-tuple-element.43.set0_ref), channel_id=1, source_target_pairs={{0,32},{32,0},{128,160},{160,128},{1,33},{33,1},{129,161},{161,129... | collective-permute-start | bytes 1179656 | tf_op jit(solution)/shard_map/ppermute | solution.py:578
  66.1 12.9 %collective-permute-start.1 = (bf16[256,768]{1,0:T(8,128)(2,1)S(1)}, bf16[256,768]{1,0:T(8,128)(2,1)S(1)}, u32[]{:S(2)}, u32[]{:S(2)}) collective-permute-start(bf16[256,768]{1,0:T(8,128)(2,1)S(1)} %get-tuple-element.43.set0_ref), channel_id=1, source_target_pairs={{0,1},{1,0},{2,3},{3,2},{4,5},{5,4},{6,7},{7,6},{8,9},{9,8},{10,11... | collective-permute-start | bytes 1179656 | tf_op jit(solution)/shard_map/ppermute | solution.py:582
  67.3 14.8 %collective-permute-start.4 = (bf16[256,768]{1,0:T(8,128)(2,1)S(1)}, bf16[256,768]{1,0:T(8,128)(2,1)S(1)}, u32[]{:S(2)}, u32[]{:S(2)}) collective-permute-start(bf16[256,768]{1,0:T(8,128)(2,1)S(1)} %get-tuple-element.43.set0_ref), channel_id=1, source_target_pairs={{0,64},{64,0},{1,65},{65,1},{2,66},{66,2},{3,67},{67,3},{4,68},{68... | collective-permute-start | bytes 1179656 | tf_op jit(solution)/shard_map/ppermute | solution.py:574
  74.4 7.8 %collective-permute-start.6 = (bf16[256,768]{1,0:T(8,128)(2,1)S(1)}, bf16[256,768]{1,0:T(8,128)(2,1)S(1)}, u32[]{:S(2)}, u32[]{:S(2)}) collective-permute-start(bf16[256,768]{1,0:T(8,128)(2,1)S(1)} %collective-permute-done.3.set2_ref), channel_id=1, source_target_pairs={{0,64},{64,0},{1,65},{65,1},{2,66},{66,2},{3,67},{67,3},{4,68},{68... | collective-permute-start | bytes 1179656 | tf_op jit(solution)/shard_map/ppermute | solution.py:574
  77.4 4.7 %collective-permute-start.5 = (bf16[256,768]{1,0:T(8,128)(2,1)S(1)}, bf16[256,768]{1,0:T(8,128)(2,1)S(1)}, u32[]{:S(2)}, u32[]{:S(2)}) collective-permute-start(bf16[256,768]{1,0:T(8,128)(2,1)S(1)} %collective-permute-done.2.set1_ref), channel_id=1, source_target_pairs={{0,64},{64,0},{1,65},{65,1},{2,66},{66,2},{3,67},{67,3},{4,68},{68... | collective-permute-start | bytes 1179656 | tf_op jit(solution)/shard_map/ppermute | solution.py:574
  79.0 13.0 %copy-start.2 = (f32[8,768]{1,0:T(8,128)S(1)}, f32[8,768]{1,0:T(8,128)}, u32[]{:S(2)}) copy-start(f32[8,768]{1,0:T(8,128)} %copy-done.1) | copy-start | bytes 73732
  79.0 3.4 %collective-permute-start.7 = (bf16[256,768]{1,0:T(8,128)(2,1)S(1)}, bf16[256,768]{1,0:T(8,128)(2,1)S(1)}, u32[]{:S(2)}, u32[]{:S(2)}) collective-permute-start(bf16[256,768]{1,0:T(8,128)(2,1)S(1)} %collective-permute-done.1.set3_ref), channel_id=1, source_target_pairs={{0,64},{64,0},{1,65},{65,1},{2,66},{66,2},{3,67},{67,3},{4,68},{68... | collective-permute-start | bytes 1179656 | tf_op jit(solution)/shard_map/ppermute | solution.py:574
  83.8 1.8 %collective-permute-start.8 = (f32[4,8,1920]{2,1,0:T(8,128)S(1)}, f32[4,8,1920]{2,1,0:T(8,128)S(1)}, u32[]{:S(2)}, u32[]{:S(2)}) collective-permute-start(f32[4,8,1920]{2,1,0:T(8,128)S(1)} %get-tuple-element.54), channel_id=1, source_target_pairs={{0,64},{64,0},{1,65},{65,1},{2,66},{66,2},{3,67},{67,3},{4,68},{68... | collective-permute-start | bytes 737288 | tf_op jit(solution)/shard_map/ppermute | solution.py:574
  85.7 4.7 %collective-permute-start.9 = (f32[8,1920]{1,0:T(8,128)S(1)}, f32[8,1920]{1,0:T(8,128)S(1)}, u32[]{:S(2)}, u32[]{:S(2)}) collective-permute-start(f32[8,1920]{1,0:T(8,128)S(1)} %get-tuple-element.56), channel_id=1, source_target_pairs={{0,128},{32,160},{128,0},{160,32},{1,129},{33,161},{129,1},{161,33... | collective-permute-start | bytes 184328 | tf_op jit(solution)/shard_map/ppermute | solution.py:578
  87.8 4.3 %collective-permute-start.10 = (f32[8,1920]{1,0:T(8,128)S(1)}, f32[8,1920]{1,0:T(8,128)S(1)}, u32[]{:S(2)}, u32[]{:S(2)}) collective-permute-start(f32[8,1920]{1,0:T(8,128)S(1)} %get-tuple-element.57), channel_id=1, source_target_pairs={{0,160},{32,128},{128,32},{160,0},{1,161},{33,129},{129,33},{161,1... | collective-permute-start | bytes 184328 | tf_op jit(solution)/shard_map/ppermute | solution.py:578
  88.7 3.4 %collective-permute-start.11 = (f32[8,1920]{1,0:T(8,128)S(1)}, f32[8,1920]{1,0:T(8,128)S(1)}, u32[]{:S(2)}, u32[]{:S(2)}) collective-permute-start(f32[8,1920]{1,0:T(8,128)S(1)} %get-tuple-element.58), channel_id=1, source_target_pairs={{0,32},{32,0},{128,160},{160,128},{1,33},{33,1},{129,161},{161,129... | collective-permute-start | bytes 184328 | tf_op jit(solution)/shard_map/ppermute | solution.py:578

commit v10 on v9

--- a/solution.py
+++ b/solution.py
@@ -106,7 +106,7 @@
         here = iota((CHUNK, CLIPS), 1) == iota((CHUNK, CLIPS), 0) + step * CHUNK
         video = jnp.where(here, jnp.broadcast_to(videos, (CHUNK, CLIPS)), 0.0)
         video = jnp.sum(video, axis=1, keepdims=True).astype(jnp.int32)
-        local = jnp.where(lane - 64 == video % 8, 1.0, 0.0)
+        local = jnp.where((lane < 96) & (lane % 8 == video % 8), 1.0, 0.0)
         tail = jnp.where(lane < 32, den_hi, jnp.where(lane < 64, den - den_hi, local))
         put(step, H, tail)
         for h in range(0, H, 2):
@@ -138,10 +138,10 @@
     pair = pair_ref[...]
     code_ref[...] = jnp.concatenate(
         [
-            jnp.zeros((1, 72), f32),
+            jnp.zeros((1, 96), f32),
             (pair // 64).astype(f32),
             (pair % 64).astype(f32),
-            jnp.zeros((1, 40), f32),
+            jnp.zeros((1, 16), f32),
         ],
         axis=1,
     )
@@ -221,19 +221,16 @@
     arrived_ref, proj_ref, emb_ref, hat_ref, norm_ref, send_ref
 ):
     rows = CLIPS * 8
-    tails = arrived_ref[:, TAIL : TAIL + HD]
-    pick = jnp.where(iota((8, HD), 1) - 64 == iota((8, HD), 0), 1.0, 0.0).astype(bf16)
-    hot = dot(pick, tails, NT)
-    hot = jnp.where(iota((8, rows), 1) % PARTS == PARTS - 1, hot, 0.0)
-    assign = jnp.concatenate(
-        [hot if p == PARTS - 1 else pltpu.roll(hot, rows - (PARTS - 1 - p), 1) for p in range(PARTS)],
-        axis=0,
-    )
-    sums = dot(assign.astype(bf16), arrived_ref[:, 0:SENT])
+    tails = arrived_ref[:, TAIL : TAIL + HD].astype(f32).reshape(CLIPS, 8, HD)
+    upper = iota((CLIPS, 8, HD), 1) < 4
+    hot = jnp.where(upper, tails[:, 3:4, :], tails[:, 7:8, :]).reshape(rows, HD)
+    lane, row = iota((rows, HD), 1), iota((rows, HD), 0)
+    hot = jnp.where(lane // 8 == 8 + row % PARTS, hot, 0.0)
+    sums = dot(hot.astype(bf16), arrived_ref[:, 0:SENT], TN)
 
     def chunk(j):
         p, q = j // WIDE, j % WIDE
-        return sums[p * 8 : (p + 1) * 8, q * HD : (q + 1) * HD]
+        return sums[64 + p * 8 : 72 + p * 8, q * HD : (q + 1) * HD]
 
     den = chunk(H)
     den = den[:, 0:32] + den[:, 32:64]
@@ -259,7 +256,7 @@
         out_specs=[VMEM] * 4,
         out_shape=[
             jax.ShapeDtypeStruct((8, E), bf16),
-            jax.ShapeDtypeStruct((8, E), f32),
+            pltpu.HBM((8, E), f32),
             jax.ShapeDtypeStruct((8, 1), f32),
             jax.ShapeDtypeStruct((32, 8, E), bf16),
         ],
@@ -270,9 +267,7 @@
     )(arrived, out_proj)
 
 
-def text_kernel(arrived_ref, hat_ref, norm_ref, text_ref, target_ref, hat_out, norm_out):
-    hat_out[...] = hat_ref[...]
-    norm_out[...] = norm_ref[...]
+def text_kernel(arrived_ref, text_ref, target_ref):
     halves = arrived_ref[:, SENT : SENT + PIECE]
     row, col = iota((TILE, CLIPS * 8), 0), iota((TILE, CLIPS * 8), 1)
     for part in range(2):
@@ -283,20 +278,18 @@
     code = arrived_ref[:, TAIL : TAIL + HD].astype(f32).reshape(CLIPS, 8, HD)[:, 3:4, :]
     code = jnp.broadcast_to(code, (CLIPS, 8, HD)).reshape(rows, HD)
     lane, own = iota((rows, HD), 1), iota((rows, HD), 0) % 8
-    code = jnp.where(lane - 72 == own, 64.0 * code, jnp.where(lane - 80 == own, code, 0.0))
+    code = jnp.where(lane - 96 == own, 64.0 * code, jnp.where(lane - 104 == own, code, 0.0))
     target_ref[...] = jnp.sum(code, axis=1, keepdims=True)
 
 
 def text_piece(*args):
     return pl.pallas_call(
         text_kernel,
-        in_specs=[VMEM] * 3,
-        out_specs=[VMEM] * 4,
+        in_specs=[VMEM],
+        out_specs=[VMEM] * 2,
         out_shape=[
             jax.ShapeDtypeStruct((TILE, E), bf16),
             jax.ShapeDtypeStruct((SET, 1), f32),
-            jax.ShapeDtypeStruct((8, E), f32),
-            jax.ShapeDtypeStruct((8, 1), f32),
         ],
         compiler_params=pltpu.CompilerParams(vmem_limit_bytes=16 << 20),
         cost_estimate=pl.CostEstimate(
@@ -591,7 +584,7 @@
     arrived = exchange(outgoing.reshape(CLIPS, 8, SENT + PIECE), ROW)
     arrived = arrived.reshape(CLIPS * 8, SENT + PIECE)
     video_embed, video_hat, video_norm, send = embed(arrived, out_proj)
-    texts, target, video_hat, video_norm = text_piece(arrived, video_hat, video_norm)
+    texts, target = text_piece(arrived)
     moved = [turn_y(texts), along(texts, 3), along(texts, 1)]
     videos, moved[0] = lax.optimization_barrier((exchange(send, PLANE), moved[0]))
     videos = videos.reshape(PLANE_ROWS, E)

time: 93.6 us -> 93.1 us (level)
  no operation moved by 1% of the time
where the time goes in v10:
time: 93.1 us; the launch traced here: 92.8 us
  blocking collectives  43.8 us (47%)
  starting transfers between devices  24.7 us (27%)
  Pallas kernels  13.5 us (15%)
  waiting for transfers between devices  10.1 us (11%)
    all_to_all x1, blocking collectives, exchange(): return lax.all_to_all(x, axes, 0, 0, tiled=True)  43.8 us
    ppermute x5, starting transfers between devices, swap(): return lax.ppermute(x, 'c', [(0, 1), (1, 0)])  8.82 us
    ppermute x6, starting transfers between devices, along(): return lax.ppermute(x, ('xh', 'xl'), [(k, k ^ step) for k in range(4)])  8.12 us
    ppermute x6, waiting for transfers between devices, along(): return lax.ppermute(x, ('xh', 'xl'), [(k, k ^ step) for k in range(4)])  7.29 us
    all_to_all x1, starting transfers between devices, exchange(): return lax.all_to_all(x, axes, 0, 0, tiled=True)  6.56 us
    pallas_call x1, Pallas kernels, clip_sums(): pl.pallas_call(clip_kernel, in_specs=[pl.BlockSpec(memory_space=pltpu.HBM...  5.59 us
    pallas_call x1, Pallas kernels, embed(): pl.pallas_call(embed_kernel, in_specs=[VMEM, VMEM], out_specs=[VMEM] * 4,...  2.36 us
  transfers between devices with their start and end apart: 13, of which 6 were waited for; matrix products, arithmetic and copies ran while one was open for 0% of the time, Pallas kernels for 8%

profile of v10, /device:TPU:1, one launch (start us, length us, event | category | flops | bytes accessed | tf_op | source)
XLA Modules:
  0.0 92.8 jit_solution(17728120536209048269)
XLA Ops:
  0.6 3.7 %collective-permute-start = (bf16[8,768]{1,0:T(8,128)(2,1)}, bf16[8,768]{1,0:T(8,128)(2,1)S(1)}, u32[]{:S(2)}, u32[]{:S(2)}) collective-permute-start(bf16[8,768]{1,0:T(8,128)(2,1)} %text_ref.1), channel_id=1, source_target_pairs={{0,128},{32,160},{128,0},{160,32},{1,129},{33,161},{129,1},{161,33... | collective-permute-start | bytes 36872 | tf_op jit(solution)/shard_map/ppermute | solution.py:571
  4.3 5.6 %shard_map.93 = (bf16[256,896]{1,0:T(8,128)(2,1)S(1)}, f32[1,256]{1,0:T(1,128)S(1)}, f32[1,128]{1,0:T(1,128)S(1)}, f32[8,768]{1,0:T(8,128)S(1)}) custom-call(s32[1,64]{1,0:T(1,128)} %bitcast.16, bf16[1024,3200]{1,0:T(8,128)(2,1)} %bitcast.15, bf16[25,3200]{1,0:T(8,128)(2,1)} %pool_hbm.1, bf16[8,768]{1,0:T(8,128)(2,1)} %text_ref.1, s32[1,8]{1,0:T(1,128)} %bitcast.17), custom_call_target="tpu_custom_call" | custom-call | flops 419430400 | bytes 8388608 | tf_op jit(solution)/shard_map/pallas_call | solution.py:198
  9.9 0.0 collective-permute-done.far_ref
  9.9 0.8 shard_map.94
  10.7 43.8 %all_to_all.10 = bf16[64,8,1280]{2,1,0:T(8,128)(2,1)S(1)} all-to-all(bf16[64,8,1280]{2,1,0:T(8,128)(2,1)S(1)} %bitcast.12), channel_id=1, replica_groups=mesh['xh'=2,'c'=2,'xl'=2,'z'=8,'y'=4] {'xl','z','y'}, dimensions={0} | all-to-all | bytes 2621440 | tf_op jit(solution)/shard_map/all_to_all | solution.py:563
  54.5 2.4 %shard_map.95 = (bf16[8,768]{1,0:T(8,128)(2,1)}, f32[8,768]{1,0:T(8,128)}, f32[8,1]{1,0:T(8,128)S(1)}, bf16[32,8,768]{2,1,0:T(8,128)(2,1)}) custom-call(bf16[512,1280]{1,0:T(8,128)(2,1)S(1)} %bitcast.7, bf16[3200,768]{1,0:T(8,128)(2,1)S(1)} %bitcast.14), custom_call_target="tpu_custom_call" | custom-call | flops 117964800 | bytes 6291456 | tf_op jit(solution)/shard_map/pallas_call | solution.py:253
  56.9 6.6 %all-to-all-start.1 = ((bf16[32,8,768]{2,1,0:T(8,128)(2,1)}), bf16[32,8,768]{2,1,0:T(8,128)(2,1)S(1)}, u32[]{:S(2)}, u32[]{:S(2)}) async-start(bf16[32,8,768]{2,1,0:T(8,128)(2,1)} %get-tuple-element.38), calls=%async_computation.1 | async-start | bytes 786432 | tf_op jit(solution)/shard_map/all_to_all | solution.py:563
  63.4 0.5 shard_map.96
  63.9 0.9 collective-permute-start.3
  64.8 0.6 collective-permute-start.2
  65.4 1.2 %collective-permute-start.1 = (bf16[256,768]{1,0:T(8,128)(2,1)S(1)}, bf16[256,768]{1,0:T(8,128)(2,1)S(1)}, u32[]{:S(2)}, u32[]{:S(2)}) collective-permute-start(bf16[256,768]{1,0:T(8,128)(2,1)S(1)} %get-tuple-element.39.set0_ref), channel_id=1, source_target_pairs={{0,1},{1,0},{2,3},{3,2},{4,5},{5,4},{6,7},{7,6},{8,9},{9,8},{10,11... | collective-permute-start | bytes 1179656 | tf_op jit(solution)/shard_map/ppermute | solution.py:575
  66.7 3.2 %collective-permute-start.4 = (bf16[256,768]{1,0:T(8,128)(2,1)S(1)}, bf16[256,768]{1,0:T(8,128)(2,1)S(1)}, u32[]{:S(2)}, u32[]{:S(2)}) collective-permute-start(bf16[256,768]{1,0:T(8,128)(2,1)S(1)} %get-tuple-element.39.set0_ref), channel_id=1, source_target_pairs={{0,64},{64,0},{1,65},{65,1},{2,66},{66,2},{3,67},{67,3},{4,68},{68... | collective-permute-start | bytes 1179656 | tf_op jit(solution)/shard_map/ppermute | solution.py:567
  69.9 3.8 %collective-permute-done.3.set2_ref = bf16[256,768]{1,0:T(8,128)(2,1)S(1)} collective-permute-done((bf16[256,768]{1,0:T(8,128)(2,1)S(1)}, bf16[256,768]{1,0:T(8,128)(2,1)S(1)}, u32[]{:S(2)}, u32[]{:S(2)}) %collective-permute-start.3) | collective-permute-done | bytes 393248 | tf_op jit(solution)/shard_map/ppermute | solution.py:571
  73.7 3.0 %collective-permute-start.6 = (bf16[256,768]{1,0:T(8,128)(2,1)S(1)}, bf16[256,768]{1,0:T(8,128)(2,1)S(1)}, u32[]{:S(2)}, u32[]{:S(2)}) collective-permute-start(bf16[256,768]{1,0:T(8,128)(2,1)S(1)} %collective-permute-done.3.set2_ref), channel_id=1, source_target_pairs={{0,64},{64,0},{1,65},{65,1},{2,66},{66,2},{3,67},{67,3},{4,68},{68... | collective-permute-start | bytes 1179656 | tf_op jit(solution)/shard_map/ppermute | solution.py:567
  76.8 0.0 collective-permute-done.2.set1_ref
  76.8 0.0 collective-permute-start.5
  76.8 1.8 %collective-permute-done.1.set3_ref = bf16[256,768]{1,0:T(8,128)(2,1)S(1)} collective-permute-done((bf16[256,768]{1,0:T(8,128)(2,1)S(1)}, bf16[256,768]{1,0:T(8,128)(2,1)S(1)}, u32[]{:S(2)}, u32[]{:S(2)}) %collective-permute-start.1) | collective-permute-done | bytes 393248 | tf_op jit(solution)/shard_map/ppermute | solution.py:575
  78.6 0.0 all-to-all-done.1
  78.6 2.1 %collective-permute-start.7 = (bf16[256,768]{1,0:T(8,128)(2,1)S(1)}, bf16[256,768]{1,0:T(8,128)(2,1)S(1)}, u32[]{:S(2)}, u32[]{:S(2)}) collective-permute-start(bf16[256,768]{1,0:T(8,128)(2,1)S(1)} %collective-permute-done.1.set3_ref), channel_id=1, source_target_pairs={{0,64},{64,0},{1,65},{65,1},{2,66},{66,2},{3,67},{67,3},{4,68},{68... | collective-permute-start | bytes 1179656 | tf_op jit(solution)/shard_map/ppermute | solution.py:567
  80.7 1.1 %shard_map.97 = (f32[8,1024]{1,0:T(8,128)S(1)}, f32[8,256]{1,0:T(8,128)S(1)}, f32[256,128]{1,0:T(8,128)S(1)}, f32[1,256]{1,0:T(1,128)S(1)}, f32[256,32]{1,0:T(8,128)S(1)}) custom-call(bf16[256,768]{1,0:T(8,128)(2,1)S(1)} %bitcast.9, f32[512,1]{1,0:T(8,128)S(1)} %get-tuple-element.41.target_ref, bf16[256,768]{1,0:T(8,128)(2,1)S(1)} %get-tuple-element.39.set0_ref, ...), custom_call_target="tpu_custom_call" | custom-call | flops 402653184 | bytes 2097152 | tf_op jit(solution)/shard_map/pallas_call | solution.py:449
  81.7 0.0 collective-permute-done.6.set6_ref
  81.8 0.0 collective-permute-done.5.set5_ref
  81.8 0.3 collective-permute-done.7.set7_ref
  82.0 1.4 %shard_map.98 = (f32[4,8,1920]{2,1,0:T(8,128)S(1)}, f32[8,1024]{1,0:T(8,128)S(1)}, f32[256,1]{1,0:T(8,128)S(1)}, f32[8,256]{1,0:T(8,128)S(1)}, f32[8,128]{1,0:T(8,128)S(1)}) custom-call(bf16[256,768]{1,0:T(8,128)(2,1)S(1)} %bitcast.10, f32[512,1]{1,0:T(8,128)S(1)} %get-tuple-element.41.target_ref, bf16[256,768]{1,0:T(8,128)(2,1)S(1)} %collective-permute-done.4.set4_ref, ...), custom_call_target="tpu_custom_call" | custom-call | flops 603979776 | bytes 4194304 | tf_op jit(solution)/shard_map/pallas_call | solution.py:469
  83.4 0.5 collective-permute-start.8
  83.9 0.4 shard_map.99.keep_ref
  84.3 0.7 collective-permute-done.8.got_ref
  85.0 2.1 %collective-permute-start.9 = (f32[8,1920]{1,0:T(8,128)S(1)}, f32[8,1920]{1,0:T(8,128)S(1)}, u32[]{:S(2)}, u32[]{:S(2)}) collective-permute-start(f32[8,1920]{1,0:T(8,128)S(1)} %get-tuple-element.52), channel_id=1, source_target_pairs={{0,128},{32,160},{128,0},{160,32},{1,129},{33,161},{129,1},{161,33... | collective-permute-start | bytes 184328 | tf_op jit(solution)/shard_map/ppermute | solution.py:571
  87.2 0.8 collective-permute-start.10
  88.0 1.7 %collective-permute-done.9.part1_ref = f32[8,1920]{1,0:T(8,128)S(1)} collective-permute-done((f32[8,1920]{1,0:T(8,128)S(1)}, f32[8,1920]{1,0:T(8,128)S(1)}, u32[]{:S(2)}, u32[]{:S(2)}) %collective-permute-start.9) | collective-permute-done | bytes 61472 | tf_op jit(solution)/shard_map/ppermute | solution.py:571
  89.7 1.8 %collective-permute-done.10.part2_ref = f32[8,1920]{1,0:T(8,128)S(1)} collective-permute-done((f32[8,1920]{1,0:T(8,128)S(1)}, f32[8,1920]{1,0:T(8,128)S(1)}, u32[]{:S(2)}, u32[]{:S(2)}) %collective-permute-start.10) | collective-permute-done | bytes 61472 | tf_op jit(solution)/shard_map/ppermute | solution.py:571
  91.5 1.3 %shard_map.101 = (f32[1,1]{1,0:T(1,128)}, f32[8,768]{1,0:T(8,128)}, f32[8,768]{1,0:T(8,128)}) custom-call(f32[8,1920]{1,0:T(8,128)S(1)} %get-tuple-element.51.part0_ref, f32[8,1920]{1,0:T(8,128)S(1)} %collective-permute-done.9.part1_ref, f32[8,1920]{1,0:T(8,128)S(1)} %collective-permute-done.10.part2_ref, f32[8,1920]{1,0:T(8,128)S(1)} %collective-permute-done.11.part3_ref, ...), custom_call_target="tpu_custom_call" | custom-call | flops 25165824 | bytes 5242880 | tf_op jit(solution)/shard_map/pallas_call | solution.py:545
  (13 shorter events, 0.0 us)
Async XLA Ops:
  0.6 9.3 %collective-permute-start = (bf16[8,768]{1,0:T(8,128)(2,1)}, bf16[8,768]{1,0:T(8,128)(2,1)S(1)}, u32[]{:S(2)}, u32[]{:S(2)}) collective-permute-start(bf16[8,768]{1,0:T(8,128)(2,1)} %text_ref.1), channel_id=1, source_target_pairs={{0,128},{32,160},{128,0},{160,32},{1,129},{33,161},{129,1},{161,33... | collective-permute-start | bytes 36872 | tf_op jit(solution)/shard_map/ppermute | solution.py:571
  4.3 50.2 %slice-start = ((s8[4915200]{0:T(1024)(128)(4,1)}), s8[4194304]{0:T(1024)(128)(4,1)S(1)}, s32[]{:S(2)}) async-start(s8[4915200]{0:T(1024)(128)(4,1)} %bitcast.13), calls=%async_computation.2 | async-start | bytes 8388608
  4.3 50.2 %slice-start.1 = ((s8[4915200]{0:T(1024)(128)(4,1)}), s8[720896]{0:T(1024)(128)(4,1)S(1)}, s32[]{:S(2)}) async-start(s8[4915200]{0:T(1024)(128)(4,1)} %bitcast.13), calls=%async_computation.3 | async-start | bytes 1441792
  56.9 34.6 %copy-start = (bf16[8,768]{1,0:T(8,128)(2,1)S(1)}, bf16[8,768]{1,0:T(8,128)(2,1)}, u32[]{:S(2)}) copy-start(bf16[8,768]{1,0:T(8,128)(2,1)} %text_ref.1) | copy-start | bytes 36868
  56.9 21.7 %all-to-all-start.1 = ((bf16[32,8,768]{2,1,0:T(8,128)(2,1)}), bf16[32,8,768]{2,1,0:T(8,128)(2,1)S(1)}, u32[]{:S(2)}, u32[]{:S(2)}) async-start(bf16[32,8,768]{2,1,0:T(8,128)(2,1)} %get-tuple-element.38), calls=%async_computation.1 | async-start | bytes 786432 | tf_op jit(solution)/shard_map/all_to_all | solution.py:563
  63.9 9.8 %collective-permute-start.3 = (bf16[256,768]{1,0:T(8,128)(2,1)S(1)}, bf16[256,768]{1,0:T(8,128)(2,1)S(1)}, u32[]{:S(2)}, u32[]{:S(2)}) collective-permute-start(bf16[256,768]{1,0:T(8,128)(2,1)S(1)} %get-tuple-element.39.set0_ref), channel_id=1, source_target_pairs={{0,160},{32,128},{128,32},{160,0},{1,161},{33,129},{129,33},{161,1... | collective-permute-start | bytes 1179656 | tf_op jit(solution)/shard_map/ppermute | solution.py:571
  64.8 11.9 %collective-permute-start.2 = (bf16[256,768]{1,0:T(8,128)(2,1)S(1)}, bf16[256,768]{1,0:T(8,128)(2,1)S(1)}, u32[]{:S(2)}, u32[]{:S(2)}) collective-permute-start(bf16[256,768]{1,0:T(8,128)(2,1)S(1)} %get-tuple-element.39.set0_ref), channel_id=1, source_target_pairs={{0,32},{32,0},{128,160},{160,128},{1,33},{33,1},{129,161},{161,129... | collective-permute-start | bytes 1179656 | tf_op jit(solution)/shard_map/ppermute | solution.py:571
  65.4 13.1 %collective-permute-start.1 = (bf16[256,768]{1,0:T(8,128)(2,1)S(1)}, bf16[256,768]{1,0:T(8,128)(2,1)S(1)}, u32[]{:S(2)}, u32[]{:S(2)}) collective-permute-start(bf16[256,768]{1,0:T(8,128)(2,1)S(1)} %get-tuple-element.39.set0_ref), channel_id=1, source_target_pairs={{0,1},{1,0},{2,3},{3,2},{4,5},{5,4},{6,7},{7,6},{8,9},{9,8},{10,11... | collective-permute-start | bytes 1179656 | tf_op jit(solution)/shard_map/ppermute | solution.py:575
  66.7 15.1 %collective-permute-start.4 = (bf16[256,768]{1,0:T(8,128)(2,1)S(1)}, bf16[256,768]{1,0:T(8,128)(2,1)S(1)}, u32[]{:S(2)}, u32[]{:S(2)}) collective-permute-start(bf16[256,768]{1,0:T(8,128)(2,1)S(1)} %get-tuple-element.39.set0_ref), channel_id=1, source_target_pairs={{0,64},{64,0},{1,65},{65,1},{2,66},{66,2},{3,67},{67,3},{4,68},{68... | collective-permute-start | bytes 1179656 | tf_op jit(solution)/shard_map/ppermute | solution.py:567
  73.7 8.0 %collective-permute-start.6 = (bf16[256,768]{1,0:T(8,128)(2,1)S(1)}, bf16[256,768]{1,0:T(8,128)(2,1)S(1)}, u32[]{:S(2)}, u32[]{:S(2)}) collective-permute-start(bf16[256,768]{1,0:T(8,128)(2,1)S(1)} %collective-permute-done.3.set2_ref), channel_id=1, source_target_pairs={{0,64},{64,0},{1,65},{65,1},{2,66},{66,2},{3,67},{67,3},{4,68},{68... | collective-permute-start | bytes 1179656 | tf_op jit(solution)/shard_map/ppermute | solution.py:567
  76.8 5.0 %collective-permute-start.5 = (bf16[256,768]{1,0:T(8,128)(2,1)S(1)}, bf16[256,768]{1,0:T(8,128)(2,1)S(1)}, u32[]{:S(2)}, u32[]{:S(2)}) collective-permute-start(bf16[256,768]{1,0:T(8,128)(2,1)S(1)} %collective-permute-done.2.set1_ref), channel_id=1, source_target_pairs={{0,64},{64,0},{1,65},{65,1},{2,66},{66,2},{3,67},{67,3},{4,68},{68... | collective-permute-start | bytes 1179656 | tf_op jit(solution)/shard_map/ppermute | solution.py:567
  78.6 12.9 %copy-start.1 = (f32[8,768]{1,0:T(8,128)S(1)}, f32[8,768]{1,0:T(8,128)}, u32[]{:S(2)}) copy-start(f32[8,768]{1,0:T(8,128)} %get-tuple-element.57.video_hat_ref) | copy-start | bytes 73732
  78.6 3.4 %collective-permute-start.7 = (bf16[256,768]{1,0:T(8,128)(2,1)S(1)}, bf16[256,768]{1,0:T(8,128)(2,1)S(1)}, u32[]{:S(2)}, u32[]{:S(2)}) collective-permute-start(bf16[256,768]{1,0:T(8,128)(2,1)S(1)} %collective-permute-done.1.set3_ref), channel_id=1, source_target_pairs={{0,64},{64,0},{1,65},{65,1},{2,66},{66,2},{3,67},{67,3},{4,68},{68... | collective-permute-start | bytes 1179656 | tf_op jit(solution)/shard_map/ppermute | solution.py:567
  83.4 1.6 %collective-permute-start.8 = (f32[4,8,1920]{2,1,0:T(8,128)S(1)}, f32[4,8,1920]{2,1,0:T(8,128)S(1)}, u32[]{:S(2)}, u32[]{:S(2)}) collective-permute-start(f32[4,8,1920]{2,1,0:T(8,128)S(1)} %get-tuple-element.50), channel_id=1, source_target_pairs={{0,64},{64,0},{1,65},{65,1},{2,66},{66,2},{3,67},{67,3},{4,68},{68... | collective-permute-start | bytes 737288 | tf_op jit(solution)/shard_map/ppermute | solution.py:567
  85.0 4.7 %collective-permute-start.9 = (f32[8,1920]{1,0:T(8,128)S(1)}, f32[8,1920]{1,0:T(8,128)S(1)}, u32[]{:S(2)}, u32[]{:S(2)}) collective-permute-start(f32[8,1920]{1,0:T(8,128)S(1)} %get-tuple-element.52), channel_id=1, source_target_pairs={{0,128},{32,160},{128,0},{160,32},{1,129},{33,161},{129,1},{161,33... | collective-permute-start | bytes 184328 | tf_op jit(solution)/shard_map/ppermute | solution.py:571
  87.2 4.3 %collective-permute-start.10 = (f32[8,1920]{1,0:T(8,128)S(1)}, f32[8,1920]{1,0:T(8,128)S(1)}, u32[]{:S(2)}, u32[]{:S(2)}) collective-permute-start(f32[8,1920]{1,0:T(8,128)S(1)} %get-tuple-element.53), channel_id=1, source_target_pairs={{0,160},{32,128},{128,32},{160,0},{1,161},{33,129},{129,33},{161,1... | collective-permute-start | bytes 184328 | tf_op jit(solution)/shard_map/ppermute | solution.py:571
  88.0 3.5 %collective-permute-start.11 = (f32[8,1920]{1,0:T(8,128)S(1)}, f32[8,1920]{1,0:T(8,128)S(1)}, u32[]{:S(2)}, u32[]{:S(2)}) collective-permute-start(f32[8,1920]{1,0:T(8,128)S(1)} %get-tuple-element.54), channel_id=1, source_target_pairs={{0,32},{32,0},{128,160},{160,128},{1,33},{33,1},{129,161},{161,129... | collective-permute-start | bytes 184328 | tf_op jit(solution)/shard_map/ppermute | solution.py:571

commit v11 on v10

--- a/solution.py
+++ b/solution.py
@@ -267,13 +267,16 @@
     )(arrived, out_proj)
 
 
-def text_kernel(arrived_ref, text_ref, target_ref):
+def text_kernel(arrived_ref, text_ref):
     halves = arrived_ref[:, SENT : SENT + PIECE]
     row, col = iota((TILE, CLIPS * 8), 0), iota((TILE, CLIPS * 8), 1)
     for part in range(2):
         pick = row // 4 * 8 + part * 4 + row % 4 == col
         texts = dot(jnp.where(pick, 1.0, 0.0).astype(bf16), halves)
         text_ref[:, part * PIECE : (part + 1) * PIECE] = texts.astype(bf16)
+
+
+def target_kernel(arrived_ref, target_ref):
     rows = CLIPS * 8
     code = arrived_ref[:, TAIL : TAIL + HD].astype(f32).reshape(CLIPS, 8, HD)[:, 3:4, :]
     code = jnp.broadcast_to(code, (CLIPS, 8, HD)).reshape(rows, HD)
@@ -282,20 +285,28 @@
     target_ref[...] = jnp.sum(code, axis=1, keepdims=True)
 
 
-def text_piece(*args):
+def text_piece(arrived):
     return pl.pallas_call(
         text_kernel,
         in_specs=[VMEM],
-        out_specs=[VMEM] * 2,
-        out_shape=[
-            jax.ShapeDtypeStruct((TILE, E), bf16),
-            jax.ShapeDtypeStruct((SET, 1), f32),
-        ],
+        out_specs=VMEM,
+        out_shape=jax.ShapeDtypeStruct((TILE, E), bf16),
         compiler_params=pltpu.CompilerParams(vmem_limit_bytes=16 << 20),
         cost_estimate=pl.CostEstimate(
             flops=4 * 256 * 512 * PIECE, bytes_accessed=1 << 20, transcendentals=0
         ),
-    )(*args)
+    )(arrived)
+
+
+def targets(arrived):
+    return pl.pallas_call(
+        target_kernel,
+        in_specs=[VMEM],
+        out_specs=VMEM,
+        out_shape=jax.ShapeDtypeStruct((SET, 1), f32),
+        compiler_params=pltpu.CompilerParams(vmem_limit_bytes=16 << 20),
+        cost_estimate=pl.CostEstimate(flops=1 << 18, bytes_accessed=1 << 19, transcendentals=0),
+    )(arrived)
 
 
 def position():
@@ -584,7 +595,7 @@
     arrived = exchange(outgoing.reshape(CLIPS, 8, SENT + PIECE), ROW)
     arrived = arrived.reshape(CLIPS * 8, SENT + PIECE)
     video_embed, video_hat, video_norm, send = embed(arrived, out_proj)
-    texts, target = text_piece(arrived)
+    texts, target = text_piece(arrived), targets(arrived)
     moved = [turn_y(texts), along(texts, 3), along(texts, 1)]
     videos, moved[0] = lax.optimization_barrier((exchange(send, PLANE), moved[0]))
     videos = videos.reshape(PLANE_ROWS, E)

time: 93.1 us -> 95.4 us (1.025)
  Pallas kernels: 13.5 us -> 16 us
    pallas_call x1, Pallas kernels: 1.38 us -> 2.62 us  [second_logits(): pl.pallas_call(second_kernel, in_specs=[VMEM] * 9, out_specs=[VMEM] * 5,...]
    pallas_call x1, Pallas kernels: 1.31 us -> 2.54 us  [gradients(): pl.pallas_call(grad_kernel, in_specs=[VMEM] * 18, out_specs=[VMEM] * 3, o...]
where the time goes in v11:
time: 95.4 us; the launch traced here: 95.1 us
  blocking collectives  43.8 us (46%)
  starting transfers between devices  24.6 us (26%)
  Pallas kernels  16 us (17%)
  waiting for transfers between devices  9.91 us (10%)
    all_to_all x1, blocking collectives, exchange(): return lax.all_to_all(x, axes, 0, 0, tiled=True)  43.8 us
    ppermute x5, starting transfers between devices, swap(): return lax.ppermute(x, 'c', [(0, 1), (1, 0)])  8.85 us
    ppermute x6, starting transfers between devices, along(): return lax.ppermute(x, ('xh', 'xl'), [(k, k ^ step) for k in range(4)])  8.12 us
    ppermute x6, waiting for transfers between devices, along(): return lax.ppermute(x, ('xh', 'xl'), [(k, k ^ step) for k in range(4)])  7.32 us
    all_to_all x1, starting transfers between devices, exchange(): return lax.all_to_all(x, axes, 0, 0, tiled=True)  6.43 us
    pallas_call x1, Pallas kernels, clip_sums(): pl.pallas_call(clip_kernel, in_specs=[pl.BlockSpec(memory_space=pltpu.HBM...  5.59 us
    pallas_call x1, Pallas kernels, second_logits(): pl.pallas_call(second_kernel, in_specs=[VMEM] * 9, out_specs=[VMEM] * 5,...  2.62 us
    pallas_call x1, Pallas kernels, gradients(): pl.pallas_call(grad_kernel, in_specs=[VMEM] * 18, out_specs=[VMEM] * 3, o...  2.54 us
  transfers between devices with their start and end apart: 13, of which 6 were waited for; matrix products, arithmetic and copies ran while one was open for 0% of the time, Pallas kernels for 8%

profile of v11, /device:TPU:1, one launch (start us, length us, event | category | flops | bytes accessed | tf_op | source)
XLA Modules:
  0.0 95.1 jit_solution(458020085847571921)
XLA Ops:
  0.6 3.7 %collective-permute-start = (bf16[8,768]{1,0:T(8,128)(2,1)}, bf16[8,768]{1,0:T(8,128)(2,1)S(1)}, u32[]{:S(2)}, u32[]{:S(2)}) collective-permute-start(bf16[8,768]{1,0:T(8,128)(2,1)} %text_ref.1), channel_id=1, source_target_pairs={{0,128},{32,160},{128,0},{160,32},{1,129},{33,161},{129,1},{161,33... | collective-permute-start | bytes 36872 | tf_op jit(solution)/shard_map/ppermute | solution.py:582
  4.3 5.6 %shard_map.93 = (bf16[256,896]{1,0:T(8,128)(2,1)S(1)}, f32[1,256]{1,0:T(1,128)S(1)}, f32[1,128]{1,0:T(1,128)S(1)}, f32[8,768]{1,0:T(8,128)S(1)}) custom-call(s32[1,64]{1,0:T(1,128)} %bitcast.17, bf16[1024,3200]{1,0:T(8,128)(2,1)} %bitcast.16, bf16[25,3200]{1,0:T(8,128)(2,1)} %pool_hbm.1, bf16[8,768]{1,0:T(8,128)(2,1)} %text_ref.1, s32[1,8]{1,0:T(1,128)} %bitcast.18), custom_call_target="tpu_custom_call" | custom-call | flops 419430400 | bytes 8388608 | tf_op jit(solution)/shard_map/pallas_call | solution.py:198
  9.9 0.8 shard_map.94
  10.7 43.8 %all_to_all.10 = bf16[64,8,1280]{2,1,0:T(8,128)(2,1)S(1)} all-to-all(bf16[64,8,1280]{2,1,0:T(8,128)(2,1)S(1)} %bitcast.13), channel_id=1, replica_groups=mesh['xh'=2,'c'=2,'xl'=2,'z'=8,'y'=4] {'xl','z','y'}, dimensions={0} | all-to-all | bytes 2621440 | tf_op jit(solution)/shard_map/all_to_all | solution.py:574
  54.5 2.4 %shard_map.95 = (bf16[8,768]{1,0:T(8,128)(2,1)}, f32[8,768]{1,0:T(8,128)}, f32[8,1]{1,0:T(8,128)S(1)}, bf16[32,8,768]{2,1,0:T(8,128)(2,1)}) custom-call(bf16[512,1280]{1,0:T(8,128)(2,1)S(1)} %bitcast.7, bf16[3200,768]{1,0:T(8,128)(2,1)S(1)} %bitcast.15), custom_call_target="tpu_custom_call" | custom-call | flops 117964800 | bytes 6291456 | tf_op jit(solution)/shard_map/pallas_call | solution.py:253
  56.9 6.4 %all-to-all-start.1 = ((bf16[32,8,768]{2,1,0:T(8,128)(2,1)}), bf16[32,8,768]{2,1,0:T(8,128)(2,1)S(1)}, u32[]{:S(2)}, u32[]{:S(2)}) async-start(bf16[32,8,768]{2,1,0:T(8,128)(2,1)} %get-tuple-element.36), calls=%async_computation.1 | async-start | bytes 786432 | tf_op jit(solution)/shard_map/all_to_all | solution.py:574
  63.3 0.0 copy-start
  63.3 0.0 copy-start.1
  63.3 0.4 shard_map.96.set0_ref
  63.8 0.9 collective-permute-start.3
  64.7 0.6 collective-permute-start.2
  65.3 1.2 %collective-permute-start.1 = (bf16[256,768]{1,0:T(8,128)(2,1)S(1)}, bf16[256,768]{1,0:T(8,128)(2,1)S(1)}, u32[]{:S(2)}, u32[]{:S(2)}) collective-permute-start(bf16[256,768]{1,0:T(8,128)(2,1)S(1)} %shard_map.96.set0_ref), channel_id=1, source_target_pairs={{0,1},{1,0},{2,3},{3,2},{4,5},{5,4},{6,7},{7,6},{8,9},{9,8},{10,11... | collective-permute-start | bytes 1179656 | tf_op jit(solution)/shard_map/ppermute | solution.py:586
  66.5 3.2 %collective-permute-start.4 = (bf16[256,768]{1,0:T(8,128)(2,1)S(1)}, bf16[256,768]{1,0:T(8,128)(2,1)}, u32[]{:S(2)}, u32[]{:S(2)}) collective-permute-start(bf16[256,768]{1,0:T(8,128)(2,1)S(1)} %shard_map.96.set0_ref), channel_id=1, source_target_pairs={{0,64},{64,0},{1,65},{65,1},{2,66},{66,2},{3,67},{67,3},{4,68},{68... | collective-permute-start | bytes 1179656 | tf_op jit(solution)/shard_map/ppermute | solution.py:578
  69.7 3.8 %collective-permute-done.3.set2_ref = bf16[256,768]{1,0:T(8,128)(2,1)S(1)} collective-permute-done((bf16[256,768]{1,0:T(8,128)(2,1)S(1)}, bf16[256,768]{1,0:T(8,128)(2,1)S(1)}, u32[]{:S(2)}, u32[]{:S(2)}) %collective-permute-start.3) | collective-permute-done | bytes 393248 | tf_op jit(solution)/shard_map/ppermute | solution.py:582
  73.6 3.0 %collective-permute-start.6 = (bf16[256,768]{1,0:T(8,128)(2,1)S(1)}, bf16[256,768]{1,0:T(8,128)(2,1)}, u32[]{:S(2)}, u32[]{:S(2)}) collective-permute-start(bf16[256,768]{1,0:T(8,128)(2,1)S(1)} %collective-permute-done.3.set2_ref), channel_id=1, source_target_pairs={{0,64},{64,0},{1,65},{65,1},{2,66},{66,2},{3,67},{67,3},{4,68},{68... | collective-permute-start | bytes 1179656 | tf_op jit(solution)/shard_map/ppermute | solution.py:578
  76.6 0.0 collective-permute-done.2.set1_ref
  76.6 0.0 collective-permute-start.5
  76.6 1.8 %collective-permute-done.1.set3_ref = bf16[256,768]{1,0:T(8,128)(2,1)S(1)} collective-permute-done((bf16[256,768]{1,0:T(8,128)(2,1)S(1)}, bf16[256,768]{1,0:T(8,128)(2,1)S(1)}, u32[]{:S(2)}, u32[]{:S(2)}) %collective-permute-start.1) | collective-permute-done | bytes 393248 | tf_op jit(solution)/shard_map/ppermute | solution.py:586
  78.4 2.1 %collective-permute-start.7 = (bf16[256,768]{1,0:T(8,128)(2,1)S(1)}, bf16[256,768]{1,0:T(8,128)(2,1)S(1)}, u32[]{:S(2)}, u32[]{:S(2)}) collective-permute-start(bf16[256,768]{1,0:T(8,128)(2,1)S(1)} %collective-permute-done.1.set3_ref), channel_id=1, source_target_pairs={{0,64},{64,0},{1,65},{65,1},{2,66},{66,2},{3,67},{67,3},{4,68},{68... | collective-permute-start | bytes 1179656 | tf_op jit(solution)/shard_map/ppermute | solution.py:578
  80.5 0.2 shard_map.97.target_ref
  80.7 1.1 %shard_map.98 = (f32[8,1024]{1,0:T(8,128)S(1)}, f32[8,256]{1,0:T(8,128)S(1)}, f32[256,128]{1,0:T(8,128)S(1)}, f32[1,256]{1,0:T(1,128)S(1)}, f32[256,32]{1,0:T(8,128)S(1)}) custom-call(bf16[256,768]{1,0:T(8,128)(2,1)S(1)} %bitcast.10, f32[512,1]{1,0:T(8,128)S(1)} %shard_map.97.target_ref, bf16[256,768]{1,0:T(8,128)(2,1)S(1)} %shard_map.96.set0_ref, ...), custom_call_target="tpu_custom_call" | custom-call | flops 402653184 | bytes 2097152 | tf_op jit(solution)/shard_map/pallas_call | solution.py:460
  81.7 0.0 collective-permute-done.4.set4_ref
  81.7 0.1 collective-permute-done.7.set7_ref
  81.8 2.6 %shard_map.99 = (f32[4,8,1920]{2,1,0:T(8,128)S(1)}, f32[8,1024]{1,0:T(8,128)S(1)}, f32[256,1]{1,0:T(8,128)S(1)}, f32[8,256]{1,0:T(8,128)S(1)}, f32[8,128]{1,0:T(8,128)S(1)}) custom-call(bf16[256,768]{1,0:T(8,128)(2,1)S(1)} %bitcast.11, f32[512,1]{1,0:T(8,128)S(1)} %shard_map.97.target_ref, bf16[256,768]{1,0:T(8,128)(2,1)} %collective-permute-done.4.set4_ref, ...), custom_call_target="tpu_custom_call" | custom-call | flops 603979776 | bytes 4194304 | tf_op jit(solution)/shard_map/pallas_call | solution.py:480
  84.5 0.5 collective-permute-start.8
  84.9 0.4 shard_map.100.keep_ref
  85.4 0.7 collective-permute-done.8.got_ref
  86.1 2.2 %collective-permute-start.9 = (f32[8,1920]{1,0:T(8,128)S(1)}, f32[8,1920]{1,0:T(8,128)S(1)}, u32[]{:S(2)}, u32[]{:S(2)}) collective-permute-start(f32[8,1920]{1,0:T(8,128)S(1)} %get-tuple-element.48), channel_id=1, source_target_pairs={{0,128},{32,160},{128,0},{160,32},{1,129},{33,161},{129,1},{161,33... | collective-permute-start | bytes 184328 | tf_op jit(solution)/shard_map/ppermute | solution.py:582
  88.3 0.8 collective-permute-start.10
  89.1 1.7 %collective-permute-done.9.part1_ref = f32[8,1920]{1,0:T(8,128)S(1)} collective-permute-done((f32[8,1920]{1,0:T(8,128)S(1)}, f32[8,1920]{1,0:T(8,128)S(1)}, u32[]{:S(2)}, u32[]{:S(2)}) %collective-permute-start.9) | collective-permute-done | bytes 61472 | tf_op jit(solution)/shard_map/ppermute | solution.py:582
  90.8 1.8 %collective-permute-done.10.part2_ref = f32[8,1920]{1,0:T(8,128)S(1)} collective-permute-done((f32[8,1920]{1,0:T(8,128)S(1)}, f32[8,1920]{1,0:T(8,128)S(1)}, u32[]{:S(2)}, u32[]{:S(2)}) %collective-permute-start.10) | collective-permute-done | bytes 61472 | tf_op jit(solution)/shard_map/ppermute | solution.py:582
  92.6 2.5 %shard_map.102 = (f32[1,1]{1,0:T(1,128)}, f32[8,768]{1,0:T(8,128)}, f32[8,768]{1,0:T(8,128)}) custom-call(f32[8,1920]{1,0:T(8,128)S(1)} %get-tuple-element.47.part0_ref, f32[8,1920]{1,0:T(8,128)S(1)} %collective-permute-done.9.part1_ref, f32[8,1920]{1,0:T(8,128)S(1)} %collective-permute-done.10.part2_ref, f32[8,1920]{1,0:T(8,128)S(1)} %collective-permute-done.11.part3_ref, ...), custom_call_target="tpu_custom_call" | custom-call | flops 25165824 | bytes 5242880 | tf_op jit(solution)/shard_map/pallas_call | solution.py:556
  (14 shorter events, 0.1 us)
Async XLA Ops:
  0.6 9.3 %collective-permute-start = (bf16[8,768]{1,0:T(8,128)(2,1)}, bf16[8,768]{1,0:T(8,128)(2,1)S(1)}, u32[]{:S(2)}, u32[]{:S(2)}) collective-permute-start(bf16[8,768]{1,0:T(8,128)(2,1)} %text_ref.1), channel_id=1, source_target_pairs={{0,128},{32,160},{128,0},{160,32},{1,129},{33,161},{129,1},{161,33... | collective-permute-start | bytes 36872 | tf_op jit(solution)/shard_map/ppermute | solution.py:582
  4.3 50.2 %slice-start = ((s8[4915200]{0:T(1024)(128)(4,1)}), s8[4194304]{0:T(1024)(128)(4,1)S(1)}, s32[]{:S(2)}) async-start(s8[4915200]{0:T(1024)(128)(4,1)} %bitcast.14), calls=%async_computation.2 | async-start | bytes 8388608
  4.3 50.2 %slice-start.1 = ((s8[4915200]{0:T(1024)(128)(4,1)}), s8[720896]{0:T(1024)(128)(4,1)S(1)}, s32[]{:S(2)}) async-start(s8[4915200]{0:T(1024)(128)(4,1)} %bitcast.14), calls=%async_computation.3 | async-start | bytes 1441792
  56.9 21.5 %all-to-all-start.1 = ((bf16[32,8,768]{2,1,0:T(8,128)(2,1)}), bf16[32,8,768]{2,1,0:T(8,128)(2,1)S(1)}, u32[]{:S(2)}, u32[]{:S(2)}) async-start(bf16[32,8,768]{2,1,0:T(8,128)(2,1)} %get-tuple-element.36), calls=%async_computation.1 | async-start | bytes 786432 | tf_op jit(solution)/shard_map/all_to_all | solution.py:574
  63.3 29.2 %copy-start = (bf16[8,768]{1,0:T(8,128)(2,1)S(1)}, bf16[8,768]{1,0:T(8,128)(2,1)}, u32[]{:S(2)}) copy-start(bf16[8,768]{1,0:T(8,128)(2,1)} %text_ref.1) | copy-start | bytes 36868
  63.3 29.2 %copy-start.1 = (f32[8,768]{1,0:T(8,128)S(1)}, f32[8,768]{1,0:T(8,128)}, u32[]{:S(2)}) copy-start(f32[8,768]{1,0:T(8,128)} %get-tuple-element.53.video_hat_ref) | copy-start | bytes 73732
  63.8 9.8 %collective-permute-start.3 = (bf16[256,768]{1,0:T(8,128)(2,1)S(1)}, bf16[256,768]{1,0:T(8,128)(2,1)S(1)}, u32[]{:S(2)}, u32[]{:S(2)}) collective-permute-start(bf16[256,768]{1,0:T(8,128)(2,1)S(1)} %shard_map.96.set0_ref), channel_id=1, source_target_pairs={{0,160},{32,128},{128,32},{160,0},{1,161},{33,129},{129,33},{161,1... | collective-permute-start | bytes 1179656 | tf_op jit(solution)/shard_map/ppermute | solution.py:582
  64.7 11.9 %collective-permute-start.2 = (bf16[256,768]{1,0:T(8,128)(2,1)S(1)}, bf16[256,768]{1,0:T(8,128)(2,1)S(1)}, u32[]{:S(2)}, u32[]{:S(2)}) collective-permute-start(bf16[256,768]{1,0:T(8,128)(2,1)S(1)} %shard_map.96.set0_ref), channel_id=1, source_target_pairs={{0,32},{32,0},{128,160},{160,128},{1,33},{33,1},{129,161},{161,129... | collective-permute-start | bytes 1179656 | tf_op jit(solution)/shard_map/ppermute | solution.py:582
  65.3 13.1 %collective-permute-start.1 = (bf16[256,768]{1,0:T(8,128)(2,1)S(1)}, bf16[256,768]{1,0:T(8,128)(2,1)S(1)}, u32[]{:S(2)}, u32[]{:S(2)}) collective-permute-start(bf16[256,768]{1,0:T(8,128)(2,1)S(1)} %shard_map.96.set0_ref), channel_id=1, source_target_pairs={{0,1},{1,0},{2,3},{3,2},{4,5},{5,4},{6,7},{7,6},{8,9},{9,8},{10,11... | collective-permute-start | bytes 1179656 | tf_op jit(solution)/shard_map/ppermute | solution.py:586
  66.5 15.2 %collective-permute-start.4 = (bf16[256,768]{1,0:T(8,128)(2,1)S(1)}, bf16[256,768]{1,0:T(8,128)(2,1)}, u32[]{:S(2)}, u32[]{:S(2)}) collective-permute-start(bf16[256,768]{1,0:T(8,128)(2,1)S(1)} %shard_map.96.set0_ref), channel_id=1, source_target_pairs={{0,64},{64,0},{1,65},{65,1},{2,66},{66,2},{3,67},{67,3},{4,68},{68... | collective-permute-start | bytes 1179656 | tf_op jit(solution)/shard_map/ppermute | solution.py:578
  73.6 8.2 %collective-permute-start.6 = (bf16[256,768]{1,0:T(8,128)(2,1)S(1)}, bf16[256,768]{1,0:T(8,128)(2,1)}, u32[]{:S(2)}, u32[]{:S(2)}) collective-permute-start(bf16[256,768]{1,0:T(8,128)(2,1)S(1)} %collective-permute-done.3.set2_ref), channel_id=1, source_target_pairs={{0,64},{64,0},{1,65},{65,1},{2,66},{66,2},{3,67},{67,3},{4,68},{68... | collective-permute-start | bytes 1179656 | tf_op jit(solution)/shard_map/ppermute | solution.py:578
  76.6 5.1 %collective-permute-start.5 = (bf16[256,768]{1,0:T(8,128)(2,1)S(1)}, bf16[256,768]{1,0:T(8,128)(2,1)}, u32[]{:S(2)}, u32[]{:S(2)}) collective-permute-start(bf16[256,768]{1,0:T(8,128)(2,1)S(1)} %collective-permute-done.2.set1_ref), channel_id=1, source_target_pairs={{0,64},{64,0},{1,65},{65,1},{2,66},{66,2},{3,67},{67,3},{4,68},{68... | collective-permute-start | bytes 1179656 | tf_op jit(solution)/shard_map/ppermute | solution.py:578
  78.4 3.5 %collective-permute-start.7 = (bf16[256,768]{1,0:T(8,128)(2,1)S(1)}, bf16[256,768]{1,0:T(8,128)(2,1)S(1)}, u32[]{:S(2)}, u32[]{:S(2)}) collective-permute-start(bf16[256,768]{1,0:T(8,128)(2,1)S(1)} %collective-permute-done.1.set3_ref), channel_id=1, source_target_pairs={{0,64},{64,0},{1,65},{65,1},{2,66},{66,2},{3,67},{67,3},{4,68},{68... | collective-permute-start | bytes 1179656 | tf_op jit(solution)/shard_map/ppermute | solution.py:578
  84.5 1.6 %collective-permute-start.8 = (f32[4,8,1920]{2,1,0:T(8,128)S(1)}, f32[4,8,1920]{2,1,0:T(8,128)S(1)}, u32[]{:S(2)}, u32[]{:S(2)}) collective-permute-start(f32[4,8,1920]{2,1,0:T(8,128)S(1)} %get-tuple-element.46), channel_id=1, source_target_pairs={{0,64},{64,0},{1,65},{65,1},{2,66},{66,2},{3,67},{67,3},{4,68},{68... | collective-permute-start | bytes 737288 | tf_op jit(solution)/shard_map/ppermute | solution.py:578
  86.1 4.7 %collective-permute-start.9 = (f32[8,1920]{1,0:T(8,128)S(1)}, f32[8,1920]{1,0:T(8,128)S(1)}, u32[]{:S(2)}, u32[]{:S(2)}) collective-permute-start(f32[8,1920]{1,0:T(8,128)S(1)} %get-tuple-element.48), channel_id=1, source_target_pairs={{0,128},{32,160},{128,0},{160,32},{1,129},{33,161},{129,1},{161,33... | collective-permute-start | bytes 184328 | tf_op jit(solution)/shard_map/ppermute | solution.py:582
  88.3 4.3 %collective-permute-start.10 = (f32[8,1920]{1,0:T(8,128)S(1)}, f32[8,1920]{1,0:T(8,128)S(1)}, u32[]{:S(2)}, u32[]{:S(2)}) collective-permute-start(f32[8,1920]{1,0:T(8,128)S(1)} %get-tuple-element.49), channel_id=1, source_target_pairs={{0,160},{32,128},{128,32},{160,0},{1,161},{33,129},{129,33},{161,1... | collective-permute-start | bytes 184328 | tf_op jit(solution)/shard_map/ppermute | solution.py:582
  89.1 3.5 %collective-permute-start.11 = (f32[8,1920]{1,0:T(8,128)S(1)}, f32[8,1920]{1,0:T(8,128)S(1)}, u32[]{:S(2)}, u32[]{:S(2)}) collective-permute-start(f32[8,1920]{1,0:T(8,128)S(1)} %get-tuple-element.50), channel_id=1, source_target_pairs={{0,32},{32,0},{128,160},{160,128},{1,33},{33,1},{129,161},{161,129... | collective-permute-start | bytes 184328 | tf_op jit(solution)/shard_map/ppermute | solution.py:582
